TPU v7x, 128 devices: a whole 4x4x4 slice. The times are simulated.
128 devices in a mesh: row: 8 (over x, core), col: 16 (over y, z).
Axes of the slice: x: 4, y: 4, z: 4, core: 2. Of those that a mesh axis runs over, the one named last changes fastest.
Arguments:
- flow_state: float32 [5, 4, 1024, 2048], P(None, None, 'row', 'col'), may hold values from -6 to 6
- viscosity: float32 [4, 1024, 2048], P(None, 'row', 'col'), may hold values from 0.5 to 2
- metric_x: float32 [1024, 2048], P('row', 'col'), may hold values from 128 to 512
- metric_y: float32 [1024, 2048], P('row', 'col'), may hold values from 128 to 512
- jacobian_x: float32 [5, 5, 1024], P(None, None, 'row'), may hold values from -2.5 to 2.5
- jacobian_y: float32 [5, 5, 2048], P(None, None, 'col'), may hold values from -2.5 to 2.5
Outputs:
- increment: float32 [5, 4, 1024, 2048], P(None, None, 'row', 'col')
All inputs are finite; a program needn't handle non-finite values.
Results may differ from a plain program's by a relative error of at most 0.0014.
Values sent between devices are 32-bit elements; how exact they have to be, the bound alone decides.
No kernel may reach another device: no remote copies, remote signals or barrier semaphores. Data moves between devices by JAX's collectives and lax.ppermute only.
A program may use at most 128 MiB of HBM per device.

v0:
```python
import functools

import jax
import jax.numpy as jnp
from jax import lax
from jax.experimental import pallas as pl
from jax.experimental.pallas import tpu as pltpu
from jax.sharding import PartitionSpec as P

F32 = jnp.float32
N = 128
HALF = 64
CHUNK = 8
STEPS = HALF // CHUNK
VMEM_LIMIT = 48 * 1024 * 1024


def zeros():
    return jnp.zeros((8, 128), F32)


def ones():
    return jnp.ones((8, 128), F32)


def lane(value, index):
    return jnp.broadcast_to(value[:, index : index + 1], (8, 128))


def mat_cols(matrix, columns):
    result = []
    for column in columns:
        out = []
        for i in range(5):
            total = matrix[i][0] * column[0]
            for k in range(1, 5):
                total = total + matrix[i][k] * column[k]
            out.append(total)
        result.append(out)
    return result


def solve(matrix, columns):
    m = [list(row) for row in matrix]
    cols = [list(column) for column in columns]
    inverse = []
    for p in range(5):
        inv = 1.0 / m[p][p]
        inverse.append(inv)
        for i in range(p + 1, 5):
            weight = m[i][p] * inv
            for j in range(p + 1, 5):
                m[i][j] = m[i][j] - weight * m[p][j]
            for column in cols:
                column[i] = column[i] - weight * column[p]
    for column in cols:
        for i in range(4, -1, -1):
            total = column[i]
            for j in range(i + 1, 5):
                total = total - m[i][j] * column[j]
            column[i] = total * inverse[i]
    return cols


def columns_of(matrix):
    return [[matrix[i][j] for i in range(5)] for j in range(5)]


def rows_of(columns):
    return [[columns[j][i] for j in range(5)] for i in range(5)]


def load_mat(ref, base):
    return [[ref[base + 5 * i + j] for j in range(5)] for i in range(5)]


def load_vec(ref, base):
    return [ref[base + i] for i in range(5)]


def store_mat(ref, base, matrix):
    for i in range(5):
        for j in range(5):
            ref[base + 5 * i + j] = matrix[i][j]


def store_vec(ref, base, vector):
    for i in range(5):
        ref[base + i] = vector[i]


R_AT, X_AT, W_AT, Q_AT, XQ_AT, Y_AT, STATE = 0, 25, 50, 55, 80, 105, 110


def init_state(state):
    for i in range(5):
        for j in range(5):
            state[R_AT + 5 * i + j] = ones() if i == j else zeros()
            state[X_AT + 5 * i + j] = zeros()
        state[W_AT + i] = zeros()


def init_first_edge(state):
    for i in range(5):
        for j in range(5):
            state[Q_AT + 5 * i + j] = ones() if i == j else zeros()
            state[XQ_AT + 5 * i + j] = zeros()
        state[Y_AT + i] = zeros()


def accumulate(state, r, x, w):
    q = load_mat(state, Q_AT)
    xq = load_mat(state, XQ_AT)
    y = load_vec(state, Y_AT)
    moved = mat_cols(q, columns_of(r) + columns_of(x) + [w])
    q_new = [[q[i][j] - moved[j][i] for j in range(5)] for i in range(5)]
    xq_new = [[xq[i][j] - moved[5 + j][i] for j in range(5)] for i in range(5)]
    y_new = [y[i] - moved[10][i] for i in range(5)]
    store_mat(state, Q_AT, q_new)
    store_mat(state, XQ_AT, xq_new)
    store_vec(state, Y_AT, y_new)
    return q_new, xq_new, y_new


def local_relation(speed, excess, right, r, x, w):
    cols = mat_cols(speed, columns_of(r) + columns_of(x) + [w])
    s = [[r[i][j] + cols[j][i] for j in range(5)] for i in range(5)]
    xn = [[x[i][j] + cols[5 + j][i] for j in range(5)] for i in range(5)]
    for i in range(5):
        s[i][i] = s[i][i] + excess
        xn[i][i] = xn[i][i] + excess
    g = [right[i] - w[i] - cols[10][i] for i in range(5)]
    return s, xn, g


def sweep_step(k, state, fac_ref, slot, get_cell):
    @pl.when(k == 1)
    def _():
        init_first_edge(state)

    r = load_mat(state, R_AT)
    x = load_mat(state, X_AT)
    w = load_vec(state, W_AT)
    speed, excess, right = get_cell(k)
    s, xn, g = local_relation(speed, excess, right, r, x, w)
    t = [[s[i][j] - speed[i][j] for j in range(5)] for i in range(5)]
    for i in range(5):
        t[i][i] = t[i][i] + 1.0
    solved = solve(t, columns_of(s) + columns_of(xn) + [g])
    r_new = rows_of(solved[:5])
    x_new = rows_of(solved[5:10])
    w_new = [-value for value in solved[10]]
    accumulate(state, r, x, w)
    store_mat(state, R_AT, r_new)
    store_mat(state, X_AT, x_new)
    store_vec(state, W_AT, w_new)
    for i in range(5):
        for j in range(5):
            fac_ref[slot, 5 * i + j] = r_new[i][j]
            fac_ref[slot, 25 + 5 * i + j] = x_new[i][j]
        fac_ref[slot, 50 + i] = w_new[i]


def even_rows():
    return lax.broadcasted_iota(jnp.int32, (8, 128), 0) % 2 == 0


def finish_sweep(first, state, port, port_ref, mid_ref, get_cell, prev_speed):
    r = load_mat(state, R_AT)
    x = load_mat(state, X_AT)
    w = load_vec(state, W_AT)
    q, xq, y = accumulate(state, r, x, w)
    speed, excess, right = get_cell(HALF - 1)
    s, xn, g = local_relation(speed, excess, right, r, x, w)

    def from_second(value):
        return pltpu.roll(value, 7, 0)

    q1 = [[from_second(e) for e in row] for row in q]
    xq1 = [[from_second(e) for e in row] for row in xq]
    y1 = [from_second(e) for e in y]
    cols = mat_cols(speed, columns_of(q1) + columns_of(xq1) + [y1])
    qq = [[q1[i][j] - cols[j][i] for j in range(5)] for i in range(5)]
    xx = [[xq1[i][j] - cols[5 + j][i] for j in range(5)] for i in range(5)]
    yy = [y1[i] - cols[10][i] for i in range(5)]
    t = [[s[i][j] + qq[i][j] - xx[i][j] for j in range(5)] for i in range(5)]
    mx_right = [[xx[i][j] - xn[i][j] for j in range(5)] for i in range(5)]
    m0_right = [yy[i] + g[i] for i in range(5)]
    solved = solve(t, columns_of(qq) + columns_of(mx_right) + [m0_right])
    mc, mx, m0 = rows_of(solved[:5]), rows_of(solved[5:10]), solved[10]
    for i in range(5):
        for j in range(5):
            mid_ref[5 * i + j] = mc[i][j]
            mid_ref[25 + 5 * i + j] = mx[i][j]
        mid_ref[50 + i] = m0[i]
    left = mat_cols(q, solved)
    start = jnp.broadcast_to(first, (8, 128)) > 0
    q_all = [
        [jnp.where(start, 1.0 if i == j else 0.0, left[j][i]) for j in range(5)] for i in range(5)
    ]
    xq_all = [[jnp.where(start, 0.0, xq[i][j] + left[5 + j][i]) for j in range(5)] for i in range(5)]
    y_all = [jnp.where(start, 0.0, y[i] + left[10][i]) for i in range(5)]
    cols = mat_cols(prev_speed, columns_of(q_all) + columns_of(xq_all) + [y_all])
    for i in range(5):
        for j in range(5):
            port[pl.ds(8 * (55 + 5 * i + j), 8), :] = q_all[i][j] - cols[j][i]
            port[pl.ds(8 * (80 + 5 * i + j), 8), :] = xq_all[i][j] - cols[5 + j][i]
        port[pl.ds(8 * (105 + i), 8), :] = y_all[i] - cols[10][i]
    s1 = [[from_second(e) for e in row] for row in s]
    xn1 = [[from_second(e) for e in row] for row in xn]
    g1 = [from_second(e) for e in g]
    n1 = [[xn1[i][j] - s1[i][j] for j in range(5)] for i in range(5)]
    cols = mat_cols(n1, solved)
    for i in range(5):
        for j in range(5):
            port[pl.ds(8 * (5 * i + j), 8), :] = s1[i][j] + cols[j][i]
            port[pl.ds(8 * (25 + 5 * i + j), 8), :] = xn1[i][j] + cols[5 + j][i]
        port[pl.ds(8 * (50 + i), 8), :] = g1[i] - cols[10][i]
    for e in range(110, 128):
        port[pl.ds(8 * e, 8), :] = zeros()
    for z in range(4):
        port_ref[pl.ds(128 * z, 128), :] = port[pl.ds(2 * z, 128, stride=8), :].T


def cell_rows(k):
    return pl.ds(k, 8, stride=HALF)


def read_prev_speed(up_ref, rows8):
    for z in range(4):
        value = 1.0 / (up_ref[pl.ds(20 + z, 1), :] * up_ref[pl.ds(24, 1), :])
        rows8[pl.ds(2 * z, 1), :] = value
        rows8[pl.ds(2 * z + 1, 1), :] = value
    scale = rows8[...]
    entries = jnp.broadcast_to(up_ref[pl.ds(25, 1), :], (8, 128))
    return [[scale * lane(entries, 5 * i + j) for j in range(5)] for i in range(5)]


def run_chunk(state, fac_ref, get_cell):
    step = pl.program_id(0)
    count = jnp.where(step == STEPS - 1, CHUNK - 1, CHUNK)

    def one(slot, carry):
        sweep_step(step * CHUNK + slot, state, fac_ref, slot, get_cell)
        return carry

    lax.fori_loop(0, count, one, 0)


def forward_x_kernel(
    first_ref, last_ref, q_ref, visc_ref, mx_ref, my_ref, jacx_ref, jacy_ref,
    west_ref, east_ref, south_ref, north_ref,
    fac_ref, port_ref, mid_ref,
    state, eps, dlt, g1, g2, tab, tin, before, after, port, rows8,
):
    step = pl.program_id(0)

    @pl.when(step == 0)
    def _():
        init_state(state)
        init_first_edge(state)
        mx = mx_ref[...]
        my = my_ref[...]
        not_first = jnp.where(first_ref[1] > 0, 0.0, 1.0)
        not_last = jnp.where(last_ref[1] > 0, 0.0, 1.0)
        tin[...] = jnp.zeros((128, 128), F32)
        tin[pl.ds(0, 25), :] = jacx_ref[...]
        for z in range(4):
            rows = pl.ds(128 * z, 128)
            visc = visc_ref[rows, :]
            e = 1.0 / (visc * mx)
            d = e * e * visc
            eps[rows, :] = e
            dlt[rows, :] = d
            g2[rows, :] = d * my
            g1[rows, :] = (d * my) * (my * visc)
            for c in range(5):
                tin[pl.ds(25 + c, 1), :] = south_ref[pl.ds(4 * c + z, 1), :] * not_first
                tin[pl.ds(30 + c, 1), :] = north_ref[pl.ds(4 * c + z, 1), :] * not_last
            tab[rows, :] = tin[...].T
        even = even_rows()
        open_first = jnp.where(first_ref[0] > 0, 0.0, 1.0)
        open_last = jnp.where(last_ref[0] > 0, 0.0, 1.0)
        for c in range(5):
            for z in range(4):
                before[c, pl.ds(2 * z, 1), :] = west_ref[pl.ds(4 * c + z, 1), :] * open_first
                before[c, pl.ds(2 * z + 1, 1), :] = q_ref[c, pl.ds(128 * z + HALF - 1, 1), :]
                after[c, pl.ds(2 * z, 1), :] = q_ref[c, pl.ds(128 * z + HALF, 1), :]
                after[c, pl.ds(2 * z + 1, 1), :] = east_ref[pl.ds(4 * c + z, 1), :] * open_last

    lanes = lax.broadcasted_iota(jnp.int32, (8, 128), 1)

    def get_cell(k):
        rows = cell_rows(k)
        table = tab[rows, :]
        e = eps[rows, :]
        d = dlt[rows, :]
        speed = [[e * lane(table, 5 * i + j) for j in range(5)] for i in range(5)]
        at_start = k == 0
        at_end = k == HALF - 1
        back = cell_rows(jnp.maximum(k - 1, 0))
        ahead = cell_rows(jnp.minimum(k + 1, HALF - 1))
        diff_x, diff_y, second_x, second_y = [], [], [], []
        for c in range(5):
            here = q_ref[c, rows, :]
            west = jnp.where(at_start, before[c], q_ref[c, back, :])
            east = jnp.where(at_end, after[c], q_ref[c, ahead, :])
            south = jnp.where(lanes == 0, lane(table, 25 + c), pltpu.roll(here, 1, 1))
            north = jnp.where(lanes == 127, lane(table, 30 + c), pltpu.roll(here, 127, 1))
            diff_x.append(east - west)
            diff_y.append(north - south)
            second_x.append((east - 2.0 * here) + west)
            second_y.append((north - 2.0 * here) + south)
        a, b = g1[rows, :], g2[rows, :]
        convect_x = mat_cols(speed, [diff_x])[0]
        right = []
        for i in range(5):
            total = jacy_ref[pl.ds(5 * i, 1), :] * diff_y[0]
            for j in range(1, 5):
                total = total + jacy_ref[pl.ds(5 * i + j, 1), :] * diff_y[j]
            right.append((second_x[i] - convect_x[i]) + (a * second_y[i] - b * total))
        return speed, d, right

    run_chunk(state, fac_ref, get_cell)

    @pl.when(step == STEPS - 1)
    def _():
        speed = read_prev_speed(west_ref, rows8)
        finish_sweep(first_ref[0], state, port, port_ref, mid_ref, get_cell, speed)


def forward_y_kernel(
    first_ref, p_ref, visc_ref, my_ref, jacy_ref, south_ref,
    fac_ref, port_ref, mid_ref,
    state, field, eps, dlt, tab, tin, port, rows8,
):
    step = pl.program_id(0)

    @pl.when(step == 0)
    def _():
        init_state(state)
        init_first_edge(state)
        my = my_ref[...].T
        tin[...] = jnp.zeros((128, 128), F32)
        tin[pl.ds(0, 25), :] = jacy_ref[...]
        table = tin[...].T
        for z in range(4):
            rows = pl.ds(128 * z, 128)
            visc = visc_ref[rows, :].T
            e = 1.0 / (visc * my)
            eps[rows, :] = e
            dlt[rows, :] = e * e * visc
            tab[rows, :] = table
            for c in range(5):
                field[c, rows, :] = p_ref[c, rows, :].T

    def get_cell(k):
        rows = cell_rows(k)
        table = tab[rows, :]
        e = eps[rows, :]
        d = dlt[rows, :]
        speed = [[e * lane(table, 5 * i + j) for j in range(5)] for i in range(5)]
        return speed, d, [d * field[c, rows, :] for c in range(5)]

    run_chunk(state, fac_ref, get_cell)

    @pl.when(step == STEPS - 1)
    def _():
        speed = read_prev_speed(south_ref, rows8)
        finish_sweep(first_ref[1], state, port, port_ref, mid_ref, get_cell, speed)


def reduced_kernel(count, lines, in_ref, out_ref, ports, gains):
    per = 128 // lines
    for group in range(count // per):
        turned = in_ref[pl.ds(128 * group, 128), :].T
        for q in range(per):
            ports[group * per + q] = turned if q == 0 else pltpu.roll(turned, 128 - lines * q, 1)

    def entry(piece, index):
        return ports[piece, pl.ds(index, 1), :]

    def matrix(piece, base):
        return [[entry(piece, base + 5 * i + j) for j in range(5)] for i in range(5)]

    def vector(piece, base):
        return [entry(piece, base + i) for i in range(5)]

    def eliminate(piece, following, s, g):
        qq, xx, yy = matrix(following, 55), matrix(following, 80), vector(following, 105)
        reduced = [[s[i][j] - xx[i][j] for j in range(5)] for i in range(5)]
        t = [[reduced[i][j] + qq[i][j] for j in range(5)] for i in range(5)]
        rhs = [yy[i] + g[i] for i in range(5)]
        solved = solve(t, columns_of(reduced) + [rhs])
        h, v = rows_of(solved[:5]), solved[5]
        for i in range(5):
            for j in range(5):
                gains[piece, pl.ds(5 * i + j, 1), :] = h[i][j]
            gains[piece, pl.ds(25 + i, 1), :] = v[i]

    eliminate(0, 1, matrix(0, 0), vector(0, 50))

    def forward(piece, carry):
        h = [[gains[piece - 1, pl.ds(5 * i + j, 1), :] for j in range(5)] for i in range(5)]
        v = [gains[piece - 1, pl.ds(25 + i, 1), :] for i in range(5)]
        s, xn, g = matrix(piece, 0), matrix(piece, 25), vector(piece, 50)
        gain = [[(1.0 if i == j else 0.0) - h[i][j] for j in range(5)] for i in range(5)]
        part = mat_cols(s, columns_of(h))
        rest = mat_cols(xn, columns_of(gain))
        s_all = [[part[j][i] + rest[j][i] for j in range(5)] for i in range(5)]
        difference = [[s[i][j] - xn[i][j] for j in range(5)] for i in range(5)]
        moved = mat_cols(difference, [v])[0]
        g_all = [g[i] + moved[i] for i in range(5)]
        eliminate(piece, lax.rem(piece + 1, count), s_all, g_all)
        return carry

    lax.fori_loop(1, count, forward, 0)
    out_ref[...] = jnp.zeros((count, 16, 128), F32)

    def backward(at, following):
        piece = count - 1 - at
        h = [[gains[piece, pl.ds(5 * i + j, 1), :] for j in range(5)] for i in range(5)]
        v = [gains[piece, pl.ds(25 + i, 1), :] for i in range(5)]
        moved = mat_cols(h, [list(following)])[0]
        here = tuple((following[i] - moved[i]) + v[i] for i in range(5))
        for i in range(5):
            out_ref[piece, pl.ds(5 + i, 1), :] = here[i]

        @pl.when(piece + 1 < count)
        def _():
            for i in range(5):
                out_ref[piece + 1, pl.ds(i, 1), :] = here[i]

        return here

    start = tuple(jnp.zeros((1, 128), F32) for _ in range(5))
    lax.fori_loop(0, count, backward, start)


def begin_backward(count, lines, ends_ref, mid_ref, edge, ends8):
    per = 128 // lines
    lanes = lax.broadcasted_iota(jnp.int32, (16, 128), 1)
    for z in range(4):
        block = ends_ref[per * z]
        for q in range(1, per):
            moved = pltpu.roll(ends_ref[per * z + q], lines * q, 1)
            block = jnp.where(lanes >= lines * q, moved, block)
        for e in range(10):
            ends8[e, pl.ds(2 * z, 1), :] = block[e : e + 1]
            ends8[e, pl.ds(2 * z + 1, 1), :] = block[e : e + 1]
    a = [ends8[i] for i in range(5)]
    c = [ends8[5 + i] for i in range(5)]
    gap = [c[i] - a[i] for i in range(5)]
    part = mat_cols(load_mat(mid_ref, 0), [gap])[0]
    rest = mat_cols(load_mat(mid_ref, 25), [a])[0]
    even = even_rows()
    for i in range(5):
        middle = a[i] + ((part[i] + rest[i]) + mid_ref[50 + i])
        edge[i] = jnp.where(even, a[i], pltpu.roll(middle, 1, 0))
        edge[5 + i] = jnp.where(even, middle, c[i])


def backward_chunk(fac_ref, edge, out):
    step = pl.program_id(0)
    a = [edge[i] for i in range(5)]
    begin = jnp.where(step == 0, 1, 0)

    def one(at, following):
        slot = CHUNK - 1 - at
        k = (STEPS - 1 - step) * CHUNK + slot
        gap = [following[i] - a[i] for i in range(5)]
        r = [[fac_ref[slot, 5 * i + j] for j in range(5)] for i in range(5)]
        x = [[fac_ref[slot, 25 + 5 * i + j] for j in range(5)] for i in range(5)]
        part = mat_cols(r, [gap])[0]
        rest = mat_cols(x, [a])[0]
        here = tuple(
            following[i] - ((part[i] + rest[i]) + fac_ref[slot, 50 + i]) for i in range(5)
        )
        for i in range(5):
            out[i, cell_rows(k), :] = here[i]
        return here

    final = lax.fori_loop(begin, CHUNK, one, tuple(edge[5 + i] for i in range(5)))
    for i in range(5):
        edge[5 + i] = final[i]


def backward_x_kernel(count, lines, fac_ref, mid_ref, ends_ref, out_ref, edge, ends8):
    @pl.when(pl.program_id(0) == 0)
    def _():
        begin_backward(count, lines, ends_ref, mid_ref, edge, ends8)
        for i in range(5):
            out_ref[i, cell_rows(HALF - 1), :] = edge[5 + i]

    backward_chunk(fac_ref, edge, out_ref)


def backward_y_kernel(count, lines, fac_ref, mid_ref, ends_ref, out_ref, edge, ends8, field):
    @pl.when(pl.program_id(0) == 0)
    def _():
        begin_backward(count, lines, ends_ref, mid_ref, edge, ends8)
        for i in range(5):
            field[i, cell_rows(HALF - 1), :] = edge[5 + i]

    backward_chunk(fac_ref, edge, field)

    @pl.when(pl.program_id(0) == STEPS - 1)
    def _():
        for c in range(5):
            for z in range(4):
                rows = pl.ds(128 * z, 128)
                out_ref[c, rows, :] = field[c, rows, :].T


def whole(shape):
    return pl.BlockSpec(shape, lambda i: (0,) * len(shape))


def scalars():
    return pl.BlockSpec(memory_space=pltpu.SMEM)


def params():
    return pltpu.CompilerParams(
        dimension_semantics=("arbitrary",), vmem_limit_bytes=VMEM_LIMIT
    )


FORWARD_OUT = (
    jax.ShapeDtypeStruct((HALF, 55, 8, 128), F32),
    jax.ShapeDtypeStruct((512, 128), F32),
    jax.ShapeDtypeStruct((55, 8, 128), F32),
)


def forward_specs():
    return (
        pl.BlockSpec((CHUNK, 55, 8, 128), lambda i: (i, 0, 0, 0)),
        whole((512, 128)),
        whole((55, 8, 128)),
    )


def plane():
    return pltpu.VMEM((512, 128), F32)


def forward_x(first, last, q, visc, mx, my, jacx, jacy, west, east, south, north):
    return pl.pallas_call(
        forward_x_kernel,
        grid=(STEPS,),
        in_specs=[scalars(), scalars()]
        + [whole(v.shape) for v in (q, visc, mx, my, jacx, jacy, west, east, south, north)],
        out_specs=forward_specs(),
        out_shape=FORWARD_OUT,
        scratch_shapes=[pltpu.VMEM((STATE, 8, 128), F32)]
        + [plane() for _ in range(5)]
        + [
            pltpu.VMEM((128, 128), F32),
            pltpu.VMEM((5, 8, 128), F32),
            pltpu.VMEM((5, 8, 128), F32),
            pltpu.VMEM((1024, 128), F32),
            pltpu.VMEM((8, 128), F32),
        ],
        compiler_params=params(),
        name="forward_x",
    )(first, last, q, visc, mx, my, jacx, jacy, west, east, south, north)


def forward_y(first, p, visc, my, jacy, south):
    return pl.pallas_call(
        forward_y_kernel,
        grid=(STEPS,),
        in_specs=[scalars()] + [whole(v.shape) for v in (p, visc, my, jacy, south)],
        out_specs=forward_specs(),
        out_shape=FORWARD_OUT,
        scratch_shapes=[pltpu.VMEM((STATE, 8, 128), F32), pltpu.VMEM((5, 512, 128), F32)]
        + [plane() for _ in range(3)]
        + [
            pltpu.VMEM((128, 128), F32),
            pltpu.VMEM((1024, 128), F32),
            pltpu.VMEM((8, 128), F32),
        ],
        compiler_params=params(),
        name="forward_y",
    )(first, p, visc, my, jacy, south)


def reduced(port, axis):
    count = lax.axis_size(axis)
    lines = 512 // count
    received = lax.all_to_all(
        port.reshape(count, lines, 128), axis, split_axis=0, concat_axis=0, tiled=True
    )
    ends = pl.pallas_call(
        functools.partial(reduced_kernel, count, lines),
        out_shape=jax.ShapeDtypeStruct((count, 16, 128), F32),
        in_specs=[pl.BlockSpec(memory_space=pltpu.VMEM)],
        out_specs=pl.BlockSpec(memory_space=pltpu.VMEM),
        scratch_shapes=[
            pltpu.VMEM((count, 128, 128), F32),
            pltpu.VMEM((count, 32, 128), F32),
        ],
        compiler_params=pltpu.CompilerParams(vmem_limit_bytes=VMEM_LIMIT),
        name="reduced_" + axis,
    )(received.reshape(512, 128))
    return lax.all_to_all(ends, axis, split_axis=0, concat_axis=0, tiled=True)


def backward(kernel, name, fac, mid, ends, extra):
    count = ends.shape[0]
    return pl.pallas_call(
        functools.partial(kernel, count, 512 // count),
        grid=(STEPS,),
        in_specs=[
            pl.BlockSpec((CHUNK, 55, 8, 128), lambda i: (STEPS - 1 - i, 0, 0, 0)),
            whole(mid.shape),
            whole(ends.shape),
        ],
        out_specs=whole((5, 512, 128)),
        out_shape=jax.ShapeDtypeStruct((5, 512, 128), F32),
        scratch_shapes=[pltpu.VMEM((10, 8, 128), F32), pltpu.VMEM((10, 8, 128), F32)] + extra,
        compiler_params=params(),
        name=name,
    )(fac, mid, ends)


def halos(axis, last, initial):
    devices = lax.axis_size(axis)
    up = [(i, (i + 1) % devices) for i in range(devices)]
    down = [(j, i) for i, j in up]
    return lax.ppermute(last, axis, up), lax.ppermute(initial, axis, down)


def body(flow_state, viscosity, metric_x, metric_y, jacobian_x, jacobian_y):
    spots = [lax.axis_index("row"), lax.axis_index("col")]
    sizes = [lax.axis_size("row"), lax.axis_size("col")]
    first = jnp.stack([(spot == 0).astype(jnp.int32) for spot in spots])
    last = jnp.stack([(spot == n - 1).astype(jnp.int32) for spot, n in zip(spots, sizes)])
    jacx = jacobian_x.reshape(25, 128)
    jacy = jacobian_y.reshape(25, 128)

    def last_cell(state, visc, metric, jac):
        entries = jnp.pad(jac[:, 127], (0, 103))[None]
        return jnp.concatenate([state.reshape(20, 128), visc, metric[None], entries], axis=0)

    west, east = halos(
        "row",
        last_cell(flow_state[:, :, 127], viscosity[:, 127], metric_x[127], jacx),
        flow_state[:, :, 0].reshape(20, 128),
    )
    south, north = halos(
        "col",
        last_cell(flow_state[:, :, :, 127], viscosity[:, :, 127], metric_y[:, 127], jacy),
        flow_state[:, :, :, 0].reshape(20, 128),
    )
    q = flow_state.reshape(5, 512, 128)
    visc = viscosity.reshape(512, 128)
    fac, port, mid = forward_x(
        first, last, q, visc, metric_x, metric_y, jacx, jacy, west, east, south, north
    )
    ends = reduced(port, "row")
    partial_value = backward(backward_x_kernel, "backward_x", fac, mid, ends, [])
    fac, port, mid = forward_y(first, partial_value, visc, metric_y, jacy, south)
    ends = reduced(port, "col")
    result = backward(
        backward_y_kernel, "backward_y", fac, mid, ends, [pltpu.VMEM((5, 512, 128), F32)]
    )
    return result.reshape(5, 4, 128, 128)


def solution(mesh):
    return jax.shard_map(
        body,
        mesh=mesh,
        in_specs=(
            P(None, None, "row", "col"),
            P(None, "row", "col"),
            P("row", "col"),
            P("row", "col"),
            P(None, None, "row"),
            P(None, None, "col"),
        ),
        out_specs=P(None, None, "row", "col"),
        check_vma=False,
    )
```

profile of v0, /device:TPU:0, one launch (start us, length us, event | category | flops | bytes accessed | tf_op | source)
XLA Modules:
  0.0 134.5 jit_solution(5959697283621572693)
XLA Ops:
  0.0 1.0 slice_reduce_fusion.5
  1.0 0.0 copy-start.3
  1.0 0.0 copy-start.1
  1.0 0.0 copy-start.4
  1.0 0.0 copy-start.2
  1.1 0.0 copy-start.5
  1.1 0.0 copy-start
  1.1 2.3 %collective-permute-start.1 = (f32[20,128]{1,0:T(8,128)S(1)}, f32[20,128]{1,0:T(8,128)S(1)}, u32[]{:S(2)}, u32[]{:S(2)}) collective-permute-start(f32[20,128]{1,0:T(8,128)S(1)} %reshape_squeeze.13), channel_id=1, source_target_pairs={{16,0},{32,16},{48,32},{64,48},{80,64},{96,80},{112,96},{0,112},{1... | collective-permute-start | bytes 30728 | tf_op jit(solution)/shard_map/ppermute | solution.py:632
  3.4 2.8 %slice_reduce_fusion = (f32[5,4,128]{2,1,0:T(4,128)S(1)}, f32[5,4,128]{2,1,0:T(4,128)S(1)}) fusion(f32[5,4,128,128]{3,2,1,0:T(8,128)} %param.6), kind=kLoop, calls=%fused_computation | loop fusion | bytes 40960 | tf_op jit(solution)/shard_map/slice | solution.py:655
  6.2 6.6 %collective-permute-start.3 = (f32[20,128]{1,0:T(8,128)S(1)}, f32[20,128]{1,0:T(8,128)S(1)}, u32[]{:S(2)}, u32[]{:S(2)}) collective-permute-start(f32[20,128]{1,0:T(8,128)S(1)} %reshape_squeeze.15), channel_id=1, source_target_pairs={{1,0},{2,1},{3,2},{4,3},{5,4},{6,5},{7,6},{8,7},{9,8},{10,9},{11,1... | collective-permute-start | bytes 30728 | tf_op jit(solution)/shard_map/ppermute | solution.py:632
  12.8 0.0 copy-done.3
  12.8 0.0 copy-done.1
  12.8 0.0 copy-done.4
  12.8 0.2 slice_reduce_fusion.4
  13.0 0.0 collective-permute-start
  13.1 0.1 slice.36
  13.2 0.0 copy-done.2
  13.2 0.2 slice_reduce_fusion.2
  13.4 0.0 copy-done.5
  13.4 0.2 slice_reduce_fusion.3
  13.6 0.1 copy.14
  13.7 0.1 collective-permute-start.2
  13.8 0.1 add_convert_fusion
  13.9 0.0 collective-permute-done.1.east_ref
  13.9 0.3 collective-permute-done.3.north_ref
  14.2 3.2 %collective-permute-done.west_ref = f32[26,128]{1,0:T(8,128)S(1)} collective-permute-done((f32[26,128]{1,0:T(8,128)S(1)}, f32[26,128]{1,0:T(8,128)S(1)}, u32[]{:S(2)}, u32[]{:S(2)}) %collective-permute-start) | collective-permute-done | bytes 13344 | tf_op jit(solution)/shard_map/ppermute | solution.py:632
  17.4 3.4 %collective-permute-done.2.south_ref = f32[26,128]{1,0:T(8,128)S(1)} collective-permute-done((f32[26,128]{1,0:T(8,128)S(1)}, f32[26,128]{1,0:T(8,128)S(1)}, u32[]{:S(2)}, u32[]{:S(2)}) %collective-permute-start.2) | collective-permute-done | bytes 13344 | tf_op jit(solution)/shard_map/ppermute | solution.py:632
  20.9 0.0 copy-done
  20.9 27.4 %forward_x.1 = (f32[64,55,8,128]{3,2,1,0:T(8,128)}, f32[512,128]{1,0:T(8,128)S(1)}, f32[55,8,128]{2,1,0:T(8,128)S(1)}) custom-call(s32[2]{0:T(128)S(1)} %get-tuple-element.21.first_ref, s32[2]{0:T(128)S(1)} %get-tuple-element.22.last_ref, f32[5,512,128]{2,1,0:T(8,128)S(1)} %bitcast.22, f32[512,128]{1,0:T(8,128)S(1)} %bitcast.23, f32[128,128]{1,0:T(8,128)S(1)} %copy-done.3, ...), custom_call_target="tpu_custom_call" | custom-call | tf_op jit(solution)/shard_map/forward_x/pallas_call | solution.py:549
  48.2 10.4 %all_to_all.20 = f32[8,64,128]{2,1,0:T(8,128)S(1)} all-to-all(f32[8,64,128]{2,1,0:T(8,128)S(1)} %bitcast.27), channel_id=1, replica_groups=mesh['row'=8,'col'=16] {'row'}, dimensions={0} | all-to-all | bytes 524288 | tf_op jit(solution)/shard_map/all_to_all | solution.py:592
  58.6 1.5 %reduced_row.1 = f32[8,16,128]{2,1,0:T(8,128)S(1)} custom-call(f32[512,128]{1,0:T(8,128)S(1)} %bitcast.25), custom_call_target="tpu_custom_call" | custom-call | tf_op jit(solution)/shard_map/reduced_row/pallas_call | solution.py:595
  60.1 8.0 %all_to_all.21.ends_ref = f32[8,16,128]{2,1,0:T(8,128)S(1)} all-to-all(f32[8,16,128]{2,1,0:T(8,128)S(1)} %reduced_row.1), channel_id=1, replica_groups=mesh['row'=8,'col'=16] {'row'}, dimensions={0} | all-to-all | bytes 131072 | tf_op jit(solution)/shard_map/all_to_all | solution.py:607
  68.1 8.0 %backward_x.1.p_ref = f32[5,512,128]{2,1,0:T(8,128)S(1)} custom-call(f32[64,55,8,128]{3,2,1,0:T(8,128)} %get-tuple-element.11.fac_ref, f32[55,8,128]{2,1,0:T(8,128)S(1)} %get-tuple-element.12.mid_ref, f32[8,16,128]{2,1,0:T(8,128)S(1)} %all_to_all.21.ends_ref), custom_call_target="tpu_custom_call" | custom-call | tf_op jit(solution)/shard_map/backward_x/pallas_call | solution.py:612
  76.1 23.4 %forward_y.1 = (f32[64,55,8,128]{3,2,1,0:T(8,128)}, f32[512,128]{1,0:T(8,128)S(1)}, f32[55,8,128]{2,1,0:T(8,128)S(1)}) custom-call(s32[2]{0:T(128)S(1)} %get-tuple-element.21.first_ref, f32[5,512,128]{2,1,0:T(8,128)S(1)} %backward_x.1.p_ref, f32[512,128]{1,0:T(8,128)S(1)} %bitcast.24, f32[128,128]{1,0:T(8,128)S(1)} %copy-done.2, ...), custom_call_target="tpu_custom_call" | custom-call | tf_op jit(solution)/shard_map/forward_y/pallas_call | solution.py:571
  99.5 11.2 %all_to_all.22 = f32[16,32,128]{2,1,0:T(8,128)S(1)} all-to-all(f32[16,32,128]{2,1,0:T(8,128)S(1)} %bitcast.28), channel_id=1, replica_groups=mesh['row'=8,'col'=16] {'col'}, dimensions={0} | all-to-all | bytes 524288 | tf_op jit(solution)/shard_map/all_to_all | solution.py:592
  110.7 3.0 %reduced_col.1 = f32[16,16,128]{2,1,0:T(8,128)S(1)} custom-call(f32[512,128]{1,0:T(8,128)S(1)} %bitcast.26), custom_call_target="tpu_custom_call" | custom-call | tf_op jit(solution)/shard_map/reduced_col/pallas_call | solution.py:595
  113.8 11.3 %all_to_all.23.ends_ref = f32[16,16,128]{2,1,0:T(8,128)S(1)} all-to-all(f32[16,16,128]{2,1,0:T(8,128)S(1)} %reduced_col.1), channel_id=1, replica_groups=mesh['row'=8,'col'=16] {'col'}, dimensions={0} | all-to-all | bytes 262144 | tf_op jit(solution)/shard_map/all_to_all | solution.py:607
  125.1 9.5 %backward_y.1 = f32[5,512,128]{2,1,0:T(8,128)} custom-call(f32[64,55,8,128]{3,2,1,0:T(8,128)} %get-tuple-element.14.fac_ref, f32[55,8,128]{2,1,0:T(8,128)S(1)} %get-tuple-element.15.mid_ref, f32[16,16,128]{2,1,0:T(8,128)S(1)} %all_to_all.23.ends_ref), custom_call_target="tpu_custom_call" | custom-call | tf_op jit(solution)/shard_map/backward_y/pallas_call | solution.py:612
  (12 shorter events, 0.1 us)
Async XLA Ops:
  1.0 11.8 %copy-start.3 = (f32[128,128]{1,0:T(8,128)S(1)}, f32[128,128]{1,0:T(8,128)}, u32[]{:S(2)}) copy-start(f32[128,128]{1,0:T(8,128)} %mx_ref.1) | copy-start | bytes 196612
  1.0 11.8 %copy-start.1 = (f32[4,128,128]{2,1,0:T(8,128)S(1)}, f32[4,128,128]{2,1,0:T(8,128)}, u32[]{:S(2)}) copy-start(f32[4,128,128]{2,1,0:T(8,128)} %param.7) | copy-start | bytes 786436
  1.0 11.8 %copy-start.4 = (f32[5,5,128]{2,1,0:T(8,128)S(1)}, f32[5,5,128]{2,1,0:T(8,128)}, u32[]{:S(2)}) copy-start(f32[5,5,128]{2,1,0:T(8,128)} %param.10) | copy-start | bytes 38404
  1.0 12.2 %copy-start.2 = (f32[128,128]{1,0:T(8,128)S(1)}, f32[128,128]{1,0:T(8,128)}, u32[]{:S(2)}) copy-start(f32[128,128]{1,0:T(8,128)} %my_ref.3) | copy-start | bytes 196612
  1.1 12.3 %copy-start.5 = (f32[5,5,128]{2,1,0:T(8,128)S(1)}, f32[5,5,128]{2,1,0:T(8,128)}, u32[]{:S(2)}) copy-start(f32[5,5,128]{2,1,0:T(8,128)} %param.11) | copy-start | bytes 38404
  1.1 19.8 %copy-start = (f32[5,4,128,128]{3,2,1,0:T(8,128)S(1)}, f32[5,4,128,128]{3,2,1,0:T(8,128)}, u32[]{:S(2)}) copy-start(f32[5,4,128,128]{3,2,1,0:T(8,128)} %param.6) | copy-start | bytes 3932164
  1.1 12.8 %collective-permute-start.1 = (f32[20,128]{1,0:T(8,128)S(1)}, f32[20,128]{1,0:T(8,128)S(1)}, u32[]{:S(2)}, u32[]{:S(2)}) collective-permute-start(f32[20,128]{1,0:T(8,128)S(1)} %reshape_squeeze.13), channel_id=1, source_target_pairs={{16,0},{32,16},{48,32},{64,48},{80,64},{96,80},{112,96},{0,112},{1... | collective-permute-start | bytes 30728 | tf_op jit(solution)/shard_map/ppermute | solution.py:632
  6.2 8.0 %collective-permute-start.3 = (f32[20,128]{1,0:T(8,128)S(1)}, f32[20,128]{1,0:T(8,128)S(1)}, u32[]{:S(2)}, u32[]{:S(2)}) collective-permute-start(f32[20,128]{1,0:T(8,128)S(1)} %reshape_squeeze.15), channel_id=1, source_target_pairs={{1,0},{2,1},{3,2},{4,3},{5,4},{6,5},{7,6},{8,7},{9,8},{10,9},{11,1... | collective-permute-start | bytes 30728 | tf_op jit(solution)/shard_map/ppermute | solution.py:632
  13.0 4.4 %collective-permute-start = (f32[26,128]{1,0:T(8,128)S(1)}, f32[26,128]{1,0:T(8,128)S(1)}, u32[]{:S(2)}, u32[]{:S(2)}) collective-permute-start(f32[26,128]{1,0:T(8,128)S(1)} %pad_maximum_fusion), channel_id=1, source_target_pairs={{0,16},{16,32},{32,48},{48,64},{64,80},{80,96},{96,112},{112,0},{1... | collective-permute-start | bytes 39944 | tf_op jit(solution)/shard_map/ppermute | solution.py:632
  13.7 7.1 %collective-permute-start.2 = (f32[26,128]{1,0:T(8,128)S(1)}, f32[26,128]{1,0:T(8,128)S(1)}, u32[]{:S(2)}, u32[]{:S(2)}) collective-permute-start(f32[26,128]{1,0:T(8,128)S(1)} %pad_maximum_fusion.1), channel_id=1, source_target_pairs={{0,1},{1,2},{2,3},{3,4},{4,5},{5,6},{6,7},{7,8},{8,9},{9,10},{10,1... | collective-permute-start | bytes 39944 | tf_op jit(solution)/shard_map/ppermute | solution.py:632
where the time goes:
time: 135 us
  Pallas kernels  72.7 us (54%)
  blocking collectives  40.9 us (30%)
  starting transfers between devices  8.94 us (7%)
  waiting for transfers between devices  6.96 us (5%)
  local copies, waits for them, and re-layouts  4.68 us (3%)
    pallas_call x1, Pallas kernels, forward_x(): pl.pallas_call(forward_x_kernel, grid=(STEPS,), in_specs=[scalars(), scal...  27.4 us
    pallas_call x1, Pallas kernels, forward_y(): pl.pallas_call(forward_y_kernel, grid=(STEPS,), in_specs=[scalars()] + [w...  23.4 us
    all_to_all x2, blocking collectives, reduced(): lax.all_to_all(port.reshape(count, lines, 128), axis, split_axis=0, conca...  21.6 us
    all_to_all x2, blocking collectives, reduced(): return lax.all_to_all(ends, axis, split_axis=0, concat_axis=0, tiled=True)  19.3 us
    pallas_call x2, Pallas kernels, backward(): pl.pallas_call(functools.partial(kernel, count, 512 // count), grid=(STEP...  17.4 us
    ppermute x4, starting transfers between devices, halos(): return (lax.ppermute(last, axis, up), lax.ppermute(initial, axis, down))  8.94 us
    ppermute x4, waiting for transfers between devices, halos(): return (lax.ppermute(last, axis, up), lax.ppermute(initial, axis, down))  6.96 us
    pallas_call x2, Pallas kernels, reduced(): pl.pallas_call(functools.partial(reduced_kernel, count, lines), out_shape...  4.52 us
  transfers between devices with their start and end apart: 4, of which 3 were waited for; matrix products, arithmetic and copies ran while one was open for 3% of the time, Pallas kernels for 0%

commit v1 on v0

v1 whole, which is shorter than its diff:
```python
import functools

import jax
import jax.numpy as jnp
from jax import lax
from jax.experimental import pallas as pl
from jax.experimental.pallas import tpu as pltpu
from jax.sharding import PartitionSpec as P

F32 = jnp.float32
N = 128
HALF = 64
KEPT = HALF // 2
CHUNK = 8
STEPS = KEPT // CHUNK
FACTORS = 60
VMEM_LIMIT = 48 * 1024 * 1024


def zeros():
    return jnp.zeros((8, 128), F32)


def ones():
    return jnp.ones((8, 128), F32)


def lane(value, index):
    return jnp.broadcast_to(value[:, index : index + 1], (8, 128))


def mat_cols(matrix, columns):
    result = []
    for column in columns:
        out = []
        for i in range(5):
            total = matrix[i][0] * column[0]
            for k in range(1, 5):
                total = total + matrix[i][k] * column[k]
            out.append(total)
        result.append(out)
    return result


def solve(matrix, columns):
    m = [list(row) for row in matrix]
    cols = [list(column) for column in columns]
    inverse = []
    for p in range(5):
        inv = 1.0 / m[p][p]
        inverse.append(inv)
        for i in range(p + 1, 5):
            weight = m[i][p] * inv
            for j in range(p + 1, 5):
                m[i][j] = m[i][j] - weight * m[p][j]
            for column in cols:
                column[i] = column[i] - weight * column[p]
    for column in cols:
        for i in range(4, -1, -1):
            total = column[i]
            for j in range(i + 1, 5):
                total = total - m[i][j] * column[j]
            column[i] = total * inverse[i]
    return cols


def columns_of(matrix):
    return [[matrix[i][j] for i in range(5)] for j in range(5)]


def rows_of(columns):
    return [[columns[j][i] for j in range(5)] for i in range(5)]


def load_mat(ref, base):
    return [[ref[base + 5 * i + j] for j in range(5)] for i in range(5)]


def load_vec(ref, base):
    return [ref[base + i] for i in range(5)]


def store_mat(ref, base, matrix):
    for i in range(5):
        for j in range(5):
            ref[base + 5 * i + j] = matrix[i][j]


def store_vec(ref, base, vector):
    for i in range(5):
        ref[base + i] = vector[i]


R_AT, X_AT, W_AT, Q_AT, XQ_AT, Y_AT, STATE = 0, 25, 50, 55, 80, 105, 110


def init_state(state):
    for i in range(5):
        for j in range(5):
            state[R_AT + 5 * i + j] = ones() if i == j else zeros()
            state[X_AT + 5 * i + j] = zeros()
        state[W_AT + i] = zeros()


def init_first_edge(state):
    for i in range(5):
        for j in range(5):
            state[Q_AT + 5 * i + j] = ones() if i == j else zeros()
            state[XQ_AT + 5 * i + j] = zeros()
        state[Y_AT + i] = zeros()


def accumulate(state, r, x, w):
    q = load_mat(state, Q_AT)
    xq = load_mat(state, XQ_AT)
    y = load_vec(state, Y_AT)
    moved = mat_cols(q, columns_of(r) + columns_of(x) + [w])
    q_new = [[q[i][j] - moved[j][i] for j in range(5)] for i in range(5)]
    xq_new = [[xq[i][j] - moved[5 + j][i] for j in range(5)] for i in range(5)]
    y_new = [y[i] - moved[10][i] for i in range(5)]
    store_mat(state, Q_AT, q_new)
    store_mat(state, XQ_AT, xq_new)
    store_vec(state, Y_AT, y_new)
    return q_new, xq_new, y_new


def table_mat(table, base):
    return [[lane(table, base + 5 * i + j) for j in range(5)] for i in range(5)]


def kept_equation(m, source, tab, eps, dlt, last):
    k = 2 * m + 1
    here, back = cell_rows(k), cell_rows(k - 1)
    table = tab[here, :]
    e0, d0 = eps[here, :], dlt[here, :]
    em, dm = eps[back, :], dlt[back, :]
    cm = 1.0 / (2.0 + dm)
    a = table_mat(table, 0)
    a1, a2 = cm * e0, cm * em
    a3 = a1 * em
    am, aam = table_mat(tab[back, :], 0), table_mat(table, 35)
    lower = [
        [(a1 * a[i][j] + a2 * am[i][j]) + a3 * aam[i][j] for j in range(5)] for i in range(5)
    ]
    fm, f0, fp = source
    low = cm * dm
    if last:
        shift, tilt = d0 + low, e0 * low
        first = [cm * fm[i] for i in range(5)]
        second = first
    else:
        ahead = cell_rows(k + 1)
        ep, dp = eps[ahead, :], dlt[ahead, :]
        cp = 1.0 / (2.0 + dp)
        b1, b2 = cp * e0, cp * ep
        b3 = b1 * ep
        ap, aap = table_mat(tab[ahead, :], 0), table_mat(table, 60)
        upper = [
            [b3 * aap[i][j] - (b1 * a[i][j] + b2 * ap[i][j]) for j in range(5)] for i in range(5)
        ]
        high = cp * dp
        shift, tilt = d0 + (low + high), e0 * (low - high)
        first = [cm * fm[i] + cp * fp[i] for i in range(5)]
        second = [cm * fm[i] - cp * fp[i] for i in range(5)]
    excess = [[tilt * a[i][j] for j in range(5)] for i in range(5)]
    for i in range(5):
        excess[i][i] = excess[i][i] + shift
        lower[i][i] = lower[i][i] + cm
        if not last:
            upper[i][i] = upper[i][i] + cp
    moved = mat_cols(a, [[e0 * value for value in second]])[0]
    right = [(f0[i] + first[i]) + moved[i] for i in range(5)]
    if last:
        speed = [[e0 * a[i][j] for j in range(5)] for i in range(5)]
        return lower, excess, right, speed
    return lower, excess, right, upper


def local_relation(lower, excess, right, r, x, w):
    cols = mat_cols(lower, columns_of(r) + columns_of(x) + [w])
    s = [[cols[j][i] + excess[i][j] for j in range(5)] for i in range(5)]
    xn = [[cols[5 + j][i] + excess[i][j] for j in range(5)] for i in range(5)]
    g = [right[i] - cols[10][i] for i in range(5)]
    return s, xn, g


def sweep_step(m, state, fac_ref, slot, raw, keep, tables):
    @pl.when(m == 1)
    def _():
        init_first_edge(state)

    r = load_mat(state, R_AT)
    x = load_mat(state, X_AT)
    w = load_vec(state, W_AT)
    fm = load_vec(keep, 0)
    f0, fp = raw(2 * m + 1), raw(2 * m + 2)
    lower, excess, right, upper = kept_equation(m, (fm, f0, fp), *tables, False)
    s, xn, g = local_relation(lower, excess, right, r, x, w)
    t = [[s[i][j] + upper[i][j] for j in range(5)] for i in range(5)]
    solved = solve(t, columns_of(s) + columns_of(xn) + [g])
    r_new = rows_of(solved[:5])
    x_new = rows_of(solved[5:10])
    w_new = [-value for value in solved[10]]
    accumulate(state, r, x, w)
    store_mat(state, R_AT, r_new)
    store_mat(state, X_AT, x_new)
    store_vec(state, W_AT, w_new)
    store_vec(keep, 0, fp)
    for i in range(5):
        for j in range(5):
            fac_ref[slot, 5 * i + j] = r_new[i][j]
            fac_ref[slot, 25 + 5 * i + j] = x_new[i][j]
        fac_ref[slot, 50 + i] = w_new[i]
        fac_ref[slot, 55 + i] = fp[i]


def even_rows():
    return lax.broadcasted_iota(jnp.int32, (8, 128), 0) % 2 == 0


def finish_sweep(first, state, port, port_ref, mid_ref, raw, keep, tables):
    tab, eps, dlt = tables
    r = load_mat(state, R_AT)
    x = load_mat(state, X_AT)
    w = load_vec(state, W_AT)
    q, xq, y = accumulate(state, r, x, w)
    rows = cell_rows(0)
    e0, d0 = eps[rows, :], dlt[rows, :]
    c0 = 1.0 / (2.0 + d0)
    start_speed = [[e0 * value for value in row] for row in table_mat(tab[rows, :], 0)]
    cols = mat_cols(start_speed, columns_of(q) + columns_of(xq) + [y])
    q = [[c0 * (q[i][j] - cols[j][i]) for j in range(5)] for i in range(5)]
    xq = [[c0 * (xq[i][j] - cols[5 + j][i]) for j in range(5)] for i in range(5)]
    for i in range(5):
        xq[i][i] = xq[i][i] - c0 * d0
    y = [c0 * ((y[i] - cols[10][i]) + mid_ref[55 + i]) for i in range(5)]
    source = (load_vec(keep, 0), raw(HALF - 1), None)
    lower, excess, right, speed = kept_equation(KEPT - 1, source, tab, eps, dlt, True)
    s, xn, g = local_relation(lower, excess, right, r, x, w)
    ahead = [[(1.0 if i == j else 0.0) - speed[i][j] for j in range(5)] for i in range(5)]
    scaled = solve(ahead, columns_of(s) + columns_of(xn) + [g])
    s, xn, g = rows_of(scaled[:5]), rows_of(scaled[5:10]), scaled[10]

    def from_second(value):
        return pltpu.roll(value, 7, 0)

    q1 = [[from_second(e) for e in row] for row in q]
    xq1 = [[from_second(e) for e in row] for row in xq]
    y1 = [from_second(e) for e in y]
    t = [[s[i][j] + (q1[i][j] - xq1[i][j]) for j in range(5)] for i in range(5)]
    mx_right = [[xq1[i][j] - xn[i][j] for j in range(5)] for i in range(5)]
    m0_right = [y1[i] + g[i] for i in range(5)]
    solved = solve(t, columns_of(q1) + columns_of(mx_right) + [m0_right])
    mc, mx, m0 = rows_of(solved[:5]), rows_of(solved[5:10]), solved[10]
    for i in range(5):
        for j in range(5):
            mid_ref[5 * i + j] = mc[i][j]
            mid_ref[25 + 5 * i + j] = mx[i][j]
        mid_ref[50 + i] = m0[i]
    left = mat_cols(q, solved)
    start = jnp.broadcast_to(first, (8, 128)) > 0
    s1 = [[from_second(e) for e in row] for row in s]
    xn1 = [[from_second(e) for e in row] for row in xn]
    g1 = [from_second(e) for e in g]
    n1 = [[xn1[i][j] - s1[i][j] for j in range(5)] for i in range(5)]
    cols = mat_cols(n1, solved)
    for i in range(5):
        for j in range(5):
            at = 5 * i + j
            unit = 1.0 if i == j else 0.0
            port[pl.ds(8 * at, 8), :] = s1[i][j] + cols[j][i]
            port[pl.ds(8 * (25 + at), 8), :] = xn1[i][j] + cols[5 + j][i]
            port[pl.ds(8 * (55 + at), 8), :] = jnp.where(start, unit, left[j][i])
            port[pl.ds(8 * (80 + at), 8), :] = jnp.where(start, 0.0, xq[i][j] + left[5 + j][i])
        port[pl.ds(8 * (50 + i), 8), :] = g1[i] - cols[10][i]
        port[pl.ds(8 * (105 + i), 8), :] = jnp.where(start, 0.0, y[i] + left[10][i])
    for e in range(110, 128):
        port[pl.ds(8 * e, 8), :] = zeros()
    for z in range(4):
        port_ref[pl.ds(128 * z, 128), :] = port[pl.ds(2 * z, 128, stride=8), :].T


def cell_rows(k):
    return pl.ds(k, 8, stride=HALF)


def start_tables(jac_ref, tin, turned):
    tin[...] = jnp.zeros((128, 128), F32)
    jac = jac_ref[...]
    tin[pl.ds(0, 25), :] = jac
    for base, shift in ((35, 1), (60, 127)):
        turned[...] = pltpu.roll(jac, shift, 1)
        for i in range(5):
            for j in range(5):
                total = jac_ref[pl.ds(5 * i, 1), :] * turned[pl.ds(j, 1), :]
                for k in range(1, 5):
                    total = total + jac_ref[pl.ds(5 * i + k, 1), :] * turned[pl.ds(5 * k + j, 1), :]
                tin[pl.ds(base + 5 * i + j, 1), :] = total


def start_sweep(state, keep, mid_ref, raw):
    init_state(state)
    init_first_edge(state)
    f = raw(0)
    for i in range(5):
        keep[i] = f[i]
        mid_ref[55 + i] = f[i]


def run_chunk(state, fac_ref, raw, keep, tables):
    step = pl.program_id(0)
    count = jnp.where(step == STEPS - 1, CHUNK - 1, CHUNK)

    def one(slot, carry):
        sweep_step(step * CHUNK + slot, state, fac_ref, slot, raw, keep, tables)
        return carry

    lax.fori_loop(0, count, one, 0)


def forward_x_kernel(
    first_ref, last_ref, q_ref, visc_ref, mx_ref, my_ref, jacx_ref, jacy_ref,
    south_ref, north_ref,
    fac_ref, port_ref, mid_ref, tab, eps, dlt,
    state, keep, g1, g2, tin, turned, port,
):
    step = pl.program_id(0)
    lanes = lax.broadcasted_iota(jnp.int32, (8, 128), 1)

    def raw(k):
        rows = cell_rows(k)
        table = tab[rows, :]
        d, a, b = dlt[rows, :], g1[rows, :], g2[rows, :]
        diff_y, base = [], []
        for c in range(5):
            here = q_ref[c, rows, :]
            south = jnp.where(lanes == 0, lane(table, 25 + c), pltpu.roll(here, 1, 1))
            north = jnp.where(lanes == 127, lane(table, 30 + c), pltpu.roll(here, 127, 1))
            diff_y.append(north - south)
            base.append(d * here + a * ((north - 2.0 * here) + south))
        right = []
        for i in range(5):
            total = jacy_ref[pl.ds(5 * i, 1), :] * diff_y[0]
            for j in range(1, 5):
                total = total + jacy_ref[pl.ds(5 * i + j, 1), :] * diff_y[j]
            right.append(base[i] - b * total)
        return right

    @pl.when(step == 0)
    def _():
        mx = mx_ref[...]
        my = my_ref[...]
        not_first = jnp.where(first_ref[1] > 0, 0.0, 1.0)
        not_last = jnp.where(last_ref[1] > 0, 0.0, 1.0)
        start_tables(jacx_ref, tin, turned)
        for z in range(4):
            rows = pl.ds(128 * z, 128)
            visc = visc_ref[rows, :]
            e = 1.0 / (visc * mx)
            d = e * e * visc
            eps[rows, :] = e
            dlt[rows, :] = d
            g2[rows, :] = d * my
            g1[rows, :] = (d * my) * (my * visc)
            for c in range(5):
                tin[pl.ds(25 + c, 1), :] = south_ref[pl.ds(4 * c + z, 1), :] * not_first
                tin[pl.ds(30 + c, 1), :] = north_ref[pl.ds(4 * c + z, 1), :] * not_last
            tab[rows, :] = tin[...].T
        start_sweep(state, keep, mid_ref, raw)

    tables = (tab, eps, dlt)
    run_chunk(state, fac_ref, raw, keep, tables)

    @pl.when(step == STEPS - 1)
    def _():
        finish_sweep(first_ref[0], state, port, port_ref, mid_ref, raw, keep, tables)


def forward_y_kernel(
    first_ref, p_ref, visc_ref, my_ref, jacy_ref,
    fac_ref, port_ref, mid_ref, tab, eps, dlt,
    state, keep, field, tin, turned, port,
):
    step = pl.program_id(0)

    def raw(k):
        rows = cell_rows(k)
        d = dlt[rows, :]
        return [d * field[c, rows, :] for c in range(5)]

    @pl.when(step == 0)
    def _():
        my = my_ref[...].T
        start_tables(jacy_ref, tin, turned)
        table = tin[...].T
        for z in range(4):
            rows = pl.ds(128 * z, 128)
            visc = visc_ref[rows, :].T
            e = 1.0 / (visc * my)
            eps[rows, :] = e
            dlt[rows, :] = e * e * visc
            tab[rows, :] = table
            for c in range(5):
                field[c, rows, :] = p_ref[c, rows, :].T
        start_sweep(state, keep, mid_ref, raw)

    tables = (tab, eps, dlt)
    run_chunk(state, fac_ref, raw, keep, tables)

    @pl.when(step == STEPS - 1)
    def _():
        finish_sweep(first_ref[1], state, port, port_ref, mid_ref, raw, keep, tables)


def reduced_kernel(count, lines, in_ref, out_ref, ports, gains):
    per = 128 // lines
    for group in range(count // per):
        turned = in_ref[pl.ds(128 * group, 128), :].T
        for q in range(per):
            ports[group * per + q] = turned if q == 0 else pltpu.roll(turned, 128 - lines * q, 1)

    def entry(piece, index):
        return ports[piece, pl.ds(index, 1), :]

    def matrix(piece, base):
        return [[entry(piece, base + 5 * i + j) for j in range(5)] for i in range(5)]

    def vector(piece, base):
        return [entry(piece, base + i) for i in range(5)]

    def eliminate(piece, following, s, g):
        qq, xx, yy = matrix(following, 55), matrix(following, 80), vector(following, 105)
        reduced = [[s[i][j] - xx[i][j] for j in range(5)] for i in range(5)]
        t = [[reduced[i][j] + qq[i][j] for j in range(5)] for i in range(5)]
        rhs = [yy[i] + g[i] for i in range(5)]
        solved = solve(t, columns_of(reduced) + [rhs])
        h, v = rows_of(solved[:5]), solved[5]
        for i in range(5):
            for j in range(5):
                gains[piece, pl.ds(5 * i + j, 1), :] = h[i][j]
            gains[piece, pl.ds(25 + i, 1), :] = v[i]

    eliminate(0, 1, matrix(0, 0), vector(0, 50))

    def forward(piece, carry):
        h = [[gains[piece - 1, pl.ds(5 * i + j, 1), :] for j in range(5)] for i in range(5)]
        v = [gains[piece - 1, pl.ds(25 + i, 1), :] for i in range(5)]
        s, xn, g = matrix(piece, 0), matrix(piece, 25), vector(piece, 50)
        gain = [[(1.0 if i == j else 0.0) - h[i][j] for j in range(5)] for i in range(5)]
        part = mat_cols(s, columns_of(h))
        rest = mat_cols(xn, columns_of(gain))
        s_all = [[part[j][i] + rest[j][i] for j in range(5)] for i in range(5)]
        difference = [[s[i][j] - xn[i][j] for j in range(5)] for i in range(5)]
        moved = mat_cols(difference, [v])[0]
        g_all = [g[i] + moved[i] for i in range(5)]
        eliminate(piece, lax.rem(piece + 1, count), s_all, g_all)
        return carry

    lax.fori_loop(1, count, forward, 0)
    out_ref[...] = jnp.zeros((count, 16, 128), F32)

    def backward(at, following):
        piece = count - 1 - at
        h = [[gains[piece, pl.ds(5 * i + j, 1), :] for j in range(5)] for i in range(5)]
        v = [gains[piece, pl.ds(25 + i, 1), :] for i in range(5)]
        moved = mat_cols(h, [list(following)])[0]
        here = tuple((following[i] - moved[i]) + v[i] for i in range(5))
        for i in range(5):
            out_ref[piece, pl.ds(5 + i, 1), :] = here[i]

        @pl.when(piece + 1 < count)
        def _():
            for i in range(5):
                out_ref[piece + 1, pl.ds(i, 1), :] = here[i]

        return here

    start = tuple(jnp.zeros((1, 128), F32) for _ in range(5))
    lax.fori_loop(0, count, backward, start)


def begin_backward(count, lines, ends_ref, mid_ref, edge, ends8):
    per = 128 // lines
    lanes = lax.broadcasted_iota(jnp.int32, (16, 128), 1)
    for z in range(4):
        block = ends_ref[per * z]
        for q in range(1, per):
            moved = pltpu.roll(ends_ref[per * z + q], lines * q, 1)
            block = jnp.where(lanes >= lines * q, moved, block)
        for e in range(10):
            ends8[e, pl.ds(2 * z, 1), :] = block[e : e + 1]
            ends8[e, pl.ds(2 * z + 1, 1), :] = block[e : e + 1]
    a = [ends8[i] for i in range(5)]
    c = [ends8[5 + i] for i in range(5)]
    gap = [c[i] - a[i] for i in range(5)]
    part = mat_cols(load_mat(mid_ref, 0), [gap])[0]
    rest = mat_cols(load_mat(mid_ref, 25), [a])[0]
    even = even_rows()
    for i in range(5):
        middle = a[i] + ((part[i] + rest[i]) + mid_ref[50 + i])
        edge[i] = jnp.where(even, a[i], pltpu.roll(middle, 1, 0))
        edge[5 + i] = jnp.where(even, middle, c[i])


def between(k, left, right, tables, source):
    tab, eps, dlt = tables
    rows = cell_rows(k)
    e, d = eps[rows, :], dlt[rows, :]
    c = 1.0 / (2.0 + d)
    gap = [right[i] - left[i] for i in range(5)]
    moved = mat_cols(table_mat(tab[rows, :], 0), [[e * value for value in gap]])[0]
    return [
        right[i] - c * ((gap[i] + moved[i]) + (d * right[i] - source[i])) for i in range(5)
    ]


def backward_chunk(fac_ref, mid_ref, edge, write, tables):
    step = pl.program_id(0)
    a = [edge[i] for i in range(5)]
    begin = jnp.where(step == 0, 1, 0)

    def one(at, following):
        slot = CHUNK - 1 - at
        m = (STEPS - 1 - step) * CHUNK + slot
        gap = [following[i] - a[i] for i in range(5)]
        r = [[fac_ref[slot, 5 * i + j] for j in range(5)] for i in range(5)]
        x = [[fac_ref[slot, 25 + 5 * i + j] for j in range(5)] for i in range(5)]
        part = mat_cols(r, [gap])[0]
        rest = mat_cols(x, [a])[0]
        here = tuple(
            following[i] - ((part[i] + rest[i]) + fac_ref[slot, 50 + i]) for i in range(5)
        )
        source = [fac_ref[slot, 55 + i] for i in range(5)]
        write(2 * m + 2, between(2 * m + 2, here, following, tables, source))
        write(2 * m + 1, here)
        return here

    final = lax.fori_loop(begin, CHUNK, one, tuple(edge[5 + i] for i in range(5)))
    for i in range(5):
        edge[5 + i] = final[i]

    @pl.when(step == STEPS - 1)
    def _():
        write(0, between(0, a, final, tables, [mid_ref[55 + i] for i in range(5)]))


def backward_x_kernel(
    count, lines, fac_ref, mid_ref, ends_ref, tab, eps, dlt, q_ref, out_ref, edge, ends8
):
    def write(k, value):
        rows = cell_rows(k)
        for i in range(5):
            out_ref[i, rows, :] = value[i] - q_ref[i, rows, :]

    @pl.when(pl.program_id(0) == 0)
    def _():
        begin_backward(count, lines, ends_ref, mid_ref, edge, ends8)
        write(HALF - 1, [edge[5 + i] for i in range(5)])

    backward_chunk(fac_ref, mid_ref, edge, write, (tab, eps, dlt))


def backward_y_kernel(
    count, lines, fac_ref, mid_ref, ends_ref, tab, eps, dlt, out_ref, edge, ends8, field
):
    def write(k, value):
        for i in range(5):
            field[i, cell_rows(k), :] = value[i]

    @pl.when(pl.program_id(0) == 0)
    def _():
        begin_backward(count, lines, ends_ref, mid_ref, edge, ends8)
        write(HALF - 1, [edge[5 + i] for i in range(5)])

    backward_chunk(fac_ref, mid_ref, edge, write, (tab, eps, dlt))

    @pl.when(pl.program_id(0) == STEPS - 1)
    def _():
        for c in range(5):
            for z in range(4):
                rows = pl.ds(128 * z, 128)
                out_ref[c, rows, :] = field[c, rows, :].T


def whole(shape):
    return pl.BlockSpec(shape, lambda i: (0,) * len(shape))


def scalars():
    return pl.BlockSpec(memory_space=pltpu.SMEM)


def params():
    return pltpu.CompilerParams(
        dimension_semantics=("arbitrary",), vmem_limit_bytes=VMEM_LIMIT
    )


PLANE = (512, 128)
FORWARD_OUT = tuple(
    jax.ShapeDtypeStruct(shape, F32)
    for shape in ((KEPT, FACTORS, 8, 128), PLANE, (60, 8, 128), PLANE, PLANE, PLANE)
)


def forward_specs():
    block = pl.BlockSpec((CHUNK, FACTORS, 8, 128), lambda i: (i, 0, 0, 0))
    return (block,) + tuple(whole(value.shape) for value in FORWARD_OUT[1:])


def forward_scratch(fields):
    return (
        [pltpu.VMEM((STATE, 8, 128), F32), pltpu.VMEM((5, 8, 128), F32)]
        + fields
        + [
            pltpu.VMEM((128, 128), F32),
            pltpu.VMEM((25, 128), F32),
            pltpu.VMEM((1024, 128), F32),
        ]
    )


def forward(kernel, name, flags, operands, fields):
    return pl.pallas_call(
        kernel,
        grid=(STEPS,),
        in_specs=[scalars() for _ in flags] + [whole(value.shape) for value in operands],
        out_specs=forward_specs(),
        out_shape=FORWARD_OUT,
        scratch_shapes=forward_scratch(fields),
        compiler_params=params(),
        name=name,
    )(*flags, *operands)


def reduced(port, axis):
    count = lax.axis_size(axis)
    lines = 512 // count
    received = lax.all_to_all(
        port.reshape(count, lines, 128), axis, split_axis=0, concat_axis=0, tiled=True
    )
    ends = pl.pallas_call(
        functools.partial(reduced_kernel, count, lines),
        out_shape=jax.ShapeDtypeStruct((count, 16, 128), F32),
        in_specs=[pl.BlockSpec(memory_space=pltpu.VMEM)],
        out_specs=pl.BlockSpec(memory_space=pltpu.VMEM),
        scratch_shapes=[
            pltpu.VMEM((count, 128, 128), F32),
            pltpu.VMEM((count, 32, 128), F32),
        ],
        compiler_params=pltpu.CompilerParams(vmem_limit_bytes=VMEM_LIMIT),
        name="reduced_" + axis,
    )(received.reshape(512, 128))
    return lax.all_to_all(ends, axis, split_axis=0, concat_axis=0, tiled=True)


def backward(kernel, name, operands, extra):
    count = operands[2].shape[0]
    return pl.pallas_call(
        functools.partial(kernel, count, 512 // count),
        grid=(STEPS,),
        in_specs=[pl.BlockSpec((CHUNK, FACTORS, 8, 128), lambda i: (STEPS - 1 - i, 0, 0, 0))]
        + [whole(value.shape) for value in operands[1:]],
        out_specs=whole((5, 512, 128)),
        out_shape=jax.ShapeDtypeStruct((5, 512, 128), F32),
        scratch_shapes=[pltpu.VMEM((10, 8, 128), F32), pltpu.VMEM((10, 8, 128), F32)] + extra,
        compiler_params=params(),
        name=name,
    )(*operands)


def halos(axis, last, initial):
    devices = lax.axis_size(axis)
    up = [(i, (i + 1) % devices) for i in range(devices)]
    down = [(j, i) for i, j in up]
    return lax.ppermute(last, axis, up), lax.ppermute(initial, axis, down)


def body(flow_state, viscosity, metric_x, metric_y, jacobian_x, jacobian_y):
    spots = [lax.axis_index("row"), lax.axis_index("col")]
    sizes = [lax.axis_size("row"), lax.axis_size("col")]
    first = jnp.stack([(spot == 0).astype(jnp.int32) for spot in spots])
    last = jnp.stack([(spot == n - 1).astype(jnp.int32) for spot, n in zip(spots, sizes)])
    jacx = jacobian_x.reshape(25, 128)
    jacy = jacobian_y.reshape(25, 128)

    south, north = halos(
        "col",
        flow_state[:, :, :, 127].reshape(20, 128),
        flow_state[:, :, :, 0].reshape(20, 128),
    )
    q = flow_state.reshape(5, 512, 128)
    visc = viscosity.reshape(512, 128)
    plane = [pltpu.VMEM(PLANE, F32), pltpu.VMEM(PLANE, F32)]
    field = pltpu.VMEM((5, 512, 128), F32)
    fac, port, mid, *tables = forward(
        forward_x_kernel, "forward_x", (first, last),
        (q, visc, metric_x, metric_y, jacx, jacy, south, north), plane,
    )
    ends = reduced(port, "row")
    partial_value = backward(
        backward_x_kernel, "backward_x", (fac, mid, ends, *tables, q), []
    )
    fac, port, mid, *tables = forward(
        forward_y_kernel, "forward_y", (first,), (partial_value, visc, metric_y, jacy), [field]
    )
    ends = reduced(port, "col")
    result = backward(
        backward_y_kernel, "backward_y", (fac, mid, ends, *tables), [field]
    )
    return result.reshape(5, 4, 128, 128)


def solution(mesh):
    return jax.shard_map(
        body,
        mesh=mesh,
        in_specs=(
            P(None, None, "row", "col"),
            P(None, "row", "col"),
            P("row", "col"),
            P("row", "col"),
            P(None, None, "row"),
            P(None, None, "col"),
        ),
        out_specs=P(None, None, "row", "col"),
        check_vma=False,
    )
```

time: 135 us -> 112 us (0.83)
  Pallas kernels: 72.7 us -> 54.7 us
  waiting for transfers between devices: 6.96 us -> 1.48 us
  blocking collectives: 40.9 us -> 46 us
  starting transfers between devices: 8.94 us -> 6.74 us
  local copies, waits for them, and re-layouts: 4.68 us -> 2.99 us
    pallas_call x2, Pallas kernels: 50.7 us -> 35.4 us  [forward(): pl.pallas_call(kernel, grid=(STEPS,), in_specs=[scalars() for _ in flags]...]
    ppermute x4 -> x2, waiting for transfers between devices: 6.96 us -> 1.48 us  [halos(): return (lax.ppermute(last, axis, up), lax.ppermute(initial, axis, down))]
    all_to_all x2, blocking collectives: 21.6 us -> 26.7 us  [reduced(): lax.all_to_all(port.reshape(count, lines, 128), axis, split_axis=0, conca...]
    pallas_call x2, Pallas kernels: 17.4 us -> 14.8 us  [backward(): pl.pallas_call(functools.partial(kernel, count, 512 // count), grid=(STEP...]
    ppermute x4 -> x2, starting transfers between devices: 8.94 us -> 6.74 us  [halos(): return (lax.ppermute(last, axis, up), lax.ppermute(initial, axis, down))]
    slice x7 -> x0, local copies, waits for them, and re-layouts: 1.65 us -> none  [the longest x1 0.99 us: body(): flow_state[:, :, 0].reshape(20, 128)]
  transfers between devices with their start and end apart: 4 -> 2, of which waited for: 3 -> 1; matrix products, arithmetic and copies ran while one was open for 3% -> 0% of each run, Pallas kernels for 0% -> 0%
where the time goes in v1:
time: 112 us
  Pallas kernels  54.7 us (49%)
  blocking collectives  46 us (41%)
  starting transfers between devices  6.74 us (6%)
  local copies, waits for them, and re-layouts  2.99 us (3%)
  waiting for transfers between devices  1.48 us (1%)
    pallas_call x2, Pallas kernels, forward(): pl.pallas_call(kernel, grid=(STEPS,), in_specs=[scalars() for _ in flags]...  35.4 us
    all_to_all x2, blocking collectives, reduced(): lax.all_to_all(port.reshape(count, lines, 128), axis, split_axis=0, conca...  26.7 us
    all_to_all x2, blocking collectives, reduced(): return lax.all_to_all(ends, axis, split_axis=0, concat_axis=0, tiled=True)  19.3 us
    pallas_call x2, Pallas kernels, backward(): pl.pallas_call(functools.partial(kernel, count, 512 // count), grid=(STEP...  14.8 us
    ppermute x2, starting transfers between devices, halos(): return (lax.ppermute(last, axis, up), lax.ppermute(initial, axis, down))  6.74 us
    pallas_call x2, Pallas kernels, reduced(): pl.pallas_call(functools.partial(reduced_kernel, count, lines), out_shape...  4.52 us
    slice x1, local copies, waits for them, and re-layouts, body(): flow_state[:, :, :, 0].reshape(20, 128)  2.94 us
  transfers between devices with their start and end apart: 2, of which 1 were waited for; matrix products, arithmetic and copies ran while one was open for 0% of the time, Pallas kernels for 0%

profile of v1, /device:TPU:0, one launch (start us, length us, event | category | flops | bytes accessed | tf_op | source)
XLA Modules:
  0.0 112.1 jit_solution(3259593236748402379)
XLA Ops:
  0.0 0.0 copy-start
  0.0 0.0 copy-start.4
  0.0 0.0 copy-start.5
  0.0 0.0 copy-start.2
  0.0 0.0 copy-start.3
  0.0 0.0 copy-start.1
  0.0 2.9 %slice_reduce_fusion = (f32[5,4,128]{2,1,0:T(4,128)S(1)}, f32[5,4,128]{2,1,0:T(4,128)S(1)}) fusion(f32[5,4,128,128]{3,2,1,0:T(8,128)} %param.6), kind=kLoop, calls=%fused_computation | loop fusion | bytes 40960 | tf_op jit(solution)/shard_map/slice | solution.py:690
  3.0 2.1 %collective-permute-start = (f32[20,128]{1,0:T(8,128)S(1)}, f32[20,128]{1,0:T(8,128)S(1)}, u32[]{:S(2)}, u32[]{:S(2)}) collective-permute-start(f32[20,128]{1,0:T(8,128)S(1)} %reshape_squeeze.6), channel_id=1, source_target_pairs={{0,1},{1,2},{2,3},{3,4},{4,5},{5,6},{6,7},{7,8},{8,9},{9,10},{10,1... | collective-permute-start | bytes 30728 | tf_op jit(solution)/shard_map/ppermute | solution.py:676
  5.1 4.7 %collective-permute-start.1 = (f32[20,128]{1,0:T(8,128)S(1)}, f32[20,128]{1,0:T(8,128)S(1)}, u32[]{:S(2)}, u32[]{:S(2)}) collective-permute-start(f32[20,128]{1,0:T(8,128)S(1)} %reshape_squeeze.7), channel_id=1, source_target_pairs={{1,0},{2,1},{3,2},{4,3},{5,4},{6,5},{7,6},{8,7},{9,8},{10,9},{11,1... | collective-permute-start | bytes 30728 | tf_op jit(solution)/shard_map/ppermute | solution.py:676
  9.7 0.1 add_convert_fusion
  9.8 0.0 copy-done.4
  9.8 0.0 copy-done.5
  9.8 1.5 %collective-permute-done.south_ref = f32[20,128]{1,0:T(8,128)S(1)} collective-permute-done((f32[20,128]{1,0:T(8,128)S(1)}, f32[20,128]{1,0:T(8,128)S(1)}, u32[]{:S(2)}, u32[]{:S(2)}) %collective-permute-start) | collective-permute-done | bytes 10272 | tf_op jit(solution)/shard_map/ppermute | solution.py:676
  11.3 0.0 collective-permute-done.1.north_ref
  11.3 0.0 copy-done
  11.3 0.0 copy-done.2
  11.3 0.0 copy-done.3
  11.3 0.0 copy-done.1
  11.3 18.6 %forward_x.1 = (f32[32,60,8,128]{3,2,1,0:T(8,128)}, f32[512,128]{1,0:T(8,128)S(1)}, f32[60,8,128]{2,1,0:T(8,128)S(1)}, f32[512,128]{1,0:T(8,128)S(1)}, f32[512,128]{1,0:T(8,128)S(1)}, /*index=5*/f32[512,128]{1,0:T(8,128)S(1)}) custom-call(s32[2]{0:T(128)S(1)} %get-tuple-element.31.first_ref, s32[2]{0:T(128)S(1)} %get-tuple-element.32.last_ref, ...), custom_call_target="tpu_custom_call" | custom-call | tf_op jit(solution)/shard_map/forward_x/pallas_call | solution.py:624
  29.9 11.6 %all_to_all.20 = f32[8,64,128]{2,1,0:T(8,128)S(1)} all-to-all(f32[8,64,128]{2,1,0:T(8,128)S(1)} %bitcast.17), channel_id=1, replica_groups=mesh['row'=8,'col'=16] {'row'}, dimensions={0} | all-to-all | bytes 524288 | tf_op jit(solution)/shard_map/all_to_all | solution.py:639
  41.6 1.5 %reduced_row.1 = f32[8,16,128]{2,1,0:T(8,128)S(1)} custom-call(f32[512,128]{1,0:T(8,128)S(1)} %bitcast.13), custom_call_target="tpu_custom_call" | custom-call | tf_op jit(solution)/shard_map/reduced_row/pallas_call | solution.py:642
  43.1 8.0 %all_to_all.21.ends_ref = f32[8,16,128]{2,1,0:T(8,128)S(1)} all-to-all(f32[8,16,128]{2,1,0:T(8,128)S(1)} %reduced_row.1), channel_id=1, replica_groups=mesh['row'=8,'col'=16] {'row'}, dimensions={0} | all-to-all | bytes 131072 | tf_op jit(solution)/shard_map/all_to_all | solution.py:654
  51.1 6.6 %backward_x.1.p_ref = f32[5,512,128]{2,1,0:T(8,128)S(1)} custom-call(f32[32,60,8,128]{3,2,1,0:T(8,128)} %get-tuple-element.17.fac_ref, f32[60,8,128]{2,1,0:T(8,128)S(1)} %get-tuple-element.18.mid_ref, f32[8,16,128]{2,1,0:T(8,128)S(1)} %all_to_all.21.ends_ref, f32[512,128]{1,0:T(8,128)S(1)} %get-tuple-element.20.tab, f32[512,128]{1,0:T(8,128)S(1)} %get-tuple-element.21.eps, ...), custom_call_target="tpu_custom_call" | custom-call | tf_op jit(solution)/shard_map/backward_x/pallas_call | solution.py:659
  57.7 16.8 %forward_y.1 = (f32[32,60,8,128]{3,2,1,0:T(8,128)}, f32[512,128]{1,0:T(8,128)S(1)}, f32[60,8,128]{2,1,0:T(8,128)S(1)}, f32[512,128]{1,0:T(8,128)S(1)}, f32[512,128]{1,0:T(8,128)S(1)}, /*index=5*/f32[512,128]{1,0:T(8,128)S(1)}) custom-call(s32[2]{0:T(128)S(1)} %get-tuple-element.31.first_ref, f32[5,512,128]{2,1,0:T(8,128)S(1)} %backward_x.1.p_ref, ...), custom_call_target="tpu_custom_call" | custom-call | tf_op jit(solution)/shard_map/forward_y/pallas_call | solution.py:624
  74.5 15.1 %all_to_all.22 = f32[16,32,128]{2,1,0:T(8,128)S(1)} all-to-all(f32[16,32,128]{2,1,0:T(8,128)S(1)} %bitcast.18), channel_id=1, replica_groups=mesh['row'=8,'col'=16] {'col'}, dimensions={0} | all-to-all | bytes 524288 | tf_op jit(solution)/shard_map/all_to_all | solution.py:639
  89.6 3.0 %reduced_col.1 = f32[16,16,128]{2,1,0:T(8,128)S(1)} custom-call(f32[512,128]{1,0:T(8,128)S(1)} %bitcast.14), custom_call_target="tpu_custom_call" | custom-call | tf_op jit(solution)/shard_map/reduced_col/pallas_call | solution.py:642
  92.6 11.3 %all_to_all.23.ends_ref = f32[16,16,128]{2,1,0:T(8,128)S(1)} all-to-all(f32[16,16,128]{2,1,0:T(8,128)S(1)} %reduced_col.1), channel_id=1, replica_groups=mesh['row'=8,'col'=16] {'col'}, dimensions={0} | all-to-all | bytes 262144 | tf_op jit(solution)/shard_map/all_to_all | solution.py:654
  103.9 8.2 %backward_y.1 = f32[5,512,128]{2,1,0:T(8,128)} custom-call(f32[32,60,8,128]{3,2,1,0:T(8,128)} %get-tuple-element.23.fac_ref, f32[60,8,128]{2,1,0:T(8,128)S(1)} %get-tuple-element.24.mid_ref, f32[16,16,128]{2,1,0:T(8,128)S(1)} %all_to_all.23.ends_ref, f32[512,128]{1,0:T(8,128)S(1)} %get-tuple-element.26.tab, f32[512,128]{1,0:T(8,128)S(1)} %get-tuple-element.27.eps, ...), custom_call_target="tpu_custom_call" | custom-call | tf_op jit(solution)/shard_map/backward_y/pallas_call | solution.py:659
  (4 shorter events, 0.0 us)
Async XLA Ops:
  0.0 11.3 %copy-start = (f32[5,4,128,128]{3,2,1,0:T(8,128)S(1)}, f32[5,4,128,128]{3,2,1,0:T(8,128)}, u32[]{:S(2)}) copy-start(f32[5,4,128,128]{3,2,1,0:T(8,128)} %param.6) | copy-start | bytes 3932164
  0.0 9.8 %copy-start.4 = (f32[5,5,128]{2,1,0:T(8,128)S(1)}, f32[5,5,128]{2,1,0:T(8,128)}, u32[]{:S(2)}) copy-start(f32[5,5,128]{2,1,0:T(8,128)} %param.11) | copy-start | bytes 38404
  0.0 9.8 %copy-start.5 = (f32[5,5,128]{2,1,0:T(8,128)S(1)}, f32[5,5,128]{2,1,0:T(8,128)}, u32[]{:S(2)}) copy-start(f32[5,5,128]{2,1,0:T(8,128)} %param.10) | copy-start | bytes 38404
  0.0 11.3 %copy-start.2 = (f32[128,128]{1,0:T(8,128)S(1)}, f32[128,128]{1,0:T(8,128)}, u32[]{:S(2)}) copy-start(f32[128,128]{1,0:T(8,128)} %my_ref.3) | copy-start | bytes 196612
  0.0 11.3 %copy-start.3 = (f32[128,128]{1,0:T(8,128)S(1)}, f32[128,128]{1,0:T(8,128)}, u32[]{:S(2)}) copy-start(f32[128,128]{1,0:T(8,128)} %mx_ref.1) | copy-start | bytes 196612
  0.0 11.3 %copy-start.1 = (f32[4,128,128]{2,1,0:T(8,128)S(1)}, f32[4,128,128]{2,1,0:T(8,128)}, u32[]{:S(2)}) copy-start(f32[4,128,128]{2,1,0:T(8,128)} %param.7) | copy-start | bytes 786436
  3.0 8.3 %collective-permute-start = (f32[20,128]{1,0:T(8,128)S(1)}, f32[20,128]{1,0:T(8,128)S(1)}, u32[]{:S(2)}, u32[]{:S(2)}) collective-permute-start(f32[20,128]{1,0:T(8,128)S(1)} %reshape_squeeze.6), channel_id=1, source_target_pairs={{0,1},{1,2},{2,3},{3,4},{4,5},{5,6},{6,7},{7,8},{8,9},{9,10},{10,1... | collective-permute-start | bytes 30728 | tf_op jit(solution)/shard_map/ppermute | solution.py:676
  5.1 6.2 %collective-permute-start.1 = (f32[20,128]{1,0:T(8,128)S(1)}, f32[20,128]{1,0:T(8,128)S(1)}, u32[]{:S(2)}, u32[]{:S(2)}) collective-permute-start(f32[20,128]{1,0:T(8,128)S(1)} %reshape_squeeze.7), channel_id=1, source_target_pairs={{1,0},{2,1},{3,2},{4,3},{5,4},{6,5},{7,6},{8,7},{9,8},{10,9},{11,1... | collective-permute-start | bytes 30728 | tf_op jit(solution)/shard_map/ppermute | solution.py:676

commit v2 on v1

v2 whole, which is shorter than its diff:
```python
import functools

import jax
import jax.numpy as jnp
from jax import lax
from jax.experimental import pallas as pl
from jax.experimental.pallas import tpu as pltpu
from jax.sharding import PartitionSpec as P

F32 = jnp.float32
N = 128
HALF = 64
KEPT = HALF // 2
CHUNK = 8
STEPS = KEPT // CHUNK
VMEM_LIMIT = 48 * 1024 * 1024


def zeros():
    return jnp.zeros((8, 128), F32)


def ones():
    return jnp.ones((8, 128), F32)


def lane(value, index):
    return jnp.broadcast_to(value[:, index : index + 1], (8, 128))


def mat_cols(matrix, columns):
    result = []
    for column in columns:
        out = []
        for i in range(5):
            total = matrix[i][0] * column[0]
            for k in range(1, 5):
                total = total + matrix[i][k] * column[k]
            out.append(total)
        result.append(out)
    return result


def inverse(matrix):
    m = [list(row) for row in matrix]
    for p in range(5):
        inv = 1.0 / m[p][p]
        for j in range(5):
            m[p][j] = inv if j == p else m[p][j] * inv
        for i in range(5):
            if i != p:
                weight = m[i][p]
                for j in range(5):
                    m[i][j] = -weight * inv if j == p else m[i][j] - weight * m[p][j]
    return m


def apply(matrix, vector):
    return mat_cols(matrix, [vector])[0]


def product(left, right):
    return rows_of(mat_cols(left, columns_of(right)))


def entrywise(function, *matrices):
    return [[function(*(m[i][j] for m in matrices)) for j in range(5)] for i in range(5)]


def add(left, right):
    return entrywise(lambda a, b: a + b, left, right)


def subtract(left, right):
    return entrywise(lambda a, b: a - b, left, right)


def unit_matrix():
    return [[ones() if i == j else zeros() for j in range(5)] for i in range(5)]


def zero_matrix():
    return [[zeros() for _ in range(5)] for _ in range(5)]


def columns_of(matrix):
    return [[matrix[i][j] for i in range(5)] for j in range(5)]


def rows_of(columns):
    return [[columns[j][i] for j in range(5)] for i in range(5)]


def load_vec(ref, base, *at):
    return [ref[(*at, base + i)] for i in range(5)]


def load_mat(ref, base, *at):
    return [load_vec(ref, base + 5 * i, *at) for i in range(5)]


def store_vec(ref, base, vector, *at):
    for i in range(5):
        ref[(*at, base + i)] = vector[i]


def store_mat(ref, base, matrix, *at):
    for i in range(5):
        store_vec(ref, base + 5 * i, matrix[i], *at)


def cell_rows(k):
    return pl.ds(k, 8, stride=HALF)


def even_rows():
    return lax.broadcasted_iota(jnp.int32, (8, 128), 0) % 2 == 0


def from_second(value):
    return pltpu.roll(value, 7, 0)


def table_mat(table, base):
    return [[lane(table, base + 5 * i + j) for j in range(5)] for i in range(5)]


R_AT, X_AT, Q_AT, XQ_AT, STATE = 0, 25, 50, 75, 100
LOWER_AT, PIVOT_AT, FIRST_AT, SWEEP = 0, 25, 50, 75


def kept_matrices(m, tables, last):
    tab, eps, dlt = tables
    k = 2 * m + 1
    here, back = cell_rows(k), cell_rows(k - 1)
    table = tab[here, :]
    e0, d0 = eps[here, :], dlt[here, :]
    em, dm = eps[back, :], dlt[back, :]
    cm = 1.0 / (2.0 + dm)
    a = table_mat(table, 0)
    a1, a2 = cm * e0, cm * em
    a3 = a1 * em
    am, aam = table_mat(tab[back, :], 0), table_mat(table, 35)
    lower = entrywise(lambda x, y, z: (a1 * x + a2 * y) + a3 * z, a, am, aam)
    low = cm * dm
    if last:
        shift, tilt = d0 + low, e0 * low
        upper = entrywise(lambda x: -(e0 * x), a)
    else:
        ahead = cell_rows(k + 1)
        ep, dp = eps[ahead, :], dlt[ahead, :]
        cp = 1.0 / (2.0 + dp)
        b1, b2 = cp * e0, cp * ep
        b3 = b1 * ep
        ap, aap = table_mat(tab[ahead, :], 0), table_mat(table, 60)
        upper = entrywise(lambda x, y, z: b3 * z - (b1 * x + b2 * y), a, ap, aap)
        high = cp * dp
        shift, tilt = d0 + (low + high), e0 * (low - high)
    excess = entrywise(lambda x: tilt * x, a)
    for i in range(5):
        excess[i][i] = excess[i][i] + shift
        lower[i][i] = lower[i][i] + cm
        upper[i][i] = upper[i][i] + (1.0 if last else cp)
    return lower, excess, upper


def kept_source(m, tables, fm, f0, fp):
    tab, eps, dlt = tables
    k = 2 * m + 1
    here = cell_rows(k)
    low = 1.0 / (2.0 + dlt[cell_rows(k - 1), :])
    first = [low * value for value in fm]
    second = first
    if fp is not None:
        high = 1.0 / (2.0 + dlt[cell_rows(k + 1), :])
        later = [high * value for value in fp]
        second = [first[i] - later[i] for i in range(5)]
        first = [first[i] + later[i] for i in range(5)]
    e0 = eps[here, :]
    moved = apply(table_mat(tab[here, :], 0), [e0 * value for value in second])
    return [(f0[i] + first[i]) + moved[i] for i in range(5)]


def left_part(lower, excess, r, x):
    cols = mat_cols(lower, columns_of(r) + columns_of(x))
    return add(rows_of(cols[:5]), excess), add(rows_of(cols[5:]), excess)


def accumulate(state, r, x):
    q = load_mat(state, Q_AT)
    moved = mat_cols(q, columns_of(r) + columns_of(x))
    q_new = subtract(q, rows_of(moved[:5]))
    xq_new = subtract(load_mat(state, XQ_AT), rows_of(moved[5:]))
    store_mat(state, Q_AT, q_new)
    store_mat(state, XQ_AT, xq_new)
    return q_new, xq_new


def matrix_step(m, state, sweep_ref, back_ref, slot, tables):
    @pl.when(m == 1)
    def _():
        store_mat(state, Q_AT, unit_matrix())
        store_mat(state, XQ_AT, zero_matrix())

    r = load_mat(state, R_AT)
    x = load_mat(state, X_AT)
    lower, excess, upper = kept_matrices(m, tables, False)
    s, xn = left_part(lower, excess, r, x)
    pivot = inverse(add(s, upper))
    solved = mat_cols(pivot, columns_of(s) + columns_of(xn))
    r_new, x_new = rows_of(solved[:5]), rows_of(solved[5:])
    q, _ = accumulate(state, r, x)
    store_mat(state, R_AT, r_new)
    store_mat(state, X_AT, x_new)
    store_mat(sweep_ref, LOWER_AT, lower, slot)
    store_mat(sweep_ref, PIVOT_AT, pivot, slot)
    store_mat(sweep_ref, FIRST_AT, q, slot)
    store_mat(back_ref, 0, r_new, slot)
    store_mat(back_ref, 25, x_new, slot)


def first_edge_scale(tables):
    tab, eps, dlt = tables
    rows = cell_rows(0)
    e0, d0 = eps[rows, :], dlt[rows, :]
    c0 = 1.0 / (2.0 + d0)
    return entrywise(lambda x: e0 * x, table_mat(tab[rows, :], 0)), c0, d0


def finish_matrices(first, state, sweep_ref, join_ref, mid_ref, port, port_ref, tables):
    r = load_mat(state, R_AT)
    x = load_mat(state, X_AT)
    q, xq = accumulate(state, r, x)
    speed, c0, d0 = first_edge_scale(tables)
    cols = mat_cols(speed, columns_of(q) + columns_of(xq))
    q = entrywise(lambda a, b: c0 * (a - b), q, rows_of(cols[:5]))
    xq = entrywise(lambda a, b: c0 * (a - b), xq, rows_of(cols[5:]))
    for i in range(5):
        xq[i][i] = xq[i][i] - c0 * d0
    lower, excess, ahead = kept_matrices(KEPT - 1, tables, True)
    s, xn = left_part(lower, excess, r, x)
    pivot = inverse(ahead)
    store_mat(sweep_ref, LOWER_AT, lower, CHUNK - 1)
    store_mat(sweep_ref, PIVOT_AT, pivot, CHUNK - 1)
    store_mat(sweep_ref, FIRST_AT, zero_matrix(), CHUNK - 1)
    s, xn = product(pivot, s), product(pivot, xn)
    q1 = entrywise(from_second, q)
    xq1 = entrywise(from_second, xq)
    coupling = inverse(add(s, subtract(q1, xq1)))
    mc = product(coupling, q1)
    mx = product(coupling, subtract(xq1, xn))
    store_mat(mid_ref, 0, mc)
    store_mat(mid_ref, 25, mx)
    s1 = entrywise(from_second, s)
    xn1 = entrywise(from_second, xn)
    n1 = subtract(xn1, s1)
    store_mat(join_ref, 0, coupling)
    store_mat(join_ref, 25, q)
    store_mat(join_ref, 50, n1)
    start = jnp.broadcast_to(first, (8, 128)) > 0
    ports = (
        add(s1, product(n1, mc)),
        add(xn1, product(n1, mx)),
        entrywise(lambda a, b: jnp.where(start, b, a), product(q, mc), unit_matrix()),
        entrywise(lambda a: jnp.where(start, 0.0, a), add(xq, product(q, mx))),
    )
    for at, matrix in enumerate(ports):
        for i in range(5):
            for j in range(5):
                port[pl.ds(8 * (25 * at + 5 * i + j), 8), :] = matrix[i][j]
    port_ref[...] = port[pl.ds(0, 400, stride=2), :]


def start_tables(jac_ref, tin, turned):
    tin[...] = jnp.zeros((128, 128), F32)
    jac = jac_ref[...]
    tin[pl.ds(0, 25), :] = jac
    for base, shift in ((35, 1), (60, 127)):
        turned[...] = pltpu.roll(jac, shift, 1)
        for i in range(5):
            for j in range(5):
                total = jac_ref[pl.ds(5 * i, 1), :] * turned[pl.ds(j, 1), :]
                for k in range(1, 5):
                    total = total + jac_ref[pl.ds(5 * i + k, 1), :] * turned[pl.ds(5 * k + j, 1), :]
                tin[pl.ds(base + 5 * i + j, 1), :] = total


def matrix_kernel(
    turn, first_ref, visc_ref, metric_ref, jac_ref,
    sweep_ref, back_ref, join_ref, mid_ref, port_ref, tab, eps, dlt,
    state, tin, turned, port,
):
    step = pl.program_id(0)

    @pl.when(step == 0)
    def _():
        store_mat(state, R_AT, unit_matrix())
        store_mat(state, X_AT, zero_matrix())
        store_mat(state, Q_AT, unit_matrix())
        store_mat(state, XQ_AT, zero_matrix())
        metric = metric_ref[...].T if turn else metric_ref[...]
        start_tables(jac_ref, tin, turned)
        table = tin[...].T
        for z in range(4):
            rows = pl.ds(128 * z, 128)
            visc = visc_ref[rows, :].T if turn else visc_ref[rows, :]
            e = 1.0 / (visc * metric)
            eps[rows, :] = e
            dlt[rows, :] = e * e * visc
            tab[rows, :] = table

    tables = (tab, eps, dlt)
    count = jnp.where(step == STEPS - 1, CHUNK - 1, CHUNK)

    def one(slot, carry):
        matrix_step(step * CHUNK + slot, state, sweep_ref, back_ref, slot, tables)
        return carry

    lax.fori_loop(0, count, one, 0)

    @pl.when(step == 0)
    def _():
        store_mat(sweep_ref, FIRST_AT, unit_matrix(), 0)

    @pl.when(step == STEPS - 1)
    def _():
        store_mat(back_ref, 0, zero_matrix(), CHUNK - 1)
        store_mat(back_ref, 25, zero_matrix(), CHUNK - 1)
        finish_matrices(
            first_ref[0], state, sweep_ref, join_ref, mid_ref, port, port_ref, tables
        )


def source_sweep(first, sweep_ref, join_ref, vec_ref, mid_ref, port_ref, state, port, raw, tables):
    step = pl.program_id(0)

    @pl.when(step == 0)
    def _():
        start = raw(0)
        for i in range(5):
            state[i] = zeros()
            state[5 + i] = zeros()
            state[10 + i] = start[i]
            mid_ref[5 + i] = start[i]

    count = jnp.where(step == STEPS - 1, CHUNK - 1, CHUNK)

    def one(slot, carry):
        w, y, fm = carry[:5], carry[5:10], carry[10:]
        m = step * CHUNK + slot
        fp = raw(2 * m + 2)
        right = kept_source(m, tables, fm, raw(2 * m + 1), fp)
        moved = apply(load_mat(sweep_ref, LOWER_AT, slot), w)
        w = apply(load_mat(sweep_ref, PIVOT_AT, slot), [moved[i] - right[i] for i in range(5)])
        moved = apply(load_mat(sweep_ref, FIRST_AT, slot), w)
        y = [y[i] - moved[i] for i in range(5)]
        store_vec(vec_ref, 0, w, slot)
        store_vec(vec_ref, 5, fp, slot)
        return tuple(w) + tuple(y) + tuple(fp)

    final = lax.fori_loop(0, count, one, tuple(state[i] for i in range(15)))
    for i in range(15):
        state[i] = final[i]

    @pl.when(step == STEPS - 1)
    def _():
        w, y, fm = load_vec(state, 0), load_vec(state, 5), load_vec(state, 10)
        for i in range(10):
            vec_ref[CHUNK - 1, i] = zeros()
        speed, c0, _ = first_edge_scale(tables)
        moved = apply(speed, y)
        y = [c0 * ((y[i] - moved[i]) + mid_ref[5 + i]) for i in range(5)]
        right = kept_source(KEPT - 1, tables, fm, raw(HALF - 1), None)
        moved = apply(load_mat(sweep_ref, LOWER_AT, CHUNK - 1), w)
        g = apply(
            load_mat(sweep_ref, PIVOT_AT, CHUNK - 1), [right[i] - moved[i] for i in range(5)]
        )
        y1, g1 = [from_second(e) for e in y], [from_second(e) for e in g]
        middle = apply(load_mat(join_ref, 0), [y1[i] + g[i] for i in range(5)])
        store_vec(mid_ref, 0, middle)
        ahead = apply(load_mat(join_ref, 25), middle)
        moved = apply(load_mat(join_ref, 50), middle)
        start = jnp.broadcast_to(first, (8, 128)) > 0
        for i in range(5):
            port[pl.ds(8 * i, 8), :] = g1[i] - moved[i]
            port[pl.ds(8 * (5 + i), 8), :] = jnp.where(start, 0.0, y[i] + ahead[i])
        port_ref[...] = port[pl.ds(0, 40, stride=2), :]


def source_x_kernel(
    first_ref, last_ref, sweep_ref, join_ref, tab, eps, dlt,
    q_ref, visc_ref, my_ref, jacy_ref, south_ref, north_ref,
    vec_ref, mid_ref, port_ref,
    state, port, g1, g2, beside, tin,
):
    lanes = lax.broadcasted_iota(jnp.int32, (8, 128), 1)

    def raw(k):
        rows = cell_rows(k)
        table = beside[rows, :]
        d, a, b = dlt[rows, :], g1[rows, :], g2[rows, :]
        diff_y, base = [], []
        for c in range(5):
            here = q_ref[c, rows, :]
            south = jnp.where(lanes == 0, lane(table, c), pltpu.roll(here, 1, 1))
            north = jnp.where(lanes == 127, lane(table, 5 + c), pltpu.roll(here, 127, 1))
            diff_y.append(north - south)
            base.append(d * here + a * ((north - 2.0 * here) + south))
        right = []
        for i in range(5):
            total = jacy_ref[pl.ds(5 * i, 1), :] * diff_y[0]
            for j in range(1, 5):
                total = total + jacy_ref[pl.ds(5 * i + j, 1), :] * diff_y[j]
            right.append(base[i] - b * total)
        return right

    @pl.when(pl.program_id(0) == 0)
    def _():
        my = my_ref[...]
        not_first = jnp.where(first_ref[1] > 0, 0.0, 1.0)
        not_last = jnp.where(last_ref[1] > 0, 0.0, 1.0)
        tin[...] = jnp.zeros((128, 128), F32)
        for z in range(4):
            rows = pl.ds(128 * z, 128)
            scaled = dlt[rows, :] * my
            g2[rows, :] = scaled
            g1[rows, :] = scaled * (my * visc_ref[rows, :])
            for c in range(5):
                tin[pl.ds(c, 1), :] = south_ref[pl.ds(4 * c + z, 1), :] * not_first
                tin[pl.ds(5 + c, 1), :] = north_ref[pl.ds(4 * c + z, 1), :] * not_last
            beside[rows, :] = tin[...].T

    source_sweep(
        first_ref[0], sweep_ref, join_ref, vec_ref, mid_ref, port_ref, state, port, raw,
        (tab, eps, dlt),
    )


def source_y_kernel(
    first_ref, sweep_ref, join_ref, tab, eps, dlt, p_ref,
    vec_ref, mid_ref, port_ref,
    state, port, field,
):
    def raw(k):
        rows = cell_rows(k)
        d = dlt[rows, :]
        return [d * field[c, rows, :] for c in range(5)]

    @pl.when(pl.program_id(0) == 0)
    def _():
        for z in range(4):
            rows = pl.ds(128 * z, 128)
            for c in range(5):
                field[c, rows, :] = p_ref[c, rows, :].T

    source_sweep(
        first_ref[1], sweep_ref, join_ref, vec_ref, mid_ref, port_ref, state, port, raw,
        (tab, eps, dlt),
    )


def line_vec(ref, piece, base):
    return [ref[piece, pl.ds(4 * (base + i), 4), :] for i in range(5)]


def line_mat(ref, piece, base):
    return [line_vec(ref, piece, base + 5 * i) for i in range(5)]


def put_line_mat(ref, piece, base, matrix):
    for i in range(5):
        for j in range(5):
            ref[piece, pl.ds(4 * (base + 5 * i + j), 4), :] = matrix[i][j]


def reduced_kernel(count, in_ref, out_ref):
    def eliminate(piece, following, s):
        reduced = subtract(s, line_mat(in_ref, following, 75))
        pivot = inverse(add(reduced, line_mat(in_ref, following, 50)))
        h = product(pivot, reduced)
        put_line_mat(out_ref, piece, 0, pivot)
        put_line_mat(out_ref, piece, 25, h)
        return h

    def forward(piece, flat):
        h = [list(flat[5 * i : 5 * i + 5]) for i in range(5)]
        s, xn = line_mat(in_ref, piece, 0), line_mat(in_ref, piece, 25)
        gain = [[(1.0 if i == j else 0.0) - h[i][j] for j in range(5)] for i in range(5)]
        put_line_mat(out_ref, piece, 50, subtract(s, xn))
        s_all = add(product(s, h), product(xn, gain))
        h = eliminate(piece, lax.rem(piece + 1, count), s_all)
        return tuple(value for row in h for value in row)

    h = eliminate(0, 1, line_mat(in_ref, 0, 0))
    for e in range(25):
        out_ref[0, pl.ds(4 * (50 + e), 4), :] = jnp.zeros((4, 128), F32)
    lax.fori_loop(1, count, forward, tuple(value for row in h for value in row))


def substitute(count, spots_ref, axis, red_ref, sources, gathered, values):
    inner = sources[0].shape[0]
    me = spots_ref[axis]
    outer_at, inner_at = me // inner, lax.rem(me, inner)
    for far, source in enumerate(sources):
        for near in range(inner):
            place = lax.rem(outer_at + far, 4) * inner + lax.rem(inner_at + near, inner)
            gathered[place] = source[near]
    zero = tuple(jnp.zeros((4, 128), F32) for _ in range(5))

    def forward(piece, v):
        moved = apply(line_mat(red_ref, piece, 50), list(v))
        g = line_vec(gathered, piece, 0)
        yy = line_vec(gathered, lax.rem(piece + 1, count), 5)
        v = apply(line_mat(red_ref, piece, 0), [(g[i] + moved[i]) + yy[i] for i in range(5)])
        for i in range(5):
            values[piece + 1, i] = v[i]
        return tuple(v)

    lax.fori_loop(0, count, forward, zero)

    def backward(at, p):
        piece = count - 1 - at
        moved = apply(line_mat(red_ref, piece, 25), list(p))
        p = tuple((p[i] - moved[i]) + values[piece + 1, i] for i in range(5))
        for i in range(5):
            values[piece + 1, i] = p[i]
        return p

    lax.fori_loop(0, count, backward, zero)
    for i in range(5):
        values[0, i] = zero[0]
    return [values[me, i] for i in range(5)], [values[me + 1, i] for i in range(5)]


def between(k, left, right, tables, source):
    tab, eps, dlt = tables
    rows = cell_rows(k)
    e, d = eps[rows, :], dlt[rows, :]
    c = 1.0 / (2.0 + d)
    gap = [right[i] - left[i] for i in range(5)]
    moved = apply(table_mat(tab[rows, :], 0), [e * value for value in gap])
    return [
        right[i] - c * ((gap[i] + moved[i]) + (d * right[i] - source[i])) for i in range(5)
    ]


def backward_sweep(
    count, axis, spots_ref, back_ref, vec_ref, join_ref, mid_ref, red_ref, sources, tables,
    edge, ends8, gathered, values, write,
):
    step = pl.program_id(0)

    @pl.when(step == 0)
    def _():
        left, right = substitute(count, spots_ref, axis, red_ref, sources, gathered, values)
        for i in range(5):
            for z in range(4):
                ends8[i, pl.ds(2 * z, 1), :] = left[i][z : z + 1]
                ends8[i, pl.ds(2 * z + 1, 1), :] = left[i][z : z + 1]
                ends8[5 + i, pl.ds(2 * z, 1), :] = right[i][z : z + 1]
                ends8[5 + i, pl.ds(2 * z + 1, 1), :] = right[i][z : z + 1]
        a, c = load_vec(ends8, 0), load_vec(ends8, 5)
        part = apply(load_mat(join_ref, 0), [c[i] - a[i] for i in range(5)])
        rest = apply(load_mat(join_ref, 25), a)
        even = even_rows()
        for i in range(5):
            middle = a[i] + ((part[i] + rest[i]) + mid_ref[i])
            edge[i] = jnp.where(even, a[i], pltpu.roll(middle, 1, 0))
            edge[5 + i] = jnp.where(even, middle, c[i])
        write(HALF - 1, load_vec(edge, 5))

    a = load_vec(edge, 0)
    begin = jnp.where(step == 0, 1, 0)

    def one(at, following):
        slot = CHUNK - 1 - at
        m = (STEPS - 1 - step) * CHUNK + slot
        part = apply(load_mat(back_ref, 0, slot), [following[i] - a[i] for i in range(5)])
        rest = apply(load_mat(back_ref, 25, slot), a)
        w, source = load_vec(vec_ref, 0, slot), load_vec(vec_ref, 5, slot)
        here = tuple(following[i] - ((part[i] + rest[i]) + w[i]) for i in range(5))
        write(2 * m + 2, between(2 * m + 2, here, following, tables, source))
        write(2 * m + 1, here)
        return here

    final = lax.fori_loop(begin, CHUNK, one, tuple(edge[5 + i] for i in range(5)))
    store_vec(edge, 5, final)

    @pl.when(step == STEPS - 1)
    def _():
        write(0, between(0, a, final, tables, load_vec(mid_ref, 5)))


def backward_x_kernel(
    count, spots_ref, back_ref, vec_ref, join_ref, mid_ref, red_ref, s0, s1, s2, s3,
    tab, eps, dlt, q_ref, out_ref, edge, ends8, gathered, values,
):
    def write(k, value):
        rows = cell_rows(k)
        for i in range(5):
            out_ref[i, rows, :] = value[i] - q_ref[i, rows, :]

    backward_sweep(
        count, 0, spots_ref, back_ref, vec_ref, join_ref, mid_ref, red_ref, (s0, s1, s2, s3),
        (tab, eps, dlt), edge, ends8, gathered, values, write,
    )


def backward_y_kernel(
    count, spots_ref, back_ref, vec_ref, join_ref, mid_ref, red_ref, s0, s1, s2, s3,
    tab, eps, dlt, out_ref, edge, ends8, gathered, values, field,
):
    def write(k, value):
        for i in range(5):
            field[i, cell_rows(k), :] = value[i]

    backward_sweep(
        count, 1, spots_ref, back_ref, vec_ref, join_ref, mid_ref, red_ref, (s0, s1, s2, s3),
        (tab, eps, dlt), edge, ends8, gathered, values, write,
    )

    @pl.when(pl.program_id(0) == STEPS - 1)
    def _():
        for c in range(5):
            for z in range(4):
                rows = pl.ds(128 * z, 128)
                out_ref[c, rows, :] = field[c, rows, :].T


def whole(shape):
    return pl.BlockSpec(shape, lambda i: (0,) * len(shape))


def rising(entries):
    return pl.BlockSpec((CHUNK, entries, 8, 128), lambda i: (i, 0, 0, 0))


def falling(entries):
    return pl.BlockSpec((CHUNK, entries, 8, 128), lambda i: (STEPS - 1 - i, 0, 0, 0))


def scalars():
    return pl.BlockSpec(memory_space=pltpu.SMEM)


def call(kernel, name, flags, operands, outputs, scratch, gflops):
    shapes = tuple(jax.ShapeDtypeStruct(shape, F32) for _, shape in outputs)
    moved = 4 * sum(value.size for _, value in operands)
    return pl.pallas_call(
        kernel,
        grid=(STEPS,),
        in_specs=[scalars() for _ in flags]
        + [whole(value.shape) if spec is None else spec for spec, value in operands],
        out_specs=tuple(whole(shape) if spec is None else spec for spec, shape in outputs),
        out_shape=shapes,
        scratch_shapes=[pltpu.VMEM(shape, F32) for shape in scratch],
        compiler_params=pltpu.CompilerParams(
            dimension_semantics=("arbitrary",), vmem_limit_bytes=VMEM_LIMIT
        ),
        cost_estimate=pl.CostEstimate(
            flops=int(gflops * 1e9), bytes_accessed=moved, transcendentals=0
        ),
        name=name,
    )(*flags, *(value for _, value in operands))


PLANE = (512, 128)
FIELD = (5, 512, 128)


def matrices(name, turn, first, visc, metric, jac):
    return call(
        functools.partial(matrix_kernel, turn),
        name,
        (first,),
        [(None, visc), (None, metric), (None, jac)],
        [
            (rising(SWEEP), (KEPT, SWEEP, 8, 128)),
            (rising(50), (KEPT, 50, 8, 128)),
            (None, (75, 8, 128)),
            (None, (50, 8, 128)),
            (None, (400, 128)),
            (None, PLANE),
            (None, PLANE),
            (None, PLANE),
        ],
        [(STATE, 8, 128), (128, 128), (25, 128), (800, 128)],
        0.12,
    )


SOURCE_OUT = [
    (rising(10), (KEPT, 10, 8, 128)),
    (None, (10, 8, 128)),
    (None, (40, 128)),
]


def reduced(name, ports):
    count = ports.shape[0]
    return pl.pallas_call(
        functools.partial(reduced_kernel, count),
        out_shape=jax.ShapeDtypeStruct((count, 300, 128), F32),
        in_specs=[pl.BlockSpec(memory_space=pltpu.VMEM)],
        out_specs=pl.BlockSpec(memory_space=pltpu.VMEM),
        compiler_params=pltpu.CompilerParams(vmem_limit_bytes=VMEM_LIMIT),
        name=name,
    )(ports)


def permute(value, axis, moves):
    return lax.ppermute(value, axis, moves)


def gather_sources(port, axis):
    count = lax.axis_size(axis)
    inner = count // 4
    groups = [port]
    for near in range(1, inner):
        moves = [((i // inner) * inner + (i + near) % inner, i) for i in range(count)]
        groups.append(permute(port, axis, moves))
    block = jnp.stack(groups)
    blocks = [block]
    for far in range(1, 4):
        moves = [((i + far * inner) % count, i) for i in range(count)]
        blocks.append(permute(block, axis, moves))
    return blocks


def after(value, other):
    return lax.optimization_barrier((value, other))[0]


def halos(axis, last, initial):
    devices = lax.axis_size(axis)
    up = [(i, (i + 1) % devices) for i in range(devices)]
    down = [(j, i) for i, j in up]
    return lax.ppermute(last, axis, up), lax.ppermute(initial, axis, down)


def body(flow_state, viscosity, metric_x, metric_y, jacobian_x, jacobian_y):
    spots = jnp.stack([lax.axis_index("row"), lax.axis_index("col")]).astype(jnp.int32)
    sizes = jnp.array([lax.axis_size("row"), lax.axis_size("col")], jnp.int32)
    first = (spots == 0).astype(jnp.int32)
    last = (spots == sizes - 1).astype(jnp.int32)
    jacx = jacobian_x.reshape(25, 128)
    jacy = jacobian_y.reshape(25, 128)
    south, north = halos(
        "col",
        flow_state[:, :, :, 127].reshape(20, 128),
        flow_state[:, :, :, 0].reshape(20, 128),
    )
    q = flow_state.reshape(5, 512, 128)
    visc = viscosity.reshape(512, 128)
    sweep_x, back_x, join_x, mid_x, port_x, *tables_x = matrices(
        "matrices_x", False, first, visc, metric_x, jacx
    )
    ports_x = lax.all_gather(port_x, "row")
    sweep_y, back_y, join_y, mid_y, port_y, *tables_y = matrices(
        "matrices_y", True, after(first[1:], port_x), visc, metric_y, jacy
    )
    ports_y = lax.all_gather(port_y, "col")
    vec, mid, port = call(
        source_x_kernel,
        "source_x",
        (after(first, port_y), last),
        [(rising(SWEEP), sweep_x), (None, join_x)]
        + [(None, value) for value in (*tables_x, q, visc, metric_y, jacy, south, north)],
        SOURCE_OUT,
        [(15, 8, 128), (80, 128), PLANE, PLANE, PLANE, (128, 128)],
        0.03,
    )
    sources = gather_sources(port, "row")
    red = reduced("reduced_x", after(ports_x, port))
    (partial_value,) = call(
        functools.partial(backward_x_kernel, 8),
        "backward_x",
        (spots,),
        [(falling(50), back_x), (falling(10), vec)]
        + [(None, value) for value in (mid_x, mid, red, *sources, *tables_x, q)],
        [(None, FIELD)],
        [(10, 8, 128), (10, 8, 128), (8, 40, 128), (9, 5, 4, 128)],
        0.03,
    )
    vec, mid, port = call(
        source_y_kernel,
        "source_y",
        (first,),
        [(rising(SWEEP), sweep_y), (None, join_y)]
        + [(None, value) for value in (*tables_y, partial_value)],
        SOURCE_OUT,
        [(15, 8, 128), (80, 128), FIELD],
        0.03,
    )
    sources = gather_sources(port, "col")
    red = reduced("reduced_y", after(ports_y, port))
    (result,) = call(
        functools.partial(backward_y_kernel, 16),
        "backward_y",
        (spots,),
        [(falling(50), back_y), (falling(10), vec)]
        + [(None, value) for value in (mid_y, mid, red, *sources, *tables_y)],
        [(None, FIELD)],
        [(10, 8, 128), (10, 8, 128), (16, 40, 128), (17, 5, 4, 128), FIELD],
        0.03,
    )
    return result.reshape(5, 4, 128, 128)


def solution(mesh):
    return jax.shard_map(
        body,
        mesh=mesh,
        in_specs=(
            P(None, None, "row", "col"),
            P(None, "row", "col"),
            P("row", "col"),
            P("row", "col"),
            P(None, None, "row"),
            P(None, None, "col"),
        ),
        out_specs=P(None, None, "row", "col"),
        check_vma=False,
    )
```

time: 112 us -> 133 us (1.19)
  blocking collectives: 46 us -> 0 us
  local copies, waits for them, and re-layouts: 2.99 us -> 19.8 us
  starting transfers between devices: 6.74 us -> 22.3 us
  Pallas kernels: 54.7 us -> 68.9 us
  between operations: 0.09 us -> 13.6 us
  waiting for transfers between devices: 1.48 us -> 6.79 us
    all_to_all x4 -> x0, blocking collectives: 46 us -> none  [the longest x2 26.7 us: reduced(): lax.all_to_all(port.reshape(count, lines, 128), axis, split_axis=0, conca...]
    unnamed x12 -> x52, local copies, waits for them, and re-layouts: 0.02 us -> 16.6 us
    ppermute x0 -> x10, starting transfers between devices: none -> 15.5 us  [permute(): return lax.ppermute(value, axis, moves)]
    pallas_call x6 -> x8, Pallas kernels: 54.7 us -> 68.9 us  [the longest x6 65.5 us: call(): pl.pallas_call(kernel, grid=(STEPS,), in_specs=[scalars() for _ in flags]...]
    ppermute x0 -> x10, waiting for transfers between devices: none -> 5.18 us  [permute(): return lax.ppermute(value, axis, moves)]
    slice x1, local copies, waits for them, and re-layouts: 2.94 us -> 1.12 us  [body(): flow_state[:, :, :, 0].reshape(20, 128)]
  transfers between devices with their start and end apart: 2 -> 14, of which waited for: 1 -> 7; matrix products, arithmetic and copies ran while one was open for 0% -> 2% of each run, Pallas kernels for 0% -> 33%
where the time goes in v2:
time: 133 us; the launch traced here: 132 us
  Pallas kernels  68.9 us (52%)
  starting transfers between devices  22.3 us (17%)
  local copies, waits for them, and re-layouts  19.8 us (15%)
  between operations  13.6 us (10%)
  waiting for transfers between devices  6.79 us (5%)
    pallas_call x6, Pallas kernels, call(): pl.pallas_call(kernel, grid=(STEPS,), in_specs=[scalars() for _ in flags]...  65.5 us
    unnamed x52, local copies, waits for them, and re-layouts  16.6 us
    ppermute x10, starting transfers between devices, permute(): return lax.ppermute(value, axis, moves)  15.5 us
    ppermute x2, starting transfers between devices, halos(): return (lax.ppermute(last, axis, up), lax.ppermute(initial, axis, down))  6.73 us
    ppermute x10, waiting for transfers between devices, permute(): return lax.ppermute(value, axis, moves)  5.18 us
    pallas_call x2, Pallas kernels, reduced(): pl.pallas_call(functools.partial(reduced_kernel, count), out_shape=jax.Sh...  3.42 us
  transfers between devices with their start and end apart: 14, of which 7 were waited for; matrix products, arithmetic and copies ran while one was open for 2% of the time, Pallas kernels for 33%

profile of v2, /device:TPU:0, one launch (start us, length us, event | category | flops | bytes accessed | tf_op | source)
XLA Modules:
  0.0 132.2 jit_solution(6162680295413969357)
XLA Ops:
  6.5 0.8 compare_convert_fusion
  7.4 0.7 reshape.16.jac_ref
  8.1 0.9 copy-done.16
  9.1 0.8 copy-done.25
  9.9 16.9 %matrices_x.1 = (f32[32,75,8,128]{3,2,1,0:T(8,128)}, f32[32,50,8,128]{3,2,1,0:T(8,128)}, f32[75,8,128]{2,1,0:T(8,128)S(1)}, f32[50,8,128]{2,1,0:T(8,128)S(1)}, f...) custom-call(s32[2]{0:T(128)S(1)} %compare_convert_fusion.1.first_ref, ...), custom_call_target="tpu_custom_call" | custom-call | flops 120000000 | bytes 340480 | tf_op jit(solution)/shard_map/matrices_x/pallas_call | solution.py:649
  26.8 0.7 copy-done.3
  27.5 0.7 copy-done.6
  28.2 0.7 copy-done.9
  28.9 0.7 copy-done.14
  29.6 0.7 copy-done.21
  30.4 0.6 slice.9.first_ref
  30.9 0.7 reshape.17.jac_ref.jacy_ref
  31.7 0.9 copy-done.17
  32.6 0.8 copy-done.23
  33.5 16.9 %matrices_y.1 = (f32[32,75,8,128]{3,2,1,0:T(8,128)}, f32[32,50,8,128]{3,2,1,0:T(8,128)}, f32[75,8,128]{2,1,0:T(8,128)S(1)}, f32[50,8,128]{2,1,0:T(8,128)S(1)}, f...) custom-call(s32[1]{0:T(128)} %slice.9.first_ref, ...), custom_call_target="tpu_custom_call" | custom-call | flops 120000000 | bytes 340480 | tf_op jit(solution)/shard_map/matrices_y/pallas_call | solution.py:649
  50.4 0.7 copy-done.12
  51.1 0.7 copy-done.19
  51.8 1.1 slice_reduce_fusion
  53.0 2.1 %collective-permute-start = (f32[20,128]{1,0:T(8,128)S(1)}, f32[20,128]{1,0:T(8,128)S(1)}, u32[]{:S(2)}, u32[]{:S(2)}) collective-permute-start(f32[20,128]{1,0:T(8,128)S(1)} %reshape_squeeze.6), channel_id=1, source_target_pairs={{0,1},{1,2},{2,3},{3,4},{4,5},{5,6},{6,7},{7,8},{8,9},{9,10},{10,1... | collective-permute-start | bytes 30728 | tf_op jit(solution)/shard_map/ppermute | solution.py:738
  55.1 4.7 %collective-permute-start.1 = (f32[20,128]{1,0:T(8,128)S(1)}, f32[20,128]{1,0:T(8,128)S(1)}, u32[]{:S(2)}, u32[]{:S(2)}) collective-permute-start(f32[20,128]{1,0:T(8,128)S(1)} %reshape_squeeze.7), channel_id=1, source_target_pairs={{1,0},{2,1},{3,2},{4,3},{5,4},{6,5},{7,6},{8,7},{9,8},{10,9},{11,1... | collective-permute-start | bytes 30728 | tf_op jit(solution)/shard_map/ppermute | solution.py:738
  59.7 1.6 %collective-permute-done.south_ref = f32[20,128]{1,0:T(8,128)S(1)} collective-permute-done((f32[20,128]{1,0:T(8,128)S(1)}, f32[20,128]{1,0:T(8,128)S(1)}, u32[]{:S(2)}, u32[]{:S(2)}) %collective-permute-start) | collective-permute-done | bytes 10272 | tf_op jit(solution)/shard_map/ppermute | solution.py:738
  61.3 0.9 copy-done.4
  62.3 0.9 copy-done.7
  63.2 0.9 copy-done.10
  64.2 1.0 copy-done.15
  65.1 0.9 copy-done.18
  66.1 8.5 %source_x.1 = (f32[32,10,8,128]{3,2,1,0:T(8,128)S(1)}, f32[10,8,128]{2,1,0:T(8,128)S(1)}, f32[40,128]{1,0:T(8,128)S(1)}) custom-call(s32[2]{0:T(128)S(1)} %compare_convert_fusion.1.first_ref, s32[2]{0:T(128)S(1)} %get-tuple-element.59.last_ref, f32[32,75,8,128]{3,2,1,0:T(8,128)} %get-tuple-element.42.sweep_ref, f32[75,8,128]{2,1,0:T(8,128)S(1)} %copy-done.15, ...), custom_call_target="tpu_custom_call" | custom-call | flops 30000000 | bytes 12595712 | tf_op jit(solution)/shard_map/source_x/pallas_call | solution.py:649
  74.6 1.2 collective-permute-done.2
  75.8 2.8 %collective-permute-start.3 = (f32[2,40,128]{2,1,0:T(8,128)S(1)}, f32[2,40,128]{2,1,0:T(8,128)S(1)}, u32[]{:S(2)}, u32[]{:S(2)}) collective-permute-start(f32[2,40,128]{2,1,0:T(8,128)S(1)} %pad_maximum_fusion.1.s0), channel_id=1, source_target_pairs={{32,0},{48,16},{64,32},{80,48},{96,64},{112,80},{0,96},{16,112},{3... | collective-permute-start | bytes 122888 | tf_op jit(solution)/shard_map/ppermute | solution.py:712
  78.6 0.8 collective-permute-start.4
  79.4 0.9 collective-permute-start.5
  80.3 1.4 %copy-done.2 = f32[3200,128]{1,0:T(8,128)S(1)} copy-done((f32[3200,128]{1,0:T(8,128)S(1)}, f32[3200,128]{1,0:T(8,128)}, u32[]{:S(2)}) %copy-start.2) | copy-done | bytes 1638424
  81.7 1.1 reduced_x.1.red_ref
  82.9 1.2 collective-permute-done.4.s2
  84.1 0.5 collective-permute-done.5.s3
  84.6 7.2 %backward_x.1.p_ref = f32[5,512,128]{2,1,0:T(8,128)S(1)} custom-call(s32[2]{0:T(128)S(1)} %get-tuple-element.60.spots_ref, f32[32,50,8,128]{3,2,1,0:T(8,128)} %get-tuple-element.39.back_ref, f32[32,10,8,128]{3,2,1,0:T(8,128)S(1)} %get-tuple-element.47.vec_ref, f32[50,8,128]{2,1,0:T(8,128)S(1)} %copy-done.22, f32[10,8,128]{2,1,0:T(8,128)S(1)} %get-tuple-element.49.mid_ref, ...), custom_call_target="tpu_custom_call" | custom-call | flops 30000000 | bytes 11599872 | tf_op jit(solution)/shard_map/backward_x/pallas_call | solution.py:649
  91.8 7.4 %source_y.1 = (f32[32,10,8,128]{3,2,1,0:T(8,128)S(1)}, f32[10,8,128]{2,1,0:T(8,128)S(1)}, f32[40,128]{1,0:T(8,128)S(1)}) custom-call(s32[2]{0:T(128)S(1)} %compare_convert_fusion.1.first_ref, f32[32,75,8,128]{3,2,1,0:T(8,128)} %get-tuple-element.34.sweep_ref, f32[75,8,128]{2,1,0:T(8,128)S(1)} %copy-done.13, f32[512,128]{1,0:T(8,128)S(1)} %get-tuple-element.36.tab, ...), custom_call_target="tpu_custom_call" | custom-call | flops 30000000 | bytes 12234752 | tf_op jit(solution)/shard_map/source_y/pallas_call | solution.py:649
  99.3 1.3 %collective-permute-start.7 = (f32[40,128]{1,0:T(8,128)S(1)}, f32[40,128]{1,0:T(8,128)S(1)}, u32[]{:S(2)}, u32[]{:S(2)}) collective-permute-start(f32[40,128]{1,0:T(8,128)S(1)} %get-tuple-element.55), channel_id=1, source_target_pairs={{2,0},{3,1},{0,2},{1,3},{6,4},{7,5},{4,6},{5,7},{10,8},{11,9},{8,1... | collective-permute-start | bytes 61448 | tf_op jit(solution)/shard_map/ppermute | solution.py:712
  100.6 1.5 %collective-permute-start.8 = (f32[40,128]{1,0:T(8,128)S(1)}, f32[40,128]{1,0:T(8,128)S(1)}, u32[]{:S(2)}, u32[]{:S(2)}) collective-permute-start(f32[40,128]{1,0:T(8,128)S(1)} %get-tuple-element.55), channel_id=1, source_target_pairs={{3,0},{0,1},{1,2},{2,3},{7,4},{4,5},{5,6},{6,7},{11,8},{8,9},{9,10... | collective-permute-start | bytes 61448 | tf_op jit(solution)/shard_map/ppermute | solution.py:712
  102.1 1.7 %collective-permute-start.6 = (f32[40,128]{1,0:T(8,128)S(1)}, f32[40,128]{1,0:T(8,128)S(1)}, u32[]{:S(2)}, u32[]{:S(2)}) collective-permute-start(f32[40,128]{1,0:T(8,128)S(1)} %get-tuple-element.55), channel_id=1, source_target_pairs={{1,0},{2,1},{3,2},{0,3},{5,4},{6,5},{7,6},{4,7},{9,8},{10,9},{11,1... | collective-permute-start | bytes 61448 | tf_op jit(solution)/shard_map/ppermute | solution.py:712
  103.9 1.2 collective-permute-done.7
  105.1 1.0 collective-permute-done.8
  106.1 3.2 %collective-permute-start.10 = (f32[4,40,128]{2,1,0:T(8,128)S(1)}, f32[4,40,128]{2,1,0:T(8,128)S(1)}, u32[]{:S(2)}, u32[]{:S(2)}) collective-permute-start(f32[4,40,128]{2,1,0:T(8,128)S(1)} %pad_maximum_fusion.s0), channel_id=1, source_target_pairs={{8,0},{9,1},{10,2},{11,3},{12,4},{13,5},{14,6},{15,7},{0,8},{1,9},... | collective-permute-start | bytes 245768 | tf_op jit(solution)/shard_map/ppermute | solution.py:712
  109.3 1.8 %collective-permute-start.11 = (f32[4,40,128]{2,1,0:T(8,128)S(1)}, f32[4,40,128]{2,1,0:T(8,128)S(1)}, u32[]{:S(2)}, u32[]{:S(2)}) collective-permute-start(f32[4,40,128]{2,1,0:T(8,128)S(1)} %pad_maximum_fusion.s0), channel_id=1, source_target_pairs={{12,0},{13,1},{14,2},{15,3},{0,4},{1,5},{2,6},{3,7},{4,8},{5,9},{6... | collective-permute-start | bytes 245768 | tf_op jit(solution)/shard_map/ppermute | solution.py:712
  111.1 1.5 %collective-permute-start.9 = (f32[4,40,128]{2,1,0:T(8,128)S(1)}, f32[4,40,128]{2,1,0:T(8,128)S(1)}, u32[]{:S(2)}, u32[]{:S(2)}) collective-permute-start(f32[4,40,128]{2,1,0:T(8,128)S(1)} %pad_maximum_fusion.s0), channel_id=1, source_target_pairs={{4,0},{5,1},{6,2},{7,3},{8,4},{9,5},{10,6},{11,7},{12,8},{13,9},{1... | collective-permute-start | bytes 245768 | tf_op jit(solution)/shard_map/ppermute | solution.py:712
  112.5 1.9 %copy-done.1 = f32[6400,128]{1,0:T(8,128)S(1)} copy-done((f32[6400,128]{1,0:T(8,128)S(1)}, f32[6400,128]{1,0:T(8,128)}, u32[]{:S(2)}) %copy-start.1) | copy-done | bytes 3276824
  114.4 2.3 %reduced_y.1.red_ref = f32[16,300,128]{2,1,0:T(8,128)S(1)} custom-call(f32[16,400,128]{2,1,0:T(8,128)S(1)} %bitcast.15), custom_call_target="tpu_custom_call" | custom-call | tf_op jit(solution)/shard_map/reduced_y/pallas_call | solution.py:701
  116.8 8.6 %backward_y.1 = f32[5,512,128]{2,1,0:T(8,128)} custom-call(s32[2]{0:T(128)S(1)} %get-tuple-element.60.spots_ref, f32[32,50,8,128]{3,2,1,0:T(8,128)} %get-tuple-element.33.back_ref, f32[32,10,8,128]{3,2,1,0:T(8,128)S(1)} %get-tuple-element.52.vec_ref, f32[50,8,128]{2,1,0:T(8,128)S(1)} %copy-done.20, f32[10,8,128]{2,1,0:T(8,128)S(1)} %get-tuple-element.54.mid_ref, ...), custom_call_target="tpu_custom_call" | custom-call | flops 30000000 | bytes 11681792 | tf_op jit(solution)/shard_map/backward_y/pallas_call | solution.py:649
  (52 shorter events, 0.4 us)
Async XLA Ops:
  6.5 45.3 %copy-start = (f32[5,4,128,128]{3,2,1,0:T(8,128)S(1)}, f32[5,4,128,128]{3,2,1,0:T(8,128)}, u32[]{:S(2)}) copy-start(f32[5,4,128,128]{3,2,1,0:T(8,128)} %param.7) | copy-start | bytes 3932164
  6.5 73.7 %all-gather.5.cloned.1.call-start = ((), (), s32[]{:S(2)}) async-start(), calls=%async_computation | async-start | bytes 1843200 | tf_op jit(solution)/shard_map/all_gather | solution.py:758
  8.1 0.9 copy-start.16
  9.1 0.8 copy-start.25
  26.8 0.7 copy-start.3
  27.5 0.7 copy-start.6
  28.2 0.7 copy-start.9
  28.9 0.7 copy-start.14
  29.6 0.7 copy-start.21
  30.3 82.2 %all-gather.7.cloned.1.call-start = ((), (), s32[]{:S(2)}) async-start(), calls=%async_computation.1 | async-start | bytes 3481600 | tf_op jit(solution)/shard_map/all_gather | solution.py:762
  31.7 0.9 copy-start.17
  32.6 0.8 copy-start.23
  50.4 0.7 copy-start.12
  51.1 0.7 copy-start.19
  51.8 9.5 %copy-start.24 = (f32[128,128]{1,0:T(8,128)S(1)}, f32[128,128]{1,0:T(8,128)}, u32[]{:S(2)}) copy-start(f32[128,128]{1,0:T(8,128)} %my_ref.1) | copy-start | bytes 196612
  53.0 8.3 %collective-permute-start = (f32[20,128]{1,0:T(8,128)S(1)}, f32[20,128]{1,0:T(8,128)S(1)}, u32[]{:S(2)}, u32[]{:S(2)}) collective-permute-start(f32[20,128]{1,0:T(8,128)S(1)} %reshape_squeeze.6), channel_id=1, source_target_pairs={{0,1},{1,2},{2,3},{3,4},{4,5},{5,6},{6,7},{7,8},{8,9},{9,10},{10,1... | collective-permute-start | bytes 30728 | tf_op jit(solution)/shard_map/ppermute | solution.py:738
  55.1 6.2 %collective-permute-start.1 = (f32[20,128]{1,0:T(8,128)S(1)}, f32[20,128]{1,0:T(8,128)S(1)}, u32[]{:S(2)}, u32[]{:S(2)}) collective-permute-start(f32[20,128]{1,0:T(8,128)S(1)} %reshape_squeeze.7), channel_id=1, source_target_pairs={{1,0},{2,1},{3,2},{4,3},{5,4},{6,5},{7,6},{8,7},{9,8},{10,9},{11,1... | collective-permute-start | bytes 30728 | tf_op jit(solution)/shard_map/ppermute | solution.py:738
  61.3 1.0 copy-start.4
  62.3 0.9 copy-start.7
  63.2 0.9 copy-start.10
  64.2 1.0 copy-start.15
  65.1 0.9 copy-start.18
  74.5 1.3 collective-permute-start.2
  75.8 7.0 %collective-permute-start.3 = (f32[2,40,128]{2,1,0:T(8,128)S(1)}, f32[2,40,128]{2,1,0:T(8,128)S(1)}, u32[]{:S(2)}, u32[]{:S(2)}) collective-permute-start(f32[2,40,128]{2,1,0:T(8,128)S(1)} %pad_maximum_fusion.1.s0), channel_id=1, source_target_pairs={{32,0},{48,16},{64,32},{80,48},{96,64},{112,80},{0,96},{16,112},{3... | collective-permute-start | bytes 122888 | tf_op jit(solution)/shard_map/ppermute | solution.py:712
  78.6 5.5 %collective-permute-start.4 = (f32[2,40,128]{2,1,0:T(8,128)S(1)}, f32[2,40,128]{2,1,0:T(8,128)S(1)}, u32[]{:S(2)}, u32[]{:S(2)}) collective-permute-start(f32[2,40,128]{2,1,0:T(8,128)S(1)} %pad_maximum_fusion.1.s0), channel_id=1, source_target_pairs={{64,0},{80,16},{96,32},{112,48},{0,64},{16,80},{32,96},{48,112},{6... | collective-permute-start | bytes 122888 | tf_op jit(solution)/shard_map/ppermute | solution.py:712
  79.4 5.2 %collective-permute-start.5 = (f32[2,40,128]{2,1,0:T(8,128)S(1)}, f32[2,40,128]{2,1,0:T(8,128)S(1)}, u32[]{:S(2)}, u32[]{:S(2)}) collective-permute-start(f32[2,40,128]{2,1,0:T(8,128)S(1)} %pad_maximum_fusion.1.s0), channel_id=1, source_target_pairs={{96,0},{112,16},{0,32},{16,48},{32,64},{48,80},{64,96},{80,112},{9... | collective-permute-start | bytes 122888 | tf_op jit(solution)/shard_map/ppermute | solution.py:712
  80.3 1.4 %copy-start.2 = (f32[3200,128]{1,0:T(8,128)S(1)}, f32[3200,128]{1,0:T(8,128)}, u32[]{:S(2)}) copy-start(f32[3200,128]{1,0:T(8,128)} %all-gather.5.cloned.1.call-done) | copy-start | bytes 4915204
  81.7 2.9 %copy-start.5 = (f32[512,128]{1,0:T(8,128)S(1)}, f32[512,128]{1,0:T(8,128)}, u32[]{:S(2)}) copy-start(f32[512,128]{1,0:T(8,128)} %copy-done.3) | copy-start | bytes 786436
  81.7 2.9 %copy-start.8 = (f32[512,128]{1,0:T(8,128)S(1)}, f32[512,128]{1,0:T(8,128)}, u32[]{:S(2)}) copy-start(f32[512,128]{1,0:T(8,128)} %copy-done.6) | copy-start | bytes 786436
  81.7 2.9 %copy-start.11 = (f32[512,128]{1,0:T(8,128)S(1)}, f32[512,128]{1,0:T(8,128)}, u32[]{:S(2)}) copy-start(f32[512,128]{1,0:T(8,128)} %copy-done.9) | copy-start | bytes 786436
  81.7 2.9 %copy-start.22 = (f32[50,8,128]{2,1,0:T(8,128)S(1)}, f32[50,8,128]{2,1,0:T(8,128)}, u32[]{:S(2)}) copy-start(f32[50,8,128]{2,1,0:T(8,128)} %copy-done.21) | copy-start | bytes 614404
  84.6 7.2 %copy-start.13 = (f32[75,8,128]{2,1,0:T(8,128)S(1)}, f32[75,8,128]{2,1,0:T(8,128)}, u32[]{:S(2)}) copy-start(f32[75,8,128]{2,1,0:T(8,128)} %copy-done.12) | copy-start | bytes 921604
  99.3 5.8 %collective-permute-start.7 = (f32[40,128]{1,0:T(8,128)S(1)}, f32[40,128]{1,0:T(8,128)S(1)}, u32[]{:S(2)}, u32[]{:S(2)}) collective-permute-start(f32[40,128]{1,0:T(8,128)S(1)} %get-tuple-element.55), channel_id=1, source_target_pairs={{2,0},{3,1},{0,2},{1,3},{6,4},{7,5},{4,6},{5,7},{10,8},{11,9},{8,1... | collective-permute-start | bytes 61448 | tf_op jit(solution)/shard_map/ppermute | solution.py:712
  100.6 5.4 %collective-permute-start.8 = (f32[40,128]{1,0:T(8,128)S(1)}, f32[40,128]{1,0:T(8,128)S(1)}, u32[]{:S(2)}, u32[]{:S(2)}) collective-permute-start(f32[40,128]{1,0:T(8,128)S(1)} %get-tuple-element.55), channel_id=1, source_target_pairs={{3,0},{0,1},{1,2},{2,3},{7,4},{4,5},{5,6},{6,7},{11,8},{8,9},{9,10... | collective-permute-start | bytes 61448 | tf_op jit(solution)/shard_map/ppermute | solution.py:712
  102.1 4.0 %collective-permute-start.6 = (f32[40,128]{1,0:T(8,128)S(1)}, f32[40,128]{1,0:T(8,128)S(1)}, u32[]{:S(2)}, u32[]{:S(2)}) collective-permute-start(f32[40,128]{1,0:T(8,128)S(1)} %get-tuple-element.55), channel_id=1, source_target_pairs={{1,0},{2,1},{3,2},{0,3},{5,4},{6,5},{7,6},{4,7},{9,8},{10,9},{11,1... | collective-permute-start | bytes 61448 | tf_op jit(solution)/shard_map/ppermute | solution.py:712
  106.1 10.6 %collective-permute-start.10 = (f32[4,40,128]{2,1,0:T(8,128)S(1)}, f32[4,40,128]{2,1,0:T(8,128)S(1)}, u32[]{:S(2)}, u32[]{:S(2)}) collective-permute-start(f32[4,40,128]{2,1,0:T(8,128)S(1)} %pad_maximum_fusion.s0), channel_id=1, source_target_pairs={{8,0},{9,1},{10,2},{11,3},{12,4},{13,5},{14,6},{15,7},{0,8},{1,9},... | collective-permute-start | bytes 245768 | tf_op jit(solution)/shard_map/ppermute | solution.py:712
  109.3 7.5 %collective-permute-start.11 = (f32[4,40,128]{2,1,0:T(8,128)S(1)}, f32[4,40,128]{2,1,0:T(8,128)S(1)}, u32[]{:S(2)}, u32[]{:S(2)}) collective-permute-start(f32[4,40,128]{2,1,0:T(8,128)S(1)} %pad_maximum_fusion.s0), channel_id=1, source_target_pairs={{12,0},{13,1},{14,2},{15,3},{0,4},{1,5},{2,6},{3,7},{4,8},{5,9},{6... | collective-permute-start | bytes 245768 | tf_op jit(solution)/shard_map/ppermute | solution.py:712
  111.1 5.7 %collective-permute-start.9 = (f32[4,40,128]{2,1,0:T(8,128)S(1)}, f32[4,40,128]{2,1,0:T(8,128)S(1)}, u32[]{:S(2)}, u32[]{:S(2)}) collective-permute-start(f32[4,40,128]{2,1,0:T(8,128)S(1)} %pad_maximum_fusion.s0), channel_id=1, source_target_pairs={{4,0},{5,1},{6,2},{7,3},{8,4},{9,5},{10,6},{11,7},{12,8},{13,9},{1... | collective-permute-start | bytes 245768 | tf_op jit(solution)/shard_map/ppermute | solution.py:712
  112.5 1.9 %copy-start.1 = (f32[6400,128]{1,0:T(8,128)S(1)}, f32[6400,128]{1,0:T(8,128)}, u32[]{:S(2)}) copy-start(f32[6400,128]{1,0:T(8,128)} %all-gather.7.cloned.1.call-done) | copy-start | bytes 9830404
  114.4 2.3 %copy-start.20 = (f32[50,8,128]{2,1,0:T(8,128)S(1)}, f32[50,8,128]{2,1,0:T(8,128)}, u32[]{:S(2)}) copy-start(f32[50,8,128]{2,1,0:T(8,128)} %copy-done.19) | copy-start | bytes 614404
Sparse Core Ops, SparseCore 0:
  30.4 26.8 all-gather.4
  59.5 49.2 all-gather.6

commit v3 on v1

--- a/solution.py
+++ b/solution.py
@@ -10,6 +10,7 @@
 F32 = jnp.float32
 N = 128
 HALF = 64
+ENTRIES = 112
 KEPT = HALF // 2
 CHUNK = 8
 STEPS = KEPT // CHUNK
@@ -42,26 +43,43 @@
     return result
 
 
-def solve(matrix, columns):
+def reciprocal(value):
+    guess = pl.reciprocal(value, approx=True)
+    return guess * (2.0 - value * guess)
+
+
+def factor(matrix):
     m = [list(row) for row in matrix]
-    cols = [list(column) for column in columns]
     inverse = []
     for p in range(5):
-        inv = 1.0 / m[p][p]
+        inv = reciprocal(m[p][p])
         inverse.append(inv)
         for i in range(p + 1, 5):
-            weight = m[i][p] * inv
+            m[i][p] = m[i][p] * inv
             for j in range(p + 1, 5):
-                m[i][j] = m[i][j] - weight * m[p][j]
-            for column in cols:
-                column[i] = column[i] - weight * column[p]
-    for column in cols:
-        for i in range(4, -1, -1):
-            total = column[i]
-            for j in range(i + 1, 5):
-                total = total - m[i][j] * column[j]
-            column[i] = total * inverse[i]
-    return cols
+                m[i][j] = m[i][j] - m[i][p] * m[p][j]
+    for i in range(5):
+        for j in range(i + 1, 5):
+            m[i][j] = m[i][j] * inverse[i]
+    return m, inverse
+
+
+def triangular(factored, column):
+    m, inverse = factored
+    x = list(column)
+    for i in range(1, 5):
+        for p in range(i):
+            x[i] = x[i] - m[i][p] * x[p]
+    x = [x[i] * inverse[i] for i in range(5)]
+    for i in range(3, -1, -1):
+        for j in range(i + 1, 5):
+            x[i] = x[i] - m[i][j] * x[j]
+    return x
+
+
+def solve(matrix, columns):
+    factored = factor(matrix)
+    return [triangular(factored, column) for column in columns]
 
 
 def columns_of(matrix):
@@ -134,7 +152,7 @@
     table = tab[here, :]
     e0, d0 = eps[here, :], dlt[here, :]
     em, dm = eps[back, :], dlt[back, :]
-    cm = 1.0 / (2.0 + dm)
+    cm = reciprocal(2.0 + dm)
     a = table_mat(table, 0)
     a1, a2 = cm * e0, cm * em
     a3 = a1 * em
@@ -151,7 +169,7 @@
     else:
         ahead = cell_rows(k + 1)
         ep, dp = eps[ahead, :], dlt[ahead, :]
-        cp = 1.0 / (2.0 + dp)
+        cp = reciprocal(2.0 + dp)
         b1, b2 = cp * e0, cp * ep
         b3 = b1 * ep
         ap, aap = table_mat(tab[ahead, :], 0), table_mat(table, 60)
@@ -185,10 +203,6 @@
 
 
 def sweep_step(m, state, fac_ref, slot, raw, keep, tables):
-    @pl.when(m == 1)
-    def _():
-        init_first_edge(state)
-
     r = load_mat(state, R_AT)
     x = load_mat(state, X_AT)
     w = load_vec(state, W_AT)
@@ -201,7 +215,13 @@
     r_new = rows_of(solved[:5])
     x_new = rows_of(solved[5:10])
     w_new = [-value for value in solved[10]]
-    accumulate(state, r, x, w)
+    live = jnp.where(m == 0, 0.0, 1.0)
+    accumulate(
+        state,
+        [[live * e for e in row] for row in r],
+        [[live * e for e in row] for row in x],
+        [live * e for e in w],
+    )
     store_mat(state, R_AT, r_new)
     store_mat(state, X_AT, x_new)
     store_vec(state, W_AT, w_new)
@@ -218,7 +238,7 @@
     return lax.broadcasted_iota(jnp.int32, (8, 128), 0) % 2 == 0
 
 
-def finish_sweep(first, state, port, port_ref, mid_ref, raw, keep, tables):
+def finish_sweep(at, inner, state, port, port_refs, mid_ref, raw, keep, tables):
     tab, eps, dlt = tables
     r = load_mat(state, R_AT)
     x = load_mat(state, X_AT)
@@ -226,7 +246,7 @@
     q, xq, y = accumulate(state, r, x, w)
     rows = cell_rows(0)
     e0, d0 = eps[rows, :], dlt[rows, :]
-    c0 = 1.0 / (2.0 + d0)
+    c0 = reciprocal(2.0 + d0)
     start_speed = [[e0 * value for value in row] for row in table_mat(tab[rows, :], 0)]
     cols = mat_cols(start_speed, columns_of(q) + columns_of(xq) + [y])
     q = [[c0 * (q[i][j] - cols[j][i]) for j in range(5)] for i in range(5)]
@@ -258,7 +278,6 @@
             mid_ref[25 + 5 * i + j] = mx[i][j]
         mid_ref[50 + i] = m0[i]
     left = mat_cols(q, solved)
-    start = jnp.broadcast_to(first, (8, 128)) > 0
     s1 = [[from_second(e) for e in row] for row in s]
     xn1 = [[from_second(e) for e in row] for row in xn]
     g1 = [from_second(e) for e in g]
@@ -266,18 +285,21 @@
     cols = mat_cols(n1, solved)
     for i in range(5):
         for j in range(5):
-            at = 5 * i + j
-            unit = 1.0 if i == j else 0.0
-            port[pl.ds(8 * at, 8), :] = s1[i][j] + cols[j][i]
-            port[pl.ds(8 * (25 + at), 8), :] = xn1[i][j] + cols[5 + j][i]
-            port[pl.ds(8 * (55 + at), 8), :] = jnp.where(start, unit, left[j][i])
-            port[pl.ds(8 * (80 + at), 8), :] = jnp.where(start, 0.0, xq[i][j] + left[5 + j][i])
+            entry = 5 * i + j
+            port[pl.ds(8 * entry, 8), :] = s1[i][j] + cols[j][i]
+            port[pl.ds(8 * (25 + entry), 8), :] = xn1[i][j] + cols[5 + j][i]
+            port[pl.ds(8 * (55 + entry), 8), :] = left[j][i]
+            port[pl.ds(8 * (80 + entry), 8), :] = xq[i][j] + left[5 + j][i]
         port[pl.ds(8 * (50 + i), 8), :] = g1[i] - cols[10][i]
-        port[pl.ds(8 * (105 + i), 8), :] = jnp.where(start, 0.0, y[i] + left[10][i])
-    for e in range(110, 128):
+        port[pl.ds(8 * (105 + i), 8), :] = y[i] + left[10][i]
+    for e in range(110, ENTRIES):
         port[pl.ds(8 * e, 8), :] = zeros()
-    for z in range(4):
-        port_ref[pl.ds(128 * z, 128), :] = port[pl.ds(2 * z, 128, stride=8), :].T
+    planes = 4 // inner
+    for offset, port_ref in enumerate(port_refs):
+        target = lax.rem(at + offset, inner) * planes
+        for z in range(planes):
+            block = port[pl.ds(2 * (target + z), ENTRIES, stride=8), :]
+            port_ref[pl.ds(z, ENTRIES, stride=planes), :] = block
 
 
 def cell_rows(k):
@@ -315,13 +337,21 @@
         sweep_step(step * CHUNK + slot, state, fac_ref, slot, raw, keep, tables)
         return carry
 
-    lax.fori_loop(0, count, one, 0)
+    def two(pair, carry):
+        one(2 * pair, carry)
+        return one(2 * pair + 1, carry)
+
+    lax.fori_loop(0, count // 2, two, 0)
+
+    @pl.when(count % 2 == 1)
+    def _():
+        one(count - 1, 0)
 
 
 def forward_x_kernel(
-    first_ref, last_ref, q_ref, visc_ref, mx_ref, my_ref, jacx_ref, jacy_ref,
+    spots_ref, first_ref, last_ref, q_ref, visc_ref, mx_ref, my_ref, jacx_ref, jacy_ref,
     south_ref, north_ref,
-    fac_ref, port_ref, mid_ref, tab, eps, dlt,
+    fac_ref, mid_ref, tab, eps, dlt, port0, port1,
     state, keep, g1, g2, tin, turned, port,
 ):
     step = pl.program_id(0)
@@ -373,12 +403,13 @@
 
     @pl.when(step == STEPS - 1)
     def _():
-        finish_sweep(first_ref[0], state, port, port_ref, mid_ref, raw, keep, tables)
+        ports = (port0, port1)
+        finish_sweep(spots_ref[1], 2, state, port, ports, mid_ref, raw, keep, tables)
 
 
 def forward_y_kernel(
-    first_ref, p_ref, visc_ref, my_ref, jacy_ref,
-    fac_ref, port_ref, mid_ref, tab, eps, dlt,
+    spots_ref, p_ref, visc_ref, my_ref, jacy_ref,
+    fac_ref, mid_ref, tab, eps, dlt, port0, port1, port2, port3,
     state, keep, field, tin, turned, port,
 ):
     step = pl.program_id(0)
@@ -409,87 +440,135 @@
 
     @pl.when(step == STEPS - 1)
     def _():
-        finish_sweep(first_ref[1], state, port, port_ref, mid_ref, raw, keep, tables)
-
-
-def reduced_kernel(count, lines, in_ref, out_ref, ports, gains):
-    per = 128 // lines
-    for group in range(count // per):
-        turned = in_ref[pl.ds(128 * group, 128), :].T
-        for q in range(per):
-            ports[group * per + q] = turned if q == 0 else pltpu.roll(turned, 128 - lines * q, 1)
-
-    def entry(piece, index):
-        return ports[piece, pl.ds(index, 1), :]
-
-    def matrix(piece, base):
-        return [[entry(piece, base + 5 * i + j) for j in range(5)] for i in range(5)]
-
-    def vector(piece, base):
-        return [entry(piece, base + i) for i in range(5)]
-
-    def eliminate(piece, following, s, g):
-        qq, xx, yy = matrix(following, 55), matrix(following, 80), vector(following, 105)
-        reduced = [[s[i][j] - xx[i][j] for j in range(5)] for i in range(5)]
-        t = [[reduced[i][j] + qq[i][j] for j in range(5)] for i in range(5)]
-        rhs = [yy[i] + g[i] for i in range(5)]
-        solved = solve(t, columns_of(reduced) + [rhs])
-        h, v = rows_of(solved[:5]), solved[5]
-        for i in range(5):
-            for j in range(5):
-                gains[piece, pl.ds(5 * i + j, 1), :] = h[i][j]
-            gains[piece, pl.ds(25 + i, 1), :] = v[i]
-
-    eliminate(0, 1, matrix(0, 0), vector(0, 50))
-
-    def forward(piece, carry):
-        h = [[gains[piece - 1, pl.ds(5 * i + j, 1), :] for j in range(5)] for i in range(5)]
-        v = [gains[piece - 1, pl.ds(25 + i, 1), :] for i in range(5)]
-        s, xn, g = matrix(piece, 0), matrix(piece, 25), vector(piece, 50)
-        gain = [[(1.0 if i == j else 0.0) - h[i][j] for j in range(5)] for i in range(5)]
-        part = mat_cols(s, columns_of(h))
-        rest = mat_cols(xn, columns_of(gain))
-        s_all = [[part[j][i] + rest[j][i] for j in range(5)] for i in range(5)]
-        difference = [[s[i][j] - xn[i][j] for j in range(5)] for i in range(5)]
-        moved = mat_cols(difference, [v])[0]
-        g_all = [g[i] + moved[i] for i in range(5)]
-        eliminate(piece, lax.rem(piece + 1, count), s_all, g_all)
-        return carry
-
-    lax.fori_loop(1, count, forward, 0)
-    out_ref[...] = jnp.zeros((count, 16, 128), F32)
-
-    def backward(at, following):
-        piece = count - 1 - at
-        h = [[gains[piece, pl.ds(5 * i + j, 1), :] for j in range(5)] for i in range(5)]
-        v = [gains[piece, pl.ds(25 + i, 1), :] for i in range(5)]
-        moved = mat_cols(h, [list(following)])[0]
-        here = tuple((following[i] - moved[i]) + v[i] for i in range(5))
-        for i in range(5):
-            out_ref[piece, pl.ds(5 + i, 1), :] = here[i]
-
-        @pl.when(piece + 1 < count)
-        def _():
-            for i in range(5):
-                out_ref[piece + 1, pl.ds(i, 1), :] = here[i]
-
-        return here
-
-    start = tuple(jnp.zeros((1, 128), F32) for _ in range(5))
-    lax.fori_loop(0, count, backward, start)
-
-
-def begin_backward(count, lines, ends_ref, mid_ref, edge, ends8):
-    per = 128 // lines
-    lanes = lax.broadcasted_iota(jnp.int32, (16, 128), 1)
-    for z in range(4):
-        block = ends_ref[per * z]
-        for q in range(1, per):
-            moved = pltpu.roll(ends_ref[per * z + q], lines * q, 1)
-            block = jnp.where(lanes >= lines * q, moved, block)
+        ports = (port0, port1, port2, port3)
+        finish_sweep(spots_ref[3], 4, state, port, ports, mid_ref, raw, keep, tables)
+
+
+S_IN, XN_IN, G_IN, QQ_IN, XX_IN, YY_IN = 0, 25, 50, 55, 80, 105
+
+
+def get_vec(ref, rows, base, *at):
+    return [ref[(*at, pl.ds(rows * (base + i), rows), slice(None))] for i in range(5)]
+
+
+def get_mat(ref, rows, base, *at):
+    return [get_vec(ref, rows, base + 5 * i, *at) for i in range(5)]
+
+
+def put_vec(ref, rows, base, vector, *at):
+    for i in range(5):
+        ref[(*at, pl.ds(rows * (base + i), rows), slice(None))] = vector[i]
+
+
+def put_mat(ref, rows, base, matrix, *at):
+    for i in range(5):
+        put_vec(ref, rows, base + 5 * i, matrix[i], *at)
+
+
+def combine(left, right, sign):
+    return [[a + sign * b for a, b in zip(p, q)] for p, q in zip(left, right)]
+
+
+def get_port(ref, rows, *at):
+    return (
+        get_mat(ref, rows, S_IN, *at),
+        get_mat(ref, rows, XN_IN, *at),
+        get_vec(ref, rows, G_IN, *at),
+        get_mat(ref, rows, QQ_IN, *at),
+        get_mat(ref, rows, XX_IN, *at),
+        get_vec(ref, rows, YY_IN, *at),
+    )
+
+
+def join_kernel(inner, *refs):
+    spots_ref, blocks = refs[0], refs[1 : 1 + inner]
+    port_ref, mid_ref, pieces = refs[1 + inner :]
+    rows = 4 // inner
+    at = spots_ref[1] if inner == 2 else spots_ref[3]
+    for offset, block in enumerate(blocks):
+        pieces[lax.rem(at + offset, inner)] = block[...]
+    whole_port = get_port(pieces, rows, 0)
+    for piece in range(1, inner):
+        s, xn, g, qq, xx, yy = whole_port
+        s1, xn1, g1, q1, x1, y1 = get_port(pieces, rows, piece)
+        t = combine(s, combine(q1, x1, -1.0), 1.0)
+        rhs = [y1[i] + g[i] for i in range(5)]
+        solved = solve(t, columns_of(q1) + columns_of(combine(x1, xn, -1.0)) + [rhs])
+        put_mat(mid_ref, rows, 0, rows_of(solved[:5]), piece - 1)
+        put_mat(mid_ref, rows, 25, rows_of(solved[5:10]), piece - 1)
+        put_vec(mid_ref, rows, 50, solved[10], piece - 1)
+        left = mat_cols(qq, solved)
+        right = mat_cols(combine(xn1, s1, -1.0), solved)
+        whole_port = (
+            combine(s1, rows_of(right[:5]), 1.0),
+            combine(xn1, rows_of(right[5:10]), 1.0),
+            [g1[i] - right[10][i] for i in range(5)],
+            rows_of(left[:5]),
+            combine(xx, rows_of(left[5:10]), 1.0),
+            [yy[i] + left[10][i] for i in range(5)],
+        )
+    for base, part in zip((S_IN, XN_IN, G_IN, QQ_IN, XX_IN, YY_IN), whole_port):
+        (put_vec if base in (G_IN, YY_IN) else put_mat)(port_ref, rows, base, part)
+    port_ref[pl.ds(110 * rows, 2 * rows), :] = jnp.zeros((2 * rows, 128), F32)
+
+
+def solve_kernel(inner, spots_ref, b0, b1, b2, b3, mid_ref, out_ref, ports, values):
+    rows = 4 // inner
+    group = spots_ref[0] if inner == 2 else spots_ref[2]
+    for far, block in enumerate((b0, b1, b2, b3)):
+        ports[lax.rem(group + far, 4)] = block[...]
+    gains = []
+    for piece in range(4):
+        s, xn = get_mat(ports, rows, S_IN, piece), get_mat(ports, rows, XN_IN, piece)
+        g = get_vec(ports, rows, G_IN, piece)
+        if piece:
+            h, v = gains[-1]
+            gain = [[(1.0 if i == j else 0.0) - h[i][j] for j in range(5)] for i in range(5)]
+            part = combine(
+                rows_of(mat_cols(s, columns_of(h))), rows_of(mat_cols(xn, columns_of(gain))), 1.0
+            )
+            moved = mat_cols(combine(s, xn, -1.0), [v])[0]
+            g = [g[i] + moved[i] for i in range(5)]
+            s = part
+        if piece < 3:
+            yy = get_vec(ports, rows, YY_IN, piece + 1)
+            reduced = combine(s, get_mat(ports, rows, XX_IN, piece + 1), -1.0)
+            t = combine(reduced, get_mat(ports, rows, QQ_IN, piece + 1), 1.0)
+            solved = solve(t, columns_of(reduced) + [[yy[i] + g[i] for i in range(5)]])
+            gains.append((rows_of(solved[:5]), solved[5]))
+        else:
+            t = [[s[i][j] + (1.0 if i == j else 0.0) for j in range(5)] for i in range(5)]
+            p = solve(t, [g])[0]
+            put_vec(values, rows, 0, p, 4)
+    for piece in range(2, -1, -1):
+        h, v = gains[piece]
+        moved = mat_cols(h, [p])[0]
+        p = [(p[i] - moved[i]) + v[i] for i in range(5)]
+        put_vec(values, rows, 0, p, piece + 1)
+    put_vec(values, rows, 0, [jnp.zeros((rows, 128), F32)] * 5, 0)
+    a = get_vec(values, rows, 0, group)
+    c = get_vec(values, rows, 0, group + 1)
+    out_ref[...] = jnp.zeros(out_ref.shape, F32)
+    put_vec(out_ref, rows, 0, a)
+    put_vec(out_ref, rows, 5 * inner, c)
+    for piece in range(inner - 1, 0, -1):
+        part = mat_cols(get_mat(mid_ref, rows, 0, piece - 1), [[c[i] - a[i] for i in range(5)]])[0]
+        rest = mat_cols(get_mat(mid_ref, rows, 25, piece - 1), [a])[0]
+        m0 = get_vec(mid_ref, rows, 50, piece - 1)
+        c = [a[i] + ((part[i] + rest[i]) + m0[i]) for i in range(5)]
+        put_vec(out_ref, rows, 5 * piece, c)
+
+
+def begin_backward(inner, spots_ref, ends_refs, mid_ref, edge, ends8):
+    rows = 4 // inner
+    at = spots_ref[1] if inner == 2 else spots_ref[3]
+    for offset, ends_ref in enumerate(ends_refs):
+        plane = lax.rem(at + offset, inner) * rows
         for e in range(10):
-            ends8[e, pl.ds(2 * z, 1), :] = block[e : e + 1]
-            ends8[e, pl.ds(2 * z + 1, 1), :] = block[e : e + 1]
+            for z in range(rows):
+                row = ends_ref[pl.ds(rows * (5 * at + e) + z, 1), :]
+                ends8[e, pl.ds(2 * (plane + z), 1), :] = row
+                ends8[e, pl.ds(2 * (plane + z) + 1, 1), :] = row
     a = [ends8[i] for i in range(5)]
     c = [ends8[5 + i] for i in range(5)]
     gap = [c[i] - a[i] for i in range(5)]
@@ -506,7 +585,7 @@
     tab, eps, dlt = tables
     rows = cell_rows(k)
     e, d = eps[rows, :], dlt[rows, :]
-    c = 1.0 / (2.0 + d)
+    c = reciprocal(2.0 + d)
     gap = [right[i] - left[i] for i in range(5)]
     moved = mat_cols(table_mat(tab[rows, :], 0), [[e * value for value in gap]])[0]
     return [
@@ -535,7 +614,16 @@
         write(2 * m + 1, here)
         return here
 
-    final = lax.fori_loop(begin, CHUNK, one, tuple(edge[5 + i] for i in range(5)))
+    @pl.when(step == 0)
+    def _():
+        here = one(1, tuple(edge[5 + i] for i in range(5)))
+        for i in range(5):
+            edge[5 + i] = here[i]
+
+    def two(pair, following):
+        return one(2 * pair + 1, one(2 * pair, following))
+
+    final = lax.fori_loop(begin, CHUNK // 2, two, tuple(edge[5 + i] for i in range(5)))
     for i in range(5):
         edge[5 + i] = final[i]
 
@@ -545,7 +633,7 @@
 
 
 def backward_x_kernel(
-    count, lines, fac_ref, mid_ref, ends_ref, tab, eps, dlt, q_ref, out_ref, edge, ends8
+    spots_ref, fac_ref, mid_ref, e0, e1, tab, eps, dlt, q_ref, out_ref, edge, ends8
 ):
     def write(k, value):
         rows = cell_rows(k)
@@ -554,14 +642,14 @@
 
     @pl.when(pl.program_id(0) == 0)
     def _():
-        begin_backward(count, lines, ends_ref, mid_ref, edge, ends8)
+        begin_backward(2, spots_ref, (e0, e1), mid_ref, edge, ends8)
         write(HALF - 1, [edge[5 + i] for i in range(5)])
 
     backward_chunk(fac_ref, mid_ref, edge, write, (tab, eps, dlt))
 
 
 def backward_y_kernel(
-    count, lines, fac_ref, mid_ref, ends_ref, tab, eps, dlt, out_ref, edge, ends8, field
+    spots_ref, fac_ref, mid_ref, e0, e1, e2, e3, tab, eps, dlt, out_ref, edge, ends8, field
 ):
     def write(k, value):
         for i in range(5):
@@ -569,7 +657,7 @@
 
     @pl.when(pl.program_id(0) == 0)
     def _():
-        begin_backward(count, lines, ends_ref, mid_ref, edge, ends8)
+        begin_backward(4, spots_ref, (e0, e1, e2, e3), mid_ref, edge, ends8)
         write(HALF - 1, [edge[5 + i] for i in range(5)])
 
     backward_chunk(fac_ref, mid_ref, edge, write, (tab, eps, dlt))
@@ -597,15 +685,17 @@
 
 
 PLANE = (512, 128)
-FORWARD_OUT = tuple(
-    jax.ShapeDtypeStruct(shape, F32)
-    for shape in ((KEPT, FACTORS, 8, 128), PLANE, (60, 8, 128), PLANE, PLANE, PLANE)
-)
-
-
-def forward_specs():
+
+
+def forward_out(inner):
+    ports = [(ENTRIES * 4 // inner, 128)] * inner
+    shapes = [(KEPT, FACTORS, 8, 128), (60, 8, 128), PLANE, PLANE, PLANE] + ports
+    return tuple(jax.ShapeDtypeStruct(shape, F32) for shape in shapes)
+
+
+def forward_specs(inner):
     block = pl.BlockSpec((CHUNK, FACTORS, 8, 128), lambda i: (i, 0, 0, 0))
-    return (block,) + tuple(whole(value.shape) for value in FORWARD_OUT[1:])
+    return (block,) + tuple(whole(value.shape) for value in forward_out(inner)[1:])
 
 
 def forward_scratch(fields):
@@ -620,53 +710,82 @@
     )
 
 
-def forward(kernel, name, flags, operands, fields):
+def forward(kernel, name, inner, flags, operands, fields):
     return pl.pallas_call(
         kernel,
         grid=(STEPS,),
         in_specs=[scalars() for _ in flags] + [whole(value.shape) for value in operands],
-        out_specs=forward_specs(),
-        out_shape=FORWARD_OUT,
+        out_specs=forward_specs(inner),
+        out_shape=forward_out(inner),
         scratch_shapes=forward_scratch(fields),
         compiler_params=params(),
         name=name,
     )(*flags, *operands)
 
 
-def reduced(port, axis):
+def small(kernel, name, flags, operands, outputs, scratch):
+    vmem = pl.BlockSpec(memory_space=pltpu.VMEM)
+    return pl.pallas_call(
+        kernel,
+        out_shape=tuple(jax.ShapeDtypeStruct(shape, F32) for shape in outputs),
+        in_specs=[scalars() for _ in flags] + [vmem for _ in operands],
+        out_specs=tuple(vmem for _ in outputs),
+        scratch_shapes=[pltpu.VMEM(shape, F32) for shape in scratch],
+        compiler_params=pltpu.CompilerParams(vmem_limit_bytes=VMEM_LIMIT),
+        name=name,
+    )(*flags, *operands)
+
+
+FARTHEST_FIRST = {2: (1,), 4: (2, 1, 3)}
+
+
+def exchange(values, axis, inner):
     count = lax.axis_size(axis)
-    lines = 512 // count
-    received = lax.all_to_all(
-        port.reshape(count, lines, 128), axis, split_axis=0, concat_axis=0, tiled=True
-    )
-    ends = pl.pallas_call(
-        functools.partial(reduced_kernel, count, lines),
-        out_shape=jax.ShapeDtypeStruct((count, 16, 128), F32),
-        in_specs=[pl.BlockSpec(memory_space=pltpu.VMEM)],
-        out_specs=pl.BlockSpec(memory_space=pltpu.VMEM),
-        scratch_shapes=[
-            pltpu.VMEM((count, 128, 128), F32),
-            pltpu.VMEM((count, 32, 128), F32),
-        ],
-        compiler_params=pltpu.CompilerParams(vmem_limit_bytes=VMEM_LIMIT),
-        name="reduced_" + axis,
-    )(received.reshape(512, 128))
-    return lax.all_to_all(ends, axis, split_axis=0, concat_axis=0, tiled=True)
-
-
-def backward(kernel, name, operands, extra):
-    count = operands[2].shape[0]
+    received = {0: values[0]}
+    for offset in FARTHEST_FIRST[inner]:
+        back = inner - offset
+        moves = [(i, (i // inner) * inner + (i + back) % inner) for i in range(count)]
+        received[offset] = lax.ppermute(values[back], axis, moves)
+    return [received[offset] for offset in range(inner)]
+
+
+def line_ends(ports, axis, spots):
+    inner = len(ports)
+    rows = 4 // inner
+    count = lax.axis_size(axis)
+    port_shape = (ENTRIES * rows, 128)
+    mid_shape = (inner - 1, 56 * rows, 128)
+    port, mid = small(
+        functools.partial(join_kernel, inner), "join_" + axis, (spots,),
+        exchange(ports, axis, inner), (port_shape, mid_shape), [(inner, *port_shape)],
+    )
+    blocks = {0: port}
+    for far in FARTHEST_FIRST[4]:
+        moves = [((i + far * inner) % count, i) for i in range(count)]
+        blocks[far] = lax.ppermute(port, axis, moves)
+    blocks = [blocks[far] for far in range(4)]
+    (ends,) = small(
+        functools.partial(solve_kernel, inner), "solve_" + axis, (spots,), (*blocks, mid),
+        ((32, 128),), [(4, *port_shape), (5, 8 * rows, 128)],
+    )
+    return exchange([ends] * inner, axis, inner)
+
+
+def backward(kernel, name, spots, operands, extra):
     return pl.pallas_call(
-        functools.partial(kernel, count, 512 // count),
+        kernel,
         grid=(STEPS,),
-        in_specs=[pl.BlockSpec((CHUNK, FACTORS, 8, 128), lambda i: (STEPS - 1 - i, 0, 0, 0))]
+        in_specs=[
+            scalars(),
+            pl.BlockSpec((CHUNK, FACTORS, 8, 128), lambda i: (STEPS - 1 - i, 0, 0, 0)),
+        ]
         + [whole(value.shape) for value in operands[1:]],
         out_specs=whole((5, 512, 128)),
         out_shape=jax.ShapeDtypeStruct((5, 512, 128), F32),
         scratch_shapes=[pltpu.VMEM((10, 8, 128), F32), pltpu.VMEM((10, 8, 128), F32)] + extra,
         compiler_params=params(),
         name=name,
-    )(*operands)
+    )(spots, *operands)
 
 
 def halos(axis, last, initial):
@@ -677,10 +796,12 @@
 
 
 def body(flow_state, viscosity, metric_x, metric_y, jacobian_x, jacobian_y):
-    spots = [lax.axis_index("row"), lax.axis_index("col")]
-    sizes = [lax.axis_size("row"), lax.axis_size("col")]
-    first = jnp.stack([(spot == 0).astype(jnp.int32) for spot in spots])
-    last = jnp.stack([(spot == n - 1).astype(jnp.int32) for spot, n in zip(spots, sizes)])
+    row, col = lax.axis_index("row"), lax.axis_index("col")
+    spots = jnp.stack([row // 2, row % 2, col // 4, col % 4]).astype(jnp.int32)
+    places = jnp.stack([row, col]).astype(jnp.int32)
+    sizes = jnp.array([lax.axis_size("row"), lax.axis_size("col")], jnp.int32)
+    first = (places == 0).astype(jnp.int32)
+    last = (places == sizes - 1).astype(jnp.int32)
     jacx = jacobian_x.reshape(25, 128)
     jacy = jacobian_y.reshape(25, 128)
 
@@ -693,20 +814,20 @@
     visc = viscosity.reshape(512, 128)
     plane = [pltpu.VMEM(PLANE, F32), pltpu.VMEM(PLANE, F32)]
     field = pltpu.VMEM((5, 512, 128), F32)
-    fac, port, mid, *tables = forward(
-        forward_x_kernel, "forward_x", (first, last),
+    fac, mid, tab, eps, dlt, *ports = forward(
+        forward_x_kernel, "forward_x", 2, (spots, first, last),
         (q, visc, metric_x, metric_y, jacx, jacy, south, north), plane,
     )
-    ends = reduced(port, "row")
+    ends = line_ends(ports, "row", spots)
     partial_value = backward(
-        backward_x_kernel, "backward_x", (fac, mid, ends, *tables, q), []
-    )
-    fac, port, mid, *tables = forward(
-        forward_y_kernel, "forward_y", (first,), (partial_value, visc, metric_y, jacy), [field]
-    )
-    ends = reduced(port, "col")
+        backward_x_kernel, "backward_x", spots, (fac, mid, *ends, tab, eps, dlt, q), []
+    )
+    fac, mid, tab, eps, dlt, *ports = forward(
+        forward_y_kernel, "forward_y", 4, (spots,), (partial_value, visc, metric_y, jacy), [field]
+    )
+    ends = line_ends(ports, "col", spots)
     result = backward(
-        backward_y_kernel, "backward_y", (fac, mid, ends, *tables), [field]
+        backward_y_kernel, "backward_y", spots, (fac, mid, *ends, tab, eps, dlt), [field]
     )
     return result.reshape(5, 4, 128, 128)
 

time: 112 us -> 99 us (0.88)
  blocking collectives: 46 us -> 0 us
  starting transfers between devices: 6.74 us -> 25.3 us
  waiting for transfers between devices: 1.48 us -> 19.3 us
  Pallas kernels: 54.7 us -> 51 us
    all_to_all x4 -> x0, blocking collectives: 46 us -> none  [the longest x2 26.7 us: reduced(): lax.all_to_all(port.reshape(count, lines, 128), axis, split_axis=0, conca...]
    ppermute x0 -> x14, starting transfers between devices: none -> 18.6 us  [the longest x6 11.5 us: line_ends(): blocks[far] = lax.ppermute(port, axis, moves)]
    ppermute x0 -> x14, waiting for transfers between devices: none -> 17.9 us  [the longest x8 9.64 us: exchange(): received[offset] = lax.ppermute(values[back], axis, moves)]
    pallas_call x2, Pallas kernels: 35.4 us -> 33.2 us  [forward(): pl.pallas_call(kernel, grid=(STEPS,), in_specs=[scalars() for _ in flags]...]
    pallas_call x4 -> x6, Pallas kernels: 19.3 us -> 17.8 us  [the longest x2 13.2 us: backward(): pl.pallas_call(kernel, grid=(STEPS,), in_specs=[scalars(), pl.BlockSpec((...]
  transfers between devices with their start and end apart: 2 -> 16, of which waited for: 1 -> 14; matrix products, arithmetic and copies ran while one was open for 0% -> 0% of each run, Pallas kernels for 0% -> 0%
where the time goes in v3:
time: 99 us; the launch traced here: 98.9 us
  Pallas kernels  51 us (52%)
  starting transfers between devices  25.3 us (26%)
  waiting for transfers between devices  19.3 us (19%)
  local copies, waits for them, and re-layouts  3 us (3%)
    pallas_call x2, Pallas kernels, forward(): pl.pallas_call(kernel, grid=(STEPS,), in_specs=[scalars() for _ in flags]...  33.2 us
    pallas_call x2, Pallas kernels, backward(): pl.pallas_call(kernel, grid=(STEPS,), in_specs=[scalars(), pl.BlockSpec((...  13.2 us
    ppermute x6, starting transfers between devices, line_ends(): blocks[far] = lax.ppermute(port, axis, moves)  11.5 us
    ppermute x8, waiting for transfers between devices, exchange(): received[offset] = lax.ppermute(values[back], axis, moves)  9.64 us
    ppermute x6, waiting for transfers between devices, line_ends(): blocks[far] = lax.ppermute(port, axis, moves)  8.24 us
    ppermute x8, starting transfers between devices, exchange(): received[offset] = lax.ppermute(values[back], axis, moves)  7.09 us
    ppermute x2, starting transfers between devices, halos(): return (lax.ppermute(last, axis, up), lax.ppermute(initial, axis, down))  6.74 us
    pallas_call x4, Pallas kernels, small(): pl.pallas_call(kernel, out_shape=tuple((jax.ShapeDtypeStruct(shape, F32)...  4.59 us
  transfers between devices with their start and end apart: 16, of which 14 were waited for; matrix products, arithmetic and copies ran while one was open for 0% of the time, Pallas kernels for 0%

profile of v3, /device:TPU:0, one launch (start us, length us, event | category | flops | bytes accessed | tf_op | source)
XLA Modules:
  0.0 98.9 jit_solution(11715073007764435179)
XLA Ops:
  0.0 0.0 copy-start.3
  0.0 0.0 copy-start.1
  0.0 2.9 %slice_reduce_fusion = (f32[5,4,128]{2,1,0:T(4,128)S(1)}, f32[5,4,128]{2,1,0:T(4,128)S(1)}) fusion(f32[5,4,128,128]{3,2,1,0:T(8,128)} %param.7), kind=kLoop, calls=%fused_computation | loop fusion | bytes 40960 | tf_op jit(solution)/shard_map/slice | solution.py:811
  3.0 2.1 %collective-permute-start = (f32[20,128]{1,0:T(8,128)S(1)}, f32[20,128]{1,0:T(8,128)S(1)}, u32[]{:S(2)}, u32[]{:S(2)}) collective-permute-start(f32[20,128]{1,0:T(8,128)S(1)} %reshape_squeeze.6), channel_id=1, source_target_pairs={{0,1},{1,2},{2,3},{3,4},{4,5},{5,6},{6,7},{7,8},{8,9},{9,10},{10,1... | collective-permute-start | bytes 30728 | tf_op jit(solution)/shard_map/ppermute | solution.py:795
  5.1 4.7 %collective-permute-start.1 = (f32[20,128]{1,0:T(8,128)S(1)}, f32[20,128]{1,0:T(8,128)S(1)}, u32[]{:S(2)}, u32[]{:S(2)}) collective-permute-start(f32[20,128]{1,0:T(8,128)S(1)} %reshape_squeeze.7), channel_id=1, source_target_pairs={{1,0},{2,1},{3,2},{4,3},{5,4},{6,5},{7,6},{8,7},{9,8},{10,9},{11,1... | collective-permute-start | bytes 30728 | tf_op jit(solution)/shard_map/ppermute | solution.py:795
  9.7 0.0 copy-done.6
  9.7 0.1 compare_convert_fusion
  9.8 0.1 pad_add_fusion.spots_ref.refs_0_
  9.9 0.0 copy-done.4
  9.9 0.0 copy-done.5
  9.9 1.4 %collective-permute-done.south_ref = f32[20,128]{1,0:T(8,128)S(1)} collective-permute-done((f32[20,128]{1,0:T(8,128)S(1)}, f32[20,128]{1,0:T(8,128)S(1)}, u32[]{:S(2)}, u32[]{:S(2)}) %collective-permute-start) | collective-permute-done | bytes 10272 | tf_op jit(solution)/shard_map/ppermute | solution.py:795
  11.3 0.0 collective-permute-done.1.north_ref
  11.4 17.3 %forward_x.1 = (f32[32,60,8,128]{3,2,1,0:T(8,128)}, f32[60,8,128]{2,1,0:T(8,128)S(1)}, f32[512,128]{1,0:T(8,128)S(1)}, f32[512,128]{1,0:T(8,128)S(1)}, f32[512,1...) custom-call(s32[4]{0:T(128)S(1)} %pad_add_fusion.spots_ref.refs_0_, ...), custom_call_target="tpu_custom_call" | custom-call | tf_op jit(solution)/shard_map/forward_x/pallas_call | solution.py:714
  28.6 0.0 collective-permute-start.2
  28.6 1.3 %collective-permute-done.2.refs_2_ = f32[224,128]{1,0:T(8,128)S(1)} collective-permute-done((f32[224,128]{1,0:T(8,128)S(1)}, f32[224,128]{1,0:T(8,128)S(1)}, u32[]{:S(2)}, u32[]{:S(2)}) %collective-permute-start.2) | collective-permute-done | bytes 114720 | tf_op jit(solution)/shard_map/ppermute | solution.py:748
  29.9 0.9 join_row.1
  30.8 1.6 %collective-permute-start.5 = (f32[224,128]{1,0:T(8,128)S(1)}, f32[224,128]{1,0:T(8,128)S(1)}, u32[]{:S(2)}, u32[]{:S(2)}) collective-permute-start(f32[224,128]{1,0:T(8,128)S(1)} %get-tuple-element.29.b0), channel_id=1, source_target_pairs={{96,0},{112,16},{0,32},{16,48},{32,64},{48,80},{64,96},{80,112},{9... | collective-permute-start | bytes 344072 | tf_op jit(solution)/shard_map/ppermute | solution.py:765
  32.4 2.7 %collective-permute-start.4 = (f32[224,128]{1,0:T(8,128)S(1)}, f32[224,128]{1,0:T(8,128)S(1)}, u32[]{:S(2)}, u32[]{:S(2)}) collective-permute-start(f32[224,128]{1,0:T(8,128)S(1)} %get-tuple-element.29.b0), channel_id=1, source_target_pairs={{64,0},{80,16},{96,32},{112,48},{0,64},{16,80},{32,96},{48,112},{6... | collective-permute-start | bytes 344072 | tf_op jit(solution)/shard_map/ppermute | solution.py:765
  35.1 1.4 %collective-permute-start.3 = (f32[224,128]{1,0:T(8,128)S(1)}, f32[224,128]{1,0:T(8,128)S(1)}, u32[]{:S(2)}, u32[]{:S(2)}) collective-permute-start(f32[224,128]{1,0:T(8,128)S(1)} %get-tuple-element.29.b0), channel_id=1, source_target_pairs={{32,0},{48,16},{64,32},{80,48},{96,64},{112,80},{0,96},{16,112},{3... | collective-permute-start | bytes 344072 | tf_op jit(solution)/shard_map/ppermute | solution.py:765
  36.5 0.8 collective-permute-done.5.b3
  37.3 3.4 %collective-permute-done.4.b2 = f32[224,128]{1,0:T(8,128)S(1)} collective-permute-done((f32[224,128]{1,0:T(8,128)S(1)}, f32[224,128]{1,0:T(8,128)S(1)}, u32[]{:S(2)}, u32[]{:S(2)}) %collective-permute-start.4) | collective-permute-done | bytes 114720 | tf_op jit(solution)/shard_map/ppermute | solution.py:765
  40.7 0.0 collective-permute-done.3.b1
  40.7 1.2 %solve_row.1.e0 = f32[32,128]{1,0:T(8,128)S(1)} custom-call(s32[4]{0:T(128)S(1)} %pad_add_fusion.spots_ref.refs_0_, f32[224,128]{1,0:T(8,128)S(1)} %get-tuple-element.29.b0, f32[224,128]{1,0:T(8,128)S(1)} %collective-permute-done.3.b1, f32[224,128]{1,0:T(8,128)S(1)} %collective-permute-done.4.b2, f32[224,128]{1,0:T(8,128)S(1)} %collective-permute-done.5.b3, ...), custom_call_target="tpu_custom_call" | custom-call | tf_op jit(solution)/shard_map/solve_row/pallas_call | solution.py:728
  41.9 0.1 collective-permute-start.6
  42.0 1.2 %collective-permute-done.6.e1 = f32[32,128]{1,0:T(8,128)S(1)} collective-permute-done((f32[32,128]{1,0:T(8,128)S(1)}, f32[32,128]{1,0:T(8,128)S(1)}, u32[]{:S(2)}, u32[]{:S(2)}) %collective-permute-start.6) | collective-permute-done | bytes 16416 | tf_op jit(solution)/shard_map/ppermute | solution.py:748
  43.1 5.9 %backward_x.1.p_ref = f32[5,512,128]{2,1,0:T(8,128)S(1)} custom-call(s32[4]{0:T(128)S(1)} %pad_add_fusion.spots_ref.refs_0_, f32[32,60,8,128]{3,2,1,0:T(8,128)} %get-tuple-element.25.fac_ref, f32[60,8,128]{2,1,0:T(8,128)S(1)} %get-tuple-element.26.mid_ref, f32[32,128]{1,0:T(8,128)S(1)} %solve_row.1.e0, f32[32,128]{1,0:T(8,128)S(1)} %collective-permute-done.6.e1, ...), custom_call_target="tpu_custom_call" | custom-call | tf_op jit(solution)/shard_map/backward_x/pallas_call | solution.py:775
  49.1 15.9 %forward_y.1 = (f32[32,60,8,128]{3,2,1,0:T(8,128)}, f32[60,8,128]{2,1,0:T(8,128)S(1)}, f32[512,128]{1,0:T(8,128)S(1)}, f32[512,128]{1,0:T(8,128)S(1)}, f32[512,1...) custom-call(s32[4]{0:T(128)S(1)} %pad_add_fusion.spots_ref.refs_0_, ...), custom_call_target="tpu_custom_call" | custom-call | tf_op jit(solution)/shard_map/forward_y/pallas_call | solution.py:714
  65.0 1.9 %collective-permute-start.7 = (f32[112,128]{1,0:T(8,128)S(1)}, f32[112,128]{1,0:T(8,128)S(1)}, u32[]{:S(2)}, u32[]{:S(2)}) collective-permute-start(f32[112,128]{1,0:T(8,128)S(1)} %get-tuple-element.37), channel_id=1, source_target_pairs={{0,3},{1,0},{2,1},{3,2},{4,7},{5,4},{6,5},{7,6},{8,11},{9,8},{10,9... | collective-permute-start | bytes 172040 | tf_op jit(solution)/shard_map/ppermute | solution.py:748
  66.9 0.0 collective-permute-start.8
  66.9 0.9 collective-permute-start.9
  67.8 2.0 %collective-permute-done.7.refs_2_ = f32[112,128]{1,0:T(8,128)S(1)} collective-permute-done((f32[112,128]{1,0:T(8,128)S(1)}, f32[112,128]{1,0:T(8,128)S(1)}, u32[]{:S(2)}, u32[]{:S(2)}) %collective-permute-start.7) | collective-permute-done | bytes 57376 | tf_op jit(solution)/shard_map/ppermute | solution.py:748
  69.7 3.1 %collective-permute-done.8.refs_3_ = f32[112,128]{1,0:T(8,128)S(1)} collective-permute-done((f32[112,128]{1,0:T(8,128)S(1)}, f32[112,128]{1,0:T(8,128)S(1)}, u32[]{:S(2)}, u32[]{:S(2)}) %collective-permute-start.8) | collective-permute-done | bytes 57376 | tf_op jit(solution)/shard_map/ppermute | solution.py:748
  72.8 0.3 collective-permute-done.9.refs_4_
  73.0 1.4 %join_col.1 = (f32[112,128]{1,0:T(8,128)S(1)}, f32[3,56,128]{2,1,0:T(8,128)S(1)}) custom-call(s32[4]{0:T(128)S(1)} %pad_add_fusion.spots_ref.refs_0_, f32[112,128]{1,0:T(8,128)S(1)} %get-tuple-element.36.refs_1_, f32[112,128]{1,0:T(8,128)S(1)} %collective-permute-done.7.refs_2_, f32[112,128]{1,0:T(8,128)S(1)} %collective-permute-done.8.refs_3_, ...), custom_call_target="tpu_custom_call" | custom-call | tf_op jit(solution)/shard_map/join_col/pallas_call | solution.py:728
  74.5 1.6 %collective-permute-start.12 = (f32[112,128]{1,0:T(8,128)S(1)}, f32[112,128]{1,0:T(8,128)S(1)}, u32[]{:S(2)}, u32[]{:S(2)}) collective-permute-start(f32[112,128]{1,0:T(8,128)S(1)} %get-tuple-element.40.b0), channel_id=1, source_target_pairs={{12,0},{13,1},{14,2},{15,3},{0,4},{1,5},{2,6},{3,7},{4,8},{5,9},{6... | collective-permute-start | bytes 172040 | tf_op jit(solution)/shard_map/ppermute | solution.py:765
  76.1 4.0 %collective-permute-start.11 = (f32[112,128]{1,0:T(8,128)S(1)}, f32[112,128]{1,0:T(8,128)S(1)}, u32[]{:S(2)}, u32[]{:S(2)}) collective-permute-start(f32[112,128]{1,0:T(8,128)S(1)} %get-tuple-element.40.b0), channel_id=1, source_target_pairs={{8,0},{9,1},{10,2},{11,3},{12,4},{13,5},{14,6},{15,7},{0,8},{1,9},... | collective-permute-start | bytes 172040 | tf_op jit(solution)/shard_map/ppermute | solution.py:765
  80.1 0.1 collective-permute-start.10
  80.2 1.2 %collective-permute-done.12.b3 = f32[112,128]{1,0:T(8,128)S(1)} collective-permute-done((f32[112,128]{1,0:T(8,128)S(1)}, f32[112,128]{1,0:T(8,128)S(1)}, u32[]{:S(2)}, u32[]{:S(2)}) %collective-permute-start.12) | collective-permute-done | bytes 57376 | tf_op jit(solution)/shard_map/ppermute | solution.py:765
  81.4 1.5 %collective-permute-done.11.b2 = f32[112,128]{1,0:T(8,128)S(1)} collective-permute-done((f32[112,128]{1,0:T(8,128)S(1)}, f32[112,128]{1,0:T(8,128)S(1)}, u32[]{:S(2)}, u32[]{:S(2)}) %collective-permute-start.11) | collective-permute-done | bytes 57376 | tf_op jit(solution)/shard_map/ppermute | solution.py:765
  82.9 1.4 %collective-permute-done.10.b1 = f32[112,128]{1,0:T(8,128)S(1)} collective-permute-done((f32[112,128]{1,0:T(8,128)S(1)}, f32[112,128]{1,0:T(8,128)S(1)}, u32[]{:S(2)}, u32[]{:S(2)}) %collective-permute-start.10) | collective-permute-done | bytes 57376 | tf_op jit(solution)/shard_map/ppermute | solution.py:765
  84.3 1.2 %solve_col.1.e0 = f32[32,128]{1,0:T(8,128)S(1)} custom-call(s32[4]{0:T(128)S(1)} %pad_add_fusion.spots_ref.refs_0_, f32[112,128]{1,0:T(8,128)S(1)} %get-tuple-element.40.b0, f32[112,128]{1,0:T(8,128)S(1)} %collective-permute-done.10.b1, f32[112,128]{1,0:T(8,128)S(1)} %collective-permute-done.11.b2, f32[112,128]{1,0:T(8,128)S(1)} %collective-permute-done.12.b3, ...), custom_call_target="tpu_custom_call" | custom-call | tf_op jit(solution)/shard_map/solve_col/pallas_call | solution.py:728
  85.4 0.1 collective-permute-start.15
  85.5 2.3 %collective-permute-start.14 = (f32[32,128]{1,0:T(8,128)S(1)}, f32[32,128]{1,0:T(8,128)S(1)}, u32[]{:S(2)}, u32[]{:S(2)}) collective-permute-start(f32[32,128]{1,0:T(8,128)S(1)} %solve_col.1.e0), channel_id=1, source_target_pairs={{0,2},{1,3},{2,0},{3,1},{4,6},{5,7},{6,4},{7,5},{8,10},{9,11},{10,... | collective-permute-start | bytes 49160 | tf_op jit(solution)/shard_map/ppermute | solution.py:748
  87.8 1.9 %collective-permute-start.13 = (f32[32,128]{1,0:T(8,128)S(1)}, f32[32,128]{1,0:T(8,128)S(1)}, u32[]{:S(2)}, u32[]{:S(2)}) collective-permute-start(f32[32,128]{1,0:T(8,128)S(1)} %solve_col.1.e0), channel_id=1, source_target_pairs={{0,3},{1,0},{2,1},{3,2},{4,7},{5,4},{6,5},{7,6},{8,11},{9,8},{10,9... | collective-permute-start | bytes 49160 | tf_op jit(solution)/shard_map/ppermute | solution.py:748
  89.7 0.8 collective-permute-done.15.e3
  90.5 0.4 collective-permute-done.14.e2
  90.9 0.7 collective-permute-done.13.e1
  91.6 7.3 %backward_y.1 = f32[5,512,128]{2,1,0:T(8,128)} custom-call(s32[4]{0:T(128)S(1)} %pad_add_fusion.spots_ref.refs_0_, f32[32,60,8,128]{3,2,1,0:T(8,128)} %get-tuple-element.34.fac_ref, f32[60,8,128]{2,1,0:T(8,128)S(1)} %get-tuple-element.35.mid_ref, f32[32,128]{1,0:T(8,128)S(1)} %solve_col.1.e0, f32[32,128]{1,0:T(8,128)S(1)} %collective-permute-done.13.e1, ...), custom_call_target="tpu_custom_call" | custom-call | tf_op jit(solution)/shard_map/backward_y/pallas_call | solution.py:775
  (13 shorter events, 0.0 us)
Async XLA Ops:
  0.0 9.7 %copy-start.6 = (s32[2]{0:T(128)S(1)}, s32[2]{0:T(128)}, u32[]{:S(2)}) copy-start(s32[2]{0:T(128)} %constant.57) | copy-start | bytes 28
  0.0 11.3 %copy-start = (f32[5,4,128,128]{3,2,1,0:T(8,128)S(1)}, f32[5,4,128,128]{3,2,1,0:T(8,128)}, u32[]{:S(2)}) copy-start(f32[5,4,128,128]{3,2,1,0:T(8,128)} %param.7) | copy-start | bytes 3932164
  0.0 9.9 %copy-start.4 = (f32[5,5,128]{2,1,0:T(8,128)S(1)}, f32[5,5,128]{2,1,0:T(8,128)}, u32[]{:S(2)}) copy-start(f32[5,5,128]{2,1,0:T(8,128)} %param.12) | copy-start | bytes 38404
  0.0 9.9 %copy-start.5 = (f32[5,5,128]{2,1,0:T(8,128)S(1)}, f32[5,5,128]{2,1,0:T(8,128)}, u32[]{:S(2)}) copy-start(f32[5,5,128]{2,1,0:T(8,128)} %param.11) | copy-start | bytes 38404
  0.0 11.3 %copy-start.2 = (f32[128,128]{1,0:T(8,128)S(1)}, f32[128,128]{1,0:T(8,128)}, u32[]{:S(2)}) copy-start(f32[128,128]{1,0:T(8,128)} %my_ref.3) | copy-start | bytes 196612
  0.0 11.3 %copy-start.3 = (f32[128,128]{1,0:T(8,128)S(1)}, f32[128,128]{1,0:T(8,128)}, u32[]{:S(2)}) copy-start(f32[128,128]{1,0:T(8,128)} %mx_ref.1) | copy-start | bytes 196612
  0.0 11.3 %copy-start.1 = (f32[4,128,128]{2,1,0:T(8,128)S(1)}, f32[4,128,128]{2,1,0:T(8,128)}, u32[]{:S(2)}) copy-start(f32[4,128,128]{2,1,0:T(8,128)} %param.8) | copy-start | bytes 786436
  3.0 8.3 %collective-permute-start = (f32[20,128]{1,0:T(8,128)S(1)}, f32[20,128]{1,0:T(8,128)S(1)}, u32[]{:S(2)}, u32[]{:S(2)}) collective-permute-start(f32[20,128]{1,0:T(8,128)S(1)} %reshape_squeeze.6), channel_id=1, source_target_pairs={{0,1},{1,2},{2,3},{3,4},{4,5},{5,6},{6,7},{7,8},{8,9},{9,10},{10,1... | collective-permute-start | bytes 30728 | tf_op jit(solution)/shard_map/ppermute | solution.py:795
  5.1 6.2 %collective-permute-start.1 = (f32[20,128]{1,0:T(8,128)S(1)}, f32[20,128]{1,0:T(8,128)S(1)}, u32[]{:S(2)}, u32[]{:S(2)}) collective-permute-start(f32[20,128]{1,0:T(8,128)S(1)} %reshape_squeeze.7), channel_id=1, source_target_pairs={{1,0},{2,1},{3,2},{4,3},{5,4},{6,5},{7,6},{8,7},{9,8},{10,9},{11,1... | collective-permute-start | bytes 30728 | tf_op jit(solution)/shard_map/ppermute | solution.py:795
  28.6 1.3 %collective-permute-start.2 = (f32[224,128]{1,0:T(8,128)S(1)}, f32[224,128]{1,0:T(8,128)S(1)}, u32[]{:S(2)}, u32[]{:S(2)}) collective-permute-start(f32[224,128]{1,0:T(8,128)S(1)} %get-tuple-element.28), channel_id=1, source_target_pairs={{0,16},{16,0},{32,48},{48,32},{64,80},{80,64},{96,112},{112,96},{1... | collective-permute-start | bytes 344072 | tf_op jit(solution)/shard_map/ppermute | solution.py:748
  30.8 6.5 %collective-permute-start.5 = (f32[224,128]{1,0:T(8,128)S(1)}, f32[224,128]{1,0:T(8,128)S(1)}, u32[]{:S(2)}, u32[]{:S(2)}) collective-permute-start(f32[224,128]{1,0:T(8,128)S(1)} %get-tuple-element.29.b0), channel_id=1, source_target_pairs={{96,0},{112,16},{0,32},{16,48},{32,64},{48,80},{64,96},{80,112},{9... | collective-permute-start | bytes 344072 | tf_op jit(solution)/shard_map/ppermute | solution.py:765
  32.4 8.4 %collective-permute-start.4 = (f32[224,128]{1,0:T(8,128)S(1)}, f32[224,128]{1,0:T(8,128)S(1)}, u32[]{:S(2)}, u32[]{:S(2)}) collective-permute-start(f32[224,128]{1,0:T(8,128)S(1)} %get-tuple-element.29.b0), channel_id=1, source_target_pairs={{64,0},{80,16},{96,32},{112,48},{0,64},{16,80},{32,96},{48,112},{6... | collective-permute-start | bytes 344072 | tf_op jit(solution)/shard_map/ppermute | solution.py:765
  35.1 5.6 %collective-permute-start.3 = (f32[224,128]{1,0:T(8,128)S(1)}, f32[224,128]{1,0:T(8,128)S(1)}, u32[]{:S(2)}, u32[]{:S(2)}) collective-permute-start(f32[224,128]{1,0:T(8,128)S(1)} %get-tuple-element.29.b0), channel_id=1, source_target_pairs={{32,0},{48,16},{64,32},{80,48},{96,64},{112,80},{0,96},{16,112},{3... | collective-permute-start | bytes 344072 | tf_op jit(solution)/shard_map/ppermute | solution.py:765
  41.9 1.3 %collective-permute-start.6 = (f32[32,128]{1,0:T(8,128)S(1)}, f32[32,128]{1,0:T(8,128)S(1)}, u32[]{:S(2)}, u32[]{:S(2)}) collective-permute-start(f32[32,128]{1,0:T(8,128)S(1)} %solve_row.1.e0), channel_id=1, source_target_pairs={{0,16},{16,0},{32,48},{48,32},{64,80},{80,64},{96,112},{112,96},{1... | collective-permute-start | bytes 49160 | tf_op jit(solution)/shard_map/ppermute | solution.py:748
  65.0 4.7 %collective-permute-start.7 = (f32[112,128]{1,0:T(8,128)S(1)}, f32[112,128]{1,0:T(8,128)S(1)}, u32[]{:S(2)}, u32[]{:S(2)}) collective-permute-start(f32[112,128]{1,0:T(8,128)S(1)} %get-tuple-element.37), channel_id=1, source_target_pairs={{0,3},{1,0},{2,1},{3,2},{4,7},{5,4},{6,5},{7,6},{8,11},{9,8},{10,9... | collective-permute-start | bytes 172040 | tf_op jit(solution)/shard_map/ppermute | solution.py:748
  66.9 5.9 %collective-permute-start.8 = (f32[112,128]{1,0:T(8,128)S(1)}, f32[112,128]{1,0:T(8,128)S(1)}, u32[]{:S(2)}, u32[]{:S(2)}) collective-permute-start(f32[112,128]{1,0:T(8,128)S(1)} %get-tuple-element.38), channel_id=1, source_target_pairs={{0,2},{1,3},{2,0},{3,1},{4,6},{5,7},{6,4},{7,5},{8,10},{9,11},{10,... | collective-permute-start | bytes 172040 | tf_op jit(solution)/shard_map/ppermute | solution.py:748
  66.9 6.1 %collective-permute-start.9 = (f32[112,128]{1,0:T(8,128)S(1)}, f32[112,128]{1,0:T(8,128)S(1)}, u32[]{:S(2)}, u32[]{:S(2)}) collective-permute-start(f32[112,128]{1,0:T(8,128)S(1)} %get-tuple-element.39), channel_id=1, source_target_pairs={{0,1},{1,2},{2,3},{3,0},{4,5},{5,6},{6,7},{7,4},{8,9},{9,10},{10,1... | collective-permute-start | bytes 172040 | tf_op jit(solution)/shard_map/ppermute | solution.py:748
  74.5 6.9 %collective-permute-start.12 = (f32[112,128]{1,0:T(8,128)S(1)}, f32[112,128]{1,0:T(8,128)S(1)}, u32[]{:S(2)}, u32[]{:S(2)}) collective-permute-start(f32[112,128]{1,0:T(8,128)S(1)} %get-tuple-element.40.b0), channel_id=1, source_target_pairs={{12,0},{13,1},{14,2},{15,3},{0,4},{1,5},{2,6},{3,7},{4,8},{5,9},{6... | collective-permute-start | bytes 172040 | tf_op jit(solution)/shard_map/ppermute | solution.py:765
  76.1 6.8 %collective-permute-start.11 = (f32[112,128]{1,0:T(8,128)S(1)}, f32[112,128]{1,0:T(8,128)S(1)}, u32[]{:S(2)}, u32[]{:S(2)}) collective-permute-start(f32[112,128]{1,0:T(8,128)S(1)} %get-tuple-element.40.b0), channel_id=1, source_target_pairs={{8,0},{9,1},{10,2},{11,3},{12,4},{13,5},{14,6},{15,7},{0,8},{1,9},... | collective-permute-start | bytes 172040 | tf_op jit(solution)/shard_map/ppermute | solution.py:765
  80.1 4.2 %collective-permute-start.10 = (f32[112,128]{1,0:T(8,128)S(1)}, f32[112,128]{1,0:T(8,128)S(1)}, u32[]{:S(2)}, u32[]{:S(2)}) collective-permute-start(f32[112,128]{1,0:T(8,128)S(1)} %get-tuple-element.40.b0), channel_id=1, source_target_pairs={{4,0},{5,1},{6,2},{7,3},{8,4},{9,5},{10,6},{11,7},{12,8},{13,9},{1... | collective-permute-start | bytes 172040 | tf_op jit(solution)/shard_map/ppermute | solution.py:765
  85.4 5.0 %collective-permute-start.15 = (f32[32,128]{1,0:T(8,128)S(1)}, f32[32,128]{1,0:T(8,128)S(1)}, u32[]{:S(2)}, u32[]{:S(2)}) collective-permute-start(f32[32,128]{1,0:T(8,128)S(1)} %solve_col.1.e0), channel_id=1, source_target_pairs={{0,1},{1,2},{2,3},{3,0},{4,5},{5,6},{6,7},{7,4},{8,9},{9,10},{10,1... | collective-permute-start | bytes 49160 | tf_op jit(solution)/shard_map/ppermute | solution.py:748
  85.5 5.3 %collective-permute-start.14 = (f32[32,128]{1,0:T(8,128)S(1)}, f32[32,128]{1,0:T(8,128)S(1)}, u32[]{:S(2)}, u32[]{:S(2)}) collective-permute-start(f32[32,128]{1,0:T(8,128)S(1)} %solve_col.1.e0), channel_id=1, source_target_pairs={{0,2},{1,3},{2,0},{3,1},{4,6},{5,7},{6,4},{7,5},{8,10},{9,11},{10,... | collective-permute-start | bytes 49160 | tf_op jit(solution)/shard_map/ppermute | solution.py:748
  87.8 3.7 %collective-permute-start.13 = (f32[32,128]{1,0:T(8,128)S(1)}, f32[32,128]{1,0:T(8,128)S(1)}, u32[]{:S(2)}, u32[]{:S(2)}) collective-permute-start(f32[32,128]{1,0:T(8,128)S(1)} %solve_col.1.e0), channel_id=1, source_target_pairs={{0,3},{1,0},{2,1},{3,2},{4,7},{5,4},{6,5},{7,6},{8,11},{9,8},{10,9... | collective-permute-start | bytes 49160 | tf_op jit(solution)/shard_map/ppermute | solution.py:748

commit v4 on v3

--- a/solution.py
+++ b/solution.py
@@ -15,7 +15,7 @@
 CHUNK = 8
 STEPS = KEPT // CHUNK
 FACTORS = 60
-VMEM_LIMIT = 48 * 1024 * 1024
+VMEM_LIMIT = 20 * 1024 * 1024
 
 
 def zeros():

time: 99 us -> 92.8 us (0.937)
  Pallas kernels: 51 us -> 44.6 us
    pallas_call x2, Pallas kernels: 13.2 us -> 9.49 us  [backward(): pl.pallas_call(kernel, grid=(STEPS,), in_specs=[scalars(), pl.BlockSpec((...]
    pallas_call x2, Pallas kernels: 33.2 us -> 30.5 us  [forward(): pl.pallas_call(kernel, grid=(STEPS,), in_specs=[scalars() for _ in flags]...]
where the time goes in v4:
time: 92.8 us; the launch traced here: 92.7 us
  Pallas kernels  44.6 us (48%)
  starting transfers between devices  25.6 us (28%)
  waiting for transfers between devices  19.2 us (21%)
  local copies, waits for them, and re-layouts  3 us (3%)
    pallas_call x2, Pallas kernels, forward(): pl.pallas_call(kernel, grid=(STEPS,), in_specs=[scalars() for _ in flags]...  30.5 us
    ppermute x6, starting transfers between devices, line_ends(): blocks[far] = lax.ppermute(port, axis, moves)  11.5 us
    ppermute x8, waiting for transfers between devices, exchange(): received[offset] = lax.ppermute(values[back], axis, moves)  9.54 us
    pallas_call x2, Pallas kernels, backward(): pl.pallas_call(kernel, grid=(STEPS,), in_specs=[scalars(), pl.BlockSpec((...  9.49 us
    ppermute x6, waiting for transfers between devices, line_ends(): blocks[far] = lax.ppermute(port, axis, moves)  8.24 us
    ppermute x8, starting transfers between devices, exchange(): received[offset] = lax.ppermute(values[back], axis, moves)  7.33 us
    ppermute x2, starting transfers between devices, halos(): return (lax.ppermute(last, axis, up), lax.ppermute(initial, axis, down))  6.74 us
    pallas_call x4, Pallas kernels, small(): pl.pallas_call(kernel, out_shape=tuple((jax.ShapeDtypeStruct(shape, F32)...  4.59 us
  transfers between devices with their start and end apart: 16, of which 14 were waited for; matrix products, arithmetic and copies ran while one was open for 0% of the time, Pallas kernels for 0%

profile of v4, /device:TPU:0, one launch (start us, length us, event | category | flops | bytes accessed | tf_op | source)
XLA Modules:
  0.0 92.7 jit_solution(6908846129167178139)
XLA Ops:
  0.0 0.0 copy-start.3
  0.0 0.0 copy-start.1
  0.0 2.9 %slice_reduce_fusion = (f32[5,4,128]{2,1,0:T(4,128)S(1)}, f32[5,4,128]{2,1,0:T(4,128)S(1)}) fusion(f32[5,4,128,128]{3,2,1,0:T(8,128)} %param.7), kind=kLoop, calls=%fused_computation | loop fusion | bytes 40960 | tf_op jit(solution)/shard_map/slice | solution.py:811
  3.0 2.1 %collective-permute-start = (f32[20,128]{1,0:T(8,128)S(1)}, f32[20,128]{1,0:T(8,128)S(1)}, u32[]{:S(2)}, u32[]{:S(2)}) collective-permute-start(f32[20,128]{1,0:T(8,128)S(1)} %reshape_squeeze.6), channel_id=1, source_target_pairs={{0,1},{1,2},{2,3},{3,4},{4,5},{5,6},{6,7},{7,8},{8,9},{9,10},{10,1... | collective-permute-start | bytes 30728 | tf_op jit(solution)/shard_map/ppermute | solution.py:795
  5.1 4.7 %collective-permute-start.1 = (f32[20,128]{1,0:T(8,128)S(1)}, f32[20,128]{1,0:T(8,128)S(1)}, u32[]{:S(2)}, u32[]{:S(2)}) collective-permute-start(f32[20,128]{1,0:T(8,128)S(1)} %reshape_squeeze.7), channel_id=1, source_target_pairs={{1,0},{2,1},{3,2},{4,3},{5,4},{6,5},{7,6},{8,7},{9,8},{10,9},{11,1... | collective-permute-start | bytes 30728 | tf_op jit(solution)/shard_map/ppermute | solution.py:795
  9.7 0.0 copy-done.6
  9.7 0.1 compare_convert_fusion
  9.8 0.1 pad_add_fusion.spots_ref.refs_0_
  9.9 0.0 copy-done.5
  9.9 1.4 %collective-permute-done.south_ref = f32[20,128]{1,0:T(8,128)S(1)} collective-permute-done((f32[20,128]{1,0:T(8,128)S(1)}, f32[20,128]{1,0:T(8,128)S(1)}, u32[]{:S(2)}, u32[]{:S(2)}) %collective-permute-start) | collective-permute-done | bytes 10272 | tf_op jit(solution)/shard_map/ppermute | solution.py:795
  11.3 0.0 collective-permute-done.1.north_ref
  11.3 0.0 copy-done.2
  11.4 15.9 %forward_x.1 = (f32[32,60,8,128]{3,2,1,0:T(8,128)S(1)}, f32[60,8,128]{2,1,0:T(8,128)S(1)}, f32[512,128]{1,0:T(8,128)S(1)}, f32[512,128]{1,0:T(8,128)S(1)}, f32[5...) custom-call(s32[4]{0:T(128)S(1)} %pad_add_fusion.spots_ref.refs_0_, ...), custom_call_target="tpu_custom_call" | custom-call | tf_op jit(solution)/shard_map/forward_x/pallas_call | solution.py:714
  27.3 0.1 collective-permute-start.2
  27.4 1.3 %collective-permute-done.2.refs_2_ = f32[224,128]{1,0:T(8,128)S(1)} collective-permute-done((f32[224,128]{1,0:T(8,128)S(1)}, f32[224,128]{1,0:T(8,128)S(1)}, u32[]{:S(2)}, u32[]{:S(2)}) %collective-permute-start.2) | collective-permute-done | bytes 114720 | tf_op jit(solution)/shard_map/ppermute | solution.py:748
  28.7 0.9 join_row.1
  29.5 1.6 %collective-permute-start.5 = (f32[224,128]{1,0:T(8,128)S(1)}, f32[224,128]{1,0:T(8,128)S(1)}, u32[]{:S(2)}, u32[]{:S(2)}) collective-permute-start(f32[224,128]{1,0:T(8,128)S(1)} %get-tuple-element.29.b0), channel_id=1, source_target_pairs={{96,0},{112,16},{0,32},{16,48},{32,64},{48,80},{64,96},{80,112},{9... | collective-permute-start | bytes 344072 | tf_op jit(solution)/shard_map/ppermute | solution.py:765
  31.1 2.7 %collective-permute-start.4 = (f32[224,128]{1,0:T(8,128)S(1)}, f32[224,128]{1,0:T(8,128)S(1)}, u32[]{:S(2)}, u32[]{:S(2)}) collective-permute-start(f32[224,128]{1,0:T(8,128)S(1)} %get-tuple-element.29.b0), channel_id=1, source_target_pairs={{64,0},{80,16},{96,32},{112,48},{0,64},{16,80},{32,96},{48,112},{6... | collective-permute-start | bytes 344072 | tf_op jit(solution)/shard_map/ppermute | solution.py:765
  33.8 1.4 %collective-permute-start.3 = (f32[224,128]{1,0:T(8,128)S(1)}, f32[224,128]{1,0:T(8,128)S(1)}, u32[]{:S(2)}, u32[]{:S(2)}) collective-permute-start(f32[224,128]{1,0:T(8,128)S(1)} %get-tuple-element.29.b0), channel_id=1, source_target_pairs={{32,0},{48,16},{64,32},{80,48},{96,64},{112,80},{0,96},{16,112},{3... | collective-permute-start | bytes 344072 | tf_op jit(solution)/shard_map/ppermute | solution.py:765
  35.3 0.8 collective-permute-done.5.b3
  36.0 3.4 %collective-permute-done.4.b2 = f32[224,128]{1,0:T(8,128)S(1)} collective-permute-done((f32[224,128]{1,0:T(8,128)S(1)}, f32[224,128]{1,0:T(8,128)S(1)}, u32[]{:S(2)}, u32[]{:S(2)}) %collective-permute-start.4) | collective-permute-done | bytes 114720 | tf_op jit(solution)/shard_map/ppermute | solution.py:765
  39.5 0.0 collective-permute-done.3.b1
  39.5 1.2 %solve_row.1.e0 = f32[32,128]{1,0:T(8,128)S(1)} custom-call(s32[4]{0:T(128)S(1)} %pad_add_fusion.spots_ref.refs_0_, f32[224,128]{1,0:T(8,128)S(1)} %get-tuple-element.29.b0, f32[224,128]{1,0:T(8,128)S(1)} %collective-permute-done.3.b1, f32[224,128]{1,0:T(8,128)S(1)} %collective-permute-done.4.b2, f32[224,128]{1,0:T(8,128)S(1)} %collective-permute-done.5.b3, ...), custom_call_target="tpu_custom_call" | custom-call | tf_op jit(solution)/shard_map/solve_row/pallas_call | solution.py:728
  40.6 0.1 collective-permute-start.6
  40.7 1.2 %collective-permute-done.6.e1 = f32[32,128]{1,0:T(8,128)S(1)} collective-permute-done((f32[32,128]{1,0:T(8,128)S(1)}, f32[32,128]{1,0:T(8,128)S(1)}, u32[]{:S(2)}, u32[]{:S(2)}) %collective-permute-start.6) | collective-permute-done | bytes 16416 | tf_op jit(solution)/shard_map/ppermute | solution.py:748
  41.9 4.1 %backward_x.1.p_ref = f32[5,512,128]{2,1,0:T(8,128)S(1)} custom-call(s32[4]{0:T(128)S(1)} %pad_add_fusion.spots_ref.refs_0_, f32[32,60,8,128]{3,2,1,0:T(8,128)S(1)} %get-tuple-element.25.fac_ref, f32[60,8,128]{2,1,0:T(8,128)S(1)} %get-tuple-element.26.mid_ref, f32[32,128]{1,0:T(8,128)S(1)} %solve_row.1.e0, f32[32,128]{1,0:T(8,128)S(1)} %collective-permute-done.6.e1, ...), custom_call_target="tpu_custom_call" | custom-call | tf_op jit(solution)/shard_map/backward_x/pallas_call | solution.py:775
  46.0 14.6 %forward_y.1 = (f32[32,60,8,128]{3,2,1,0:T(8,128)S(1)}, f32[60,8,128]{2,1,0:T(8,128)S(1)}, f32[512,128]{1,0:T(8,128)S(1)}, f32[512,128]{1,0:T(8,128)S(1)}, f32[5...) custom-call(s32[4]{0:T(128)S(1)} %pad_add_fusion.spots_ref.refs_0_, ...), custom_call_target="tpu_custom_call" | custom-call | tf_op jit(solution)/shard_map/forward_y/pallas_call | solution.py:714
  60.7 2.0 %collective-permute-start.7 = (f32[112,128]{1,0:T(8,128)S(1)}, f32[112,128]{1,0:T(8,128)S(1)}, u32[]{:S(2)}, u32[]{:S(2)}) collective-permute-start(f32[112,128]{1,0:T(8,128)S(1)} %get-tuple-element.37), channel_id=1, source_target_pairs={{0,3},{1,0},{2,1},{3,2},{4,7},{5,4},{6,5},{7,6},{8,11},{9,8},{10,9... | collective-permute-start | bytes 172040 | tf_op jit(solution)/shard_map/ppermute | solution.py:748
  62.6 0.0 collective-permute-start.8
  62.6 0.9 %collective-permute-start.9 = (f32[112,128]{1,0:T(8,128)S(1)}, f32[112,128]{1,0:T(8,128)S(1)}, u32[]{:S(2)}, u32[]{:S(2)}) collective-permute-start(f32[112,128]{1,0:T(8,128)S(1)} %get-tuple-element.39), channel_id=1, source_target_pairs={{0,1},{1,2},{2,3},{3,0},{4,5},{5,6},{6,7},{7,4},{8,9},{9,10},{10,1... | collective-permute-start | bytes 172040 | tf_op jit(solution)/shard_map/ppermute | solution.py:748
  63.6 1.9 %collective-permute-done.7.refs_2_ = f32[112,128]{1,0:T(8,128)S(1)} collective-permute-done((f32[112,128]{1,0:T(8,128)S(1)}, f32[112,128]{1,0:T(8,128)S(1)}, u32[]{:S(2)}, u32[]{:S(2)}) %collective-permute-start.7) | collective-permute-done | bytes 57376 | tf_op jit(solution)/shard_map/ppermute | solution.py:748
  65.5 3.0 %collective-permute-done.8.refs_3_ = f32[112,128]{1,0:T(8,128)S(1)} collective-permute-done((f32[112,128]{1,0:T(8,128)S(1)}, f32[112,128]{1,0:T(8,128)S(1)}, u32[]{:S(2)}, u32[]{:S(2)}) %collective-permute-start.8) | collective-permute-done | bytes 57376 | tf_op jit(solution)/shard_map/ppermute | solution.py:748
  68.5 0.3 collective-permute-done.9.refs_4_
  68.8 1.4 %join_col.1 = (f32[112,128]{1,0:T(8,128)S(1)}, f32[3,56,128]{2,1,0:T(8,128)S(1)}) custom-call(s32[4]{0:T(128)S(1)} %pad_add_fusion.spots_ref.refs_0_, f32[112,128]{1,0:T(8,128)S(1)} %get-tuple-element.36.refs_1_, f32[112,128]{1,0:T(8,128)S(1)} %collective-permute-done.7.refs_2_, f32[112,128]{1,0:T(8,128)S(1)} %collective-permute-done.8.refs_3_, ...), custom_call_target="tpu_custom_call" | custom-call | tf_op jit(solution)/shard_map/join_col/pallas_call | solution.py:728
  70.2 1.6 %collective-permute-start.12 = (f32[112,128]{1,0:T(8,128)S(1)}, f32[112,128]{1,0:T(8,128)S(1)}, u32[]{:S(2)}, u32[]{:S(2)}) collective-permute-start(f32[112,128]{1,0:T(8,128)S(1)} %get-tuple-element.40.b0), channel_id=1, source_target_pairs={{12,0},{13,1},{14,2},{15,3},{0,4},{1,5},{2,6},{3,7},{4,8},{5,9},{6... | collective-permute-start | bytes 172040 | tf_op jit(solution)/shard_map/ppermute | solution.py:765
  71.8 4.0 %collective-permute-start.11 = (f32[112,128]{1,0:T(8,128)S(1)}, f32[112,128]{1,0:T(8,128)S(1)}, u32[]{:S(2)}, u32[]{:S(2)}) collective-permute-start(f32[112,128]{1,0:T(8,128)S(1)} %get-tuple-element.40.b0), channel_id=1, source_target_pairs={{8,0},{9,1},{10,2},{11,3},{12,4},{13,5},{14,6},{15,7},{0,8},{1,9},... | collective-permute-start | bytes 172040 | tf_op jit(solution)/shard_map/ppermute | solution.py:765
  75.8 0.1 collective-permute-start.10
  75.9 1.2 %collective-permute-done.12.b3 = f32[112,128]{1,0:T(8,128)S(1)} collective-permute-done((f32[112,128]{1,0:T(8,128)S(1)}, f32[112,128]{1,0:T(8,128)S(1)}, u32[]{:S(2)}, u32[]{:S(2)}) %collective-permute-start.12) | collective-permute-done | bytes 57376 | tf_op jit(solution)/shard_map/ppermute | solution.py:765
  77.1 1.5 %collective-permute-done.11.b2 = f32[112,128]{1,0:T(8,128)S(1)} collective-permute-done((f32[112,128]{1,0:T(8,128)S(1)}, f32[112,128]{1,0:T(8,128)S(1)}, u32[]{:S(2)}, u32[]{:S(2)}) %collective-permute-start.11) | collective-permute-done | bytes 57376 | tf_op jit(solution)/shard_map/ppermute | solution.py:765
  78.6 1.4 %collective-permute-done.10.b1 = f32[112,128]{1,0:T(8,128)S(1)} collective-permute-done((f32[112,128]{1,0:T(8,128)S(1)}, f32[112,128]{1,0:T(8,128)S(1)}, u32[]{:S(2)}, u32[]{:S(2)}) %collective-permute-start.10) | collective-permute-done | bytes 57376 | tf_op jit(solution)/shard_map/ppermute | solution.py:765
  80.0 1.2 %solve_col.1.e0 = f32[32,128]{1,0:T(8,128)S(1)} custom-call(s32[4]{0:T(128)S(1)} %pad_add_fusion.spots_ref.refs_0_, f32[112,128]{1,0:T(8,128)S(1)} %get-tuple-element.40.b0, f32[112,128]{1,0:T(8,128)S(1)} %collective-permute-done.10.b1, f32[112,128]{1,0:T(8,128)S(1)} %collective-permute-done.11.b2, f32[112,128]{1,0:T(8,128)S(1)} %collective-permute-done.12.b3, ...), custom_call_target="tpu_custom_call" | custom-call | tf_op jit(solution)/shard_map/solve_col/pallas_call | solution.py:728
  81.2 0.1 collective-permute-start.15
  81.2 2.3 %collective-permute-start.14 = (f32[32,128]{1,0:T(8,128)S(1)}, f32[32,128]{1,0:T(8,128)S(1)}, u32[]{:S(2)}, u32[]{:S(2)}) collective-permute-start(f32[32,128]{1,0:T(8,128)S(1)} %solve_col.1.e0), channel_id=1, source_target_pairs={{0,2},{1,3},{2,0},{3,1},{4,6},{5,7},{6,4},{7,5},{8,10},{9,11},{10,... | collective-permute-start | bytes 49160 | tf_op jit(solution)/shard_map/ppermute | solution.py:748
  83.5 1.9 %collective-permute-start.13 = (f32[32,128]{1,0:T(8,128)S(1)}, f32[32,128]{1,0:T(8,128)S(1)}, u32[]{:S(2)}, u32[]{:S(2)}) collective-permute-start(f32[32,128]{1,0:T(8,128)S(1)} %solve_col.1.e0), channel_id=1, source_target_pairs={{0,3},{1,0},{2,1},{3,2},{4,7},{5,4},{6,5},{7,6},{8,11},{9,8},{10,9... | collective-permute-start | bytes 49160 | tf_op jit(solution)/shard_map/ppermute | solution.py:748
  85.4 0.8 collective-permute-done.15.e3
  86.2 0.4 collective-permute-done.14.e2
  86.6 0.7 collective-permute-done.13.e1
  87.3 5.4 %backward_y.1 = f32[5,512,128]{2,1,0:T(8,128)} custom-call(s32[4]{0:T(128)S(1)} %pad_add_fusion.spots_ref.refs_0_, f32[32,60,8,128]{3,2,1,0:T(8,128)S(1)} %get-tuple-element.34.fac_ref, f32[60,8,128]{2,1,0:T(8,128)S(1)} %get-tuple-element.35.mid_ref, f32[32,128]{1,0:T(8,128)S(1)} %solve_col.1.e0, f32[32,128]{1,0:T(8,128)S(1)} %collective-permute-done.13.e1, ...), custom_call_target="tpu_custom_call" | custom-call | tf_op jit(solution)/shard_map/backward_y/pallas_call | solution.py:775
  (13 shorter events, 0.0 us)
Async XLA Ops:
  0.0 9.7 %copy-start.6 = (s32[2]{0:T(128)S(1)}, s32[2]{0:T(128)}, u32[]{:S(2)}) copy-start(s32[2]{0:T(128)} %constant.57) | copy-start | bytes 28
  0.0 11.3 %copy-start = (f32[5,4,128,128]{3,2,1,0:T(8,128)S(1)}, f32[5,4,128,128]{3,2,1,0:T(8,128)}, u32[]{:S(2)}) copy-start(f32[5,4,128,128]{3,2,1,0:T(8,128)} %param.7) | copy-start | bytes 3932164
  0.0 9.9 %copy-start.4 = (f32[5,5,128]{2,1,0:T(8,128)S(1)}, f32[5,5,128]{2,1,0:T(8,128)}, u32[]{:S(2)}) copy-start(f32[5,5,128]{2,1,0:T(8,128)} %param.12) | copy-start | bytes 38404
  0.0 9.9 %copy-start.5 = (f32[5,5,128]{2,1,0:T(8,128)S(1)}, f32[5,5,128]{2,1,0:T(8,128)}, u32[]{:S(2)}) copy-start(f32[5,5,128]{2,1,0:T(8,128)} %param.11) | copy-start | bytes 38404
  0.0 11.3 %copy-start.2 = (f32[128,128]{1,0:T(8,128)S(1)}, f32[128,128]{1,0:T(8,128)}, u32[]{:S(2)}) copy-start(f32[128,128]{1,0:T(8,128)} %my_ref.3) | copy-start | bytes 196612
  0.0 11.3 %copy-start.3 = (f32[128,128]{1,0:T(8,128)S(1)}, f32[128,128]{1,0:T(8,128)}, u32[]{:S(2)}) copy-start(f32[128,128]{1,0:T(8,128)} %mx_ref.1) | copy-start | bytes 196612
  0.0 11.3 %copy-start.1 = (f32[4,128,128]{2,1,0:T(8,128)S(1)}, f32[4,128,128]{2,1,0:T(8,128)}, u32[]{:S(2)}) copy-start(f32[4,128,128]{2,1,0:T(8,128)} %param.8) | copy-start | bytes 786436
  3.0 8.3 %collective-permute-start = (f32[20,128]{1,0:T(8,128)S(1)}, f32[20,128]{1,0:T(8,128)S(1)}, u32[]{:S(2)}, u32[]{:S(2)}) collective-permute-start(f32[20,128]{1,0:T(8,128)S(1)} %reshape_squeeze.6), channel_id=1, source_target_pairs={{0,1},{1,2},{2,3},{3,4},{4,5},{5,6},{6,7},{7,8},{8,9},{9,10},{10,1... | collective-permute-start | bytes 30728 | tf_op jit(solution)/shard_map/ppermute | solution.py:795
  5.1 6.2 %collective-permute-start.1 = (f32[20,128]{1,0:T(8,128)S(1)}, f32[20,128]{1,0:T(8,128)S(1)}, u32[]{:S(2)}, u32[]{:S(2)}) collective-permute-start(f32[20,128]{1,0:T(8,128)S(1)} %reshape_squeeze.7), channel_id=1, source_target_pairs={{1,0},{2,1},{3,2},{4,3},{5,4},{6,5},{7,6},{8,7},{9,8},{10,9},{11,1... | collective-permute-start | bytes 30728 | tf_op jit(solution)/shard_map/ppermute | solution.py:795
  27.3 1.4 %collective-permute-start.2 = (f32[224,128]{1,0:T(8,128)S(1)}, f32[224,128]{1,0:T(8,128)S(1)}, u32[]{:S(2)}, u32[]{:S(2)}) collective-permute-start(f32[224,128]{1,0:T(8,128)S(1)} %get-tuple-element.28), channel_id=1, source_target_pairs={{0,16},{16,0},{32,48},{48,32},{64,80},{80,64},{96,112},{112,96},{1... | collective-permute-start | bytes 344072 | tf_op jit(solution)/shard_map/ppermute | solution.py:748
  29.5 6.5 %collective-permute-start.5 = (f32[224,128]{1,0:T(8,128)S(1)}, f32[224,128]{1,0:T(8,128)S(1)}, u32[]{:S(2)}, u32[]{:S(2)}) collective-permute-start(f32[224,128]{1,0:T(8,128)S(1)} %get-tuple-element.29.b0), channel_id=1, source_target_pairs={{96,0},{112,16},{0,32},{16,48},{32,64},{48,80},{64,96},{80,112},{9... | collective-permute-start | bytes 344072 | tf_op jit(solution)/shard_map/ppermute | solution.py:765
  31.1 8.4 %collective-permute-start.4 = (f32[224,128]{1,0:T(8,128)S(1)}, f32[224,128]{1,0:T(8,128)S(1)}, u32[]{:S(2)}, u32[]{:S(2)}) collective-permute-start(f32[224,128]{1,0:T(8,128)S(1)} %get-tuple-element.29.b0), channel_id=1, source_target_pairs={{64,0},{80,16},{96,32},{112,48},{0,64},{16,80},{32,96},{48,112},{6... | collective-permute-start | bytes 344072 | tf_op jit(solution)/shard_map/ppermute | solution.py:765
  33.8 5.6 %collective-permute-start.3 = (f32[224,128]{1,0:T(8,128)S(1)}, f32[224,128]{1,0:T(8,128)S(1)}, u32[]{:S(2)}, u32[]{:S(2)}) collective-permute-start(f32[224,128]{1,0:T(8,128)S(1)} %get-tuple-element.29.b0), channel_id=1, source_target_pairs={{32,0},{48,16},{64,32},{80,48},{96,64},{112,80},{0,96},{16,112},{3... | collective-permute-start | bytes 344072 | tf_op jit(solution)/shard_map/ppermute | solution.py:765
  40.6 1.3 %collective-permute-start.6 = (f32[32,128]{1,0:T(8,128)S(1)}, f32[32,128]{1,0:T(8,128)S(1)}, u32[]{:S(2)}, u32[]{:S(2)}) collective-permute-start(f32[32,128]{1,0:T(8,128)S(1)} %solve_row.1.e0), channel_id=1, source_target_pairs={{0,16},{16,0},{32,48},{48,32},{64,80},{80,64},{96,112},{112,96},{1... | collective-permute-start | bytes 49160 | tf_op jit(solution)/shard_map/ppermute | solution.py:748
  60.7 4.9 %collective-permute-start.7 = (f32[112,128]{1,0:T(8,128)S(1)}, f32[112,128]{1,0:T(8,128)S(1)}, u32[]{:S(2)}, u32[]{:S(2)}) collective-permute-start(f32[112,128]{1,0:T(8,128)S(1)} %get-tuple-element.37), channel_id=1, source_target_pairs={{0,3},{1,0},{2,1},{3,2},{4,7},{5,4},{6,5},{7,6},{8,11},{9,8},{10,9... | collective-permute-start | bytes 172040 | tf_op jit(solution)/shard_map/ppermute | solution.py:748
  62.6 5.9 %collective-permute-start.8 = (f32[112,128]{1,0:T(8,128)S(1)}, f32[112,128]{1,0:T(8,128)S(1)}, u32[]{:S(2)}, u32[]{:S(2)}) collective-permute-start(f32[112,128]{1,0:T(8,128)S(1)} %get-tuple-element.38), channel_id=1, source_target_pairs={{0,2},{1,3},{2,0},{3,1},{4,6},{5,7},{6,4},{7,5},{8,10},{9,11},{10,... | collective-permute-start | bytes 172040 | tf_op jit(solution)/shard_map/ppermute | solution.py:748
  62.6 6.1 %collective-permute-start.9 = (f32[112,128]{1,0:T(8,128)S(1)}, f32[112,128]{1,0:T(8,128)S(1)}, u32[]{:S(2)}, u32[]{:S(2)}) collective-permute-start(f32[112,128]{1,0:T(8,128)S(1)} %get-tuple-element.39), channel_id=1, source_target_pairs={{0,1},{1,2},{2,3},{3,0},{4,5},{5,6},{6,7},{7,4},{8,9},{9,10},{10,1... | collective-permute-start | bytes 172040 | tf_op jit(solution)/shard_map/ppermute | solution.py:748
  70.2 6.9 %collective-permute-start.12 = (f32[112,128]{1,0:T(8,128)S(1)}, f32[112,128]{1,0:T(8,128)S(1)}, u32[]{:S(2)}, u32[]{:S(2)}) collective-permute-start(f32[112,128]{1,0:T(8,128)S(1)} %get-tuple-element.40.b0), channel_id=1, source_target_pairs={{12,0},{13,1},{14,2},{15,3},{0,4},{1,5},{2,6},{3,7},{4,8},{5,9},{6... | collective-permute-start | bytes 172040 | tf_op jit(solution)/shard_map/ppermute | solution.py:765
  71.8 6.8 %collective-permute-start.11 = (f32[112,128]{1,0:T(8,128)S(1)}, f32[112,128]{1,0:T(8,128)S(1)}, u32[]{:S(2)}, u32[]{:S(2)}) collective-permute-start(f32[112,128]{1,0:T(8,128)S(1)} %get-tuple-element.40.b0), channel_id=1, source_target_pairs={{8,0},{9,1},{10,2},{11,3},{12,4},{13,5},{14,6},{15,7},{0,8},{1,9},... | collective-permute-start | bytes 172040 | tf_op jit(solution)/shard_map/ppermute | solution.py:765
  75.8 4.2 %collective-permute-start.10 = (f32[112,128]{1,0:T(8,128)S(1)}, f32[112,128]{1,0:T(8,128)S(1)}, u32[]{:S(2)}, u32[]{:S(2)}) collective-permute-start(f32[112,128]{1,0:T(8,128)S(1)} %get-tuple-element.40.b0), channel_id=1, source_target_pairs={{4,0},{5,1},{6,2},{7,3},{8,4},{9,5},{10,6},{11,7},{12,8},{13,9},{1... | collective-permute-start | bytes 172040 | tf_op jit(solution)/shard_map/ppermute | solution.py:765
  81.2 5.0 %collective-permute-start.15 = (f32[32,128]{1,0:T(8,128)S(1)}, f32[32,128]{1,0:T(8,128)S(1)}, u32[]{:S(2)}, u32[]{:S(2)}) collective-permute-start(f32[32,128]{1,0:T(8,128)S(1)} %solve_col.1.e0), channel_id=1, source_target_pairs={{0,1},{1,2},{2,3},{3,0},{4,5},{5,6},{6,7},{7,4},{8,9},{9,10},{10,1... | collective-permute-start | bytes 49160 | tf_op jit(solution)/shard_map/ppermute | solution.py:748
  81.2 5.3 %collective-permute-start.14 = (f32[32,128]{1,0:T(8,128)S(1)}, f32[32,128]{1,0:T(8,128)S(1)}, u32[]{:S(2)}, u32[]{:S(2)}) collective-permute-start(f32[32,128]{1,0:T(8,128)S(1)} %solve_col.1.e0), channel_id=1, source_target_pairs={{0,2},{1,3},{2,0},{3,1},{4,6},{5,7},{6,4},{7,5},{8,10},{9,11},{10,... | collective-permute-start | bytes 49160 | tf_op jit(solution)/shard_map/ppermute | solution.py:748
  83.5 3.7 %collective-permute-start.13 = (f32[32,128]{1,0:T(8,128)S(1)}, f32[32,128]{1,0:T(8,128)S(1)}, u32[]{:S(2)}, u32[]{:S(2)}) collective-permute-start(f32[32,128]{1,0:T(8,128)S(1)} %solve_col.1.e0), channel_id=1, source_target_pairs={{0,3},{1,0},{2,1},{3,2},{4,7},{5,4},{6,5},{7,6},{8,11},{9,8},{10,9... | collective-permute-start | bytes 49160 | tf_op jit(solution)/shard_map/ppermute | solution.py:748

commit v5 on v4

--- a/solution.py
+++ b/solution.py
@@ -341,10 +341,15 @@
         one(2 * pair, carry)
         return one(2 * pair + 1, carry)
 
-    lax.fori_loop(0, count // 2, two, 0)
-
-    @pl.when(count % 2 == 1)
-    def _():
+    def four(quad, carry):
+        two(2 * quad, carry)
+        return two(2 * quad + 1, carry)
+
+    lax.fori_loop(0, count // 4, four, 0)
+
+    @pl.when(count % 4 == 3)
+    def _():
+        two(count // 2 - 1, 0)
         one(count - 1, 0)
 
 

time: 92.8 us -> 92.2 us (level)
  no operation moved by 1% of the time
where the time goes in v5:
time: 92.2 us; the launch traced here: 92.1 us
  Pallas kernels  43.9 us (48%)
  starting transfers between devices  25.7 us (28%)
  waiting for transfers between devices  19.2 us (21%)
  local copies, waits for them, and re-layouts  3 us (3%)
    pallas_call x2, Pallas kernels, forward(): pl.pallas_call(kernel, grid=(STEPS,), in_specs=[scalars() for _ in flags]...  29.8 us
    ppermute x6, starting transfers between devices, line_ends(): blocks[far] = lax.ppermute(port, axis, moves)  11.5 us
    ppermute x8, waiting for transfers between devices, exchange(): received[offset] = lax.ppermute(values[back], axis, moves)  9.54 us
    pallas_call x2, Pallas kernels, backward(): pl.pallas_call(kernel, grid=(STEPS,), in_specs=[scalars(), pl.BlockSpec((...  9.49 us
    ppermute x6, waiting for transfers between devices, line_ends(): blocks[far] = lax.ppermute(port, axis, moves)  8.24 us
    ppermute x8, starting transfers between devices, exchange(): received[offset] = lax.ppermute(values[back], axis, moves)  7.51 us
    ppermute x2, starting transfers between devices, halos(): return (lax.ppermute(last, axis, up), lax.ppermute(initial, axis, down))  6.74 us
    pallas_call x4, Pallas kernels, small(): pl.pallas_call(kernel, out_shape=tuple((jax.ShapeDtypeStruct(shape, F32)...  4.59 us
  transfers between devices with their start and end apart: 16, of which 14 were waited for; matrix products, arithmetic and copies ran while one was open for 0% of the time, Pallas kernels for 0%

profile of v5, /device:TPU:0, one launch (start us, length us, event | category | flops | bytes accessed | tf_op | source)
XLA Modules:
  0.0 92.1 jit_solution(451308245121200103)
XLA Ops:
  0.0 0.0 copy-start.3
  0.0 0.0 copy-start.1
  0.0 2.9 %slice_reduce_fusion = (f32[5,4,128]{2,1,0:T(4,128)S(1)}, f32[5,4,128]{2,1,0:T(4,128)S(1)}) fusion(f32[5,4,128,128]{3,2,1,0:T(8,128)} %param.7), kind=kLoop, calls=%fused_computation | loop fusion | bytes 40960 | tf_op jit(solution)/shard_map/slice | solution.py:816
  3.0 2.1 %collective-permute-start = (f32[20,128]{1,0:T(8,128)S(1)}, f32[20,128]{1,0:T(8,128)S(1)}, u32[]{:S(2)}, u32[]{:S(2)}) collective-permute-start(f32[20,128]{1,0:T(8,128)S(1)} %reshape_squeeze.6), channel_id=1, source_target_pairs={{0,1},{1,2},{2,3},{3,4},{4,5},{5,6},{6,7},{7,8},{8,9},{9,10},{10,1... | collective-permute-start | bytes 30728 | tf_op jit(solution)/shard_map/ppermute | solution.py:800
  5.1 4.7 %collective-permute-start.1 = (f32[20,128]{1,0:T(8,128)S(1)}, f32[20,128]{1,0:T(8,128)S(1)}, u32[]{:S(2)}, u32[]{:S(2)}) collective-permute-start(f32[20,128]{1,0:T(8,128)S(1)} %reshape_squeeze.7), channel_id=1, source_target_pairs={{1,0},{2,1},{3,2},{4,3},{5,4},{6,5},{7,6},{8,7},{9,8},{10,9},{11,1... | collective-permute-start | bytes 30728 | tf_op jit(solution)/shard_map/ppermute | solution.py:800
  9.7 0.1 compare_convert_fusion
  9.8 0.1 pad_add_fusion.spots_ref.refs_0_
  9.9 0.0 copy-done.4
  9.9 1.4 %collective-permute-done.south_ref = f32[20,128]{1,0:T(8,128)S(1)} collective-permute-done((f32[20,128]{1,0:T(8,128)S(1)}, f32[20,128]{1,0:T(8,128)S(1)}, u32[]{:S(2)}, u32[]{:S(2)}) %collective-permute-start) | collective-permute-done | bytes 10272 | tf_op jit(solution)/shard_map/ppermute | solution.py:800
  11.3 0.0 collective-permute-done.1.north_ref
  11.3 0.0 copy-done.3
  11.3 0.0 copy-done.1
  11.4 15.7 %forward_x.1 = (f32[32,60,8,128]{3,2,1,0:T(8,128)S(1)}, f32[60,8,128]{2,1,0:T(8,128)S(1)}, f32[512,128]{1,0:T(8,128)S(1)}, f32[512,128]{1,0:T(8,128)S(1)}, f32[5...) custom-call(s32[4]{0:T(128)S(1)} %pad_add_fusion.spots_ref.refs_0_, ...), custom_call_target="tpu_custom_call" | custom-call | tf_op jit(solution)/shard_map/forward_x/pallas_call | solution.py:719
  27.1 0.1 collective-permute-start.2
  27.2 1.3 %collective-permute-done.2.refs_2_ = f32[224,128]{1,0:T(8,128)S(1)} collective-permute-done((f32[224,128]{1,0:T(8,128)S(1)}, f32[224,128]{1,0:T(8,128)S(1)}, u32[]{:S(2)}, u32[]{:S(2)}) %collective-permute-start.2) | collective-permute-done | bytes 114720 | tf_op jit(solution)/shard_map/ppermute | solution.py:753
  28.5 0.9 join_row.1
  29.3 1.6 %collective-permute-start.5 = (f32[224,128]{1,0:T(8,128)S(1)}, f32[224,128]{1,0:T(8,128)S(1)}, u32[]{:S(2)}, u32[]{:S(2)}) collective-permute-start(f32[224,128]{1,0:T(8,128)S(1)} %get-tuple-element.29.b0), channel_id=1, source_target_pairs={{96,0},{112,16},{0,32},{16,48},{32,64},{48,80},{64,96},{80,112},{9... | collective-permute-start | bytes 344072 | tf_op jit(solution)/shard_map/ppermute | solution.py:770
  30.9 2.7 %collective-permute-start.4 = (f32[224,128]{1,0:T(8,128)S(1)}, f32[224,128]{1,0:T(8,128)S(1)}, u32[]{:S(2)}, u32[]{:S(2)}) collective-permute-start(f32[224,128]{1,0:T(8,128)S(1)} %get-tuple-element.29.b0), channel_id=1, source_target_pairs={{64,0},{80,16},{96,32},{112,48},{0,64},{16,80},{32,96},{48,112},{6... | collective-permute-start | bytes 344072 | tf_op jit(solution)/shard_map/ppermute | solution.py:770
  33.6 1.4 %collective-permute-start.3 = (f32[224,128]{1,0:T(8,128)S(1)}, f32[224,128]{1,0:T(8,128)S(1)}, u32[]{:S(2)}, u32[]{:S(2)}) collective-permute-start(f32[224,128]{1,0:T(8,128)S(1)} %get-tuple-element.29.b0), channel_id=1, source_target_pairs={{32,0},{48,16},{64,32},{80,48},{96,64},{112,80},{0,96},{16,112},{3... | collective-permute-start | bytes 344072 | tf_op jit(solution)/shard_map/ppermute | solution.py:770
  35.1 0.8 collective-permute-done.5.b3
  35.8 3.4 %collective-permute-done.4.b2 = f32[224,128]{1,0:T(8,128)S(1)} collective-permute-done((f32[224,128]{1,0:T(8,128)S(1)}, f32[224,128]{1,0:T(8,128)S(1)}, u32[]{:S(2)}, u32[]{:S(2)}) %collective-permute-start.4) | collective-permute-done | bytes 114720 | tf_op jit(solution)/shard_map/ppermute | solution.py:770
  39.3 0.0 collective-permute-done.3.b1
  39.3 1.2 %solve_row.1.e0 = f32[32,128]{1,0:T(8,128)S(1)} custom-call(s32[4]{0:T(128)S(1)} %pad_add_fusion.spots_ref.refs_0_, f32[224,128]{1,0:T(8,128)S(1)} %get-tuple-element.29.b0, f32[224,128]{1,0:T(8,128)S(1)} %collective-permute-done.3.b1, f32[224,128]{1,0:T(8,128)S(1)} %collective-permute-done.4.b2, f32[224,128]{1,0:T(8,128)S(1)} %collective-permute-done.5.b3, ...), custom_call_target="tpu_custom_call" | custom-call | tf_op jit(solution)/shard_map/solve_row/pallas_call | solution.py:733
  40.4 0.3 collective-permute-start.6
  40.7 1.2 %collective-permute-done.6.e1 = f32[32,128]{1,0:T(8,128)S(1)} collective-permute-done((f32[32,128]{1,0:T(8,128)S(1)}, f32[32,128]{1,0:T(8,128)S(1)}, u32[]{:S(2)}, u32[]{:S(2)}) %collective-permute-start.6) | collective-permute-done | bytes 16416 | tf_op jit(solution)/shard_map/ppermute | solution.py:753
  41.9 4.1 %backward_x.1.p_ref = f32[5,512,128]{2,1,0:T(8,128)S(1)} custom-call(s32[4]{0:T(128)S(1)} %pad_add_fusion.spots_ref.refs_0_, f32[32,60,8,128]{3,2,1,0:T(8,128)S(1)} %get-tuple-element.25.fac_ref, f32[60,8,128]{2,1,0:T(8,128)S(1)} %get-tuple-element.26.mid_ref, f32[32,128]{1,0:T(8,128)S(1)} %solve_row.1.e0, f32[32,128]{1,0:T(8,128)S(1)} %collective-permute-done.6.e1, ...), custom_call_target="tpu_custom_call" | custom-call | tf_op jit(solution)/shard_map/backward_x/pallas_call | solution.py:780
  46.0 14.1 %forward_y.1 = (f32[32,60,8,128]{3,2,1,0:T(8,128)S(1)}, f32[60,8,128]{2,1,0:T(8,128)S(1)}, f32[512,128]{1,0:T(8,128)S(1)}, f32[512,128]{1,0:T(8,128)S(1)}, f32[5...) custom-call(s32[4]{0:T(128)S(1)} %pad_add_fusion.spots_ref.refs_0_, ...), custom_call_target="tpu_custom_call" | custom-call | tf_op jit(solution)/shard_map/forward_y/pallas_call | solution.py:719
  60.1 2.0 %collective-permute-start.7 = (f32[112,128]{1,0:T(8,128)S(1)}, f32[112,128]{1,0:T(8,128)S(1)}, u32[]{:S(2)}, u32[]{:S(2)}) collective-permute-start(f32[112,128]{1,0:T(8,128)S(1)} %get-tuple-element.37), channel_id=1, source_target_pairs={{0,3},{1,0},{2,1},{3,2},{4,7},{5,4},{6,5},{7,6},{8,11},{9,8},{10,9... | collective-permute-start | bytes 172040 | tf_op jit(solution)/shard_map/ppermute | solution.py:753
  62.1 0.0 collective-permute-start.8
  62.1 0.9 %collective-permute-start.9 = (f32[112,128]{1,0:T(8,128)S(1)}, f32[112,128]{1,0:T(8,128)S(1)}, u32[]{:S(2)}, u32[]{:S(2)}) collective-permute-start(f32[112,128]{1,0:T(8,128)S(1)} %get-tuple-element.39), channel_id=1, source_target_pairs={{0,1},{1,2},{2,3},{3,0},{4,5},{5,6},{6,7},{7,4},{8,9},{9,10},{10,1... | collective-permute-start | bytes 172040 | tf_op jit(solution)/shard_map/ppermute | solution.py:753
  63.0 1.9 %collective-permute-done.7.refs_2_ = f32[112,128]{1,0:T(8,128)S(1)} collective-permute-done((f32[112,128]{1,0:T(8,128)S(1)}, f32[112,128]{1,0:T(8,128)S(1)}, u32[]{:S(2)}, u32[]{:S(2)}) %collective-permute-start.7) | collective-permute-done | bytes 57376 | tf_op jit(solution)/shard_map/ppermute | solution.py:753
  64.9 3.0 %collective-permute-done.8.refs_3_ = f32[112,128]{1,0:T(8,128)S(1)} collective-permute-done((f32[112,128]{1,0:T(8,128)S(1)}, f32[112,128]{1,0:T(8,128)S(1)}, u32[]{:S(2)}, u32[]{:S(2)}) %collective-permute-start.8) | collective-permute-done | bytes 57376 | tf_op jit(solution)/shard_map/ppermute | solution.py:753
  67.9 0.3 collective-permute-done.9.refs_4_
  68.2 1.4 %join_col.1 = (f32[112,128]{1,0:T(8,128)S(1)}, f32[3,56,128]{2,1,0:T(8,128)S(1)}) custom-call(s32[4]{0:T(128)S(1)} %pad_add_fusion.spots_ref.refs_0_, f32[112,128]{1,0:T(8,128)S(1)} %get-tuple-element.36.refs_1_, f32[112,128]{1,0:T(8,128)S(1)} %collective-permute-done.7.refs_2_, f32[112,128]{1,0:T(8,128)S(1)} %collective-permute-done.8.refs_3_, ...), custom_call_target="tpu_custom_call" | custom-call | tf_op jit(solution)/shard_map/join_col/pallas_call | solution.py:733
  69.6 1.6 %collective-permute-start.12 = (f32[112,128]{1,0:T(8,128)S(1)}, f32[112,128]{1,0:T(8,128)S(1)}, u32[]{:S(2)}, u32[]{:S(2)}) collective-permute-start(f32[112,128]{1,0:T(8,128)S(1)} %get-tuple-element.40.b0), channel_id=1, source_target_pairs={{12,0},{13,1},{14,2},{15,3},{0,4},{1,5},{2,6},{3,7},{4,8},{5,9},{6... | collective-permute-start | bytes 172040 | tf_op jit(solution)/shard_map/ppermute | solution.py:770
  71.3 4.0 %collective-permute-start.11 = (f32[112,128]{1,0:T(8,128)S(1)}, f32[112,128]{1,0:T(8,128)S(1)}, u32[]{:S(2)}, u32[]{:S(2)}) collective-permute-start(f32[112,128]{1,0:T(8,128)S(1)} %get-tuple-element.40.b0), channel_id=1, source_target_pairs={{8,0},{9,1},{10,2},{11,3},{12,4},{13,5},{14,6},{15,7},{0,8},{1,9},... | collective-permute-start | bytes 172040 | tf_op jit(solution)/shard_map/ppermute | solution.py:770
  75.3 0.1 collective-permute-start.10
  75.4 1.2 %collective-permute-done.12.b3 = f32[112,128]{1,0:T(8,128)S(1)} collective-permute-done((f32[112,128]{1,0:T(8,128)S(1)}, f32[112,128]{1,0:T(8,128)S(1)}, u32[]{:S(2)}, u32[]{:S(2)}) %collective-permute-start.12) | collective-permute-done | bytes 57376 | tf_op jit(solution)/shard_map/ppermute | solution.py:770
  76.6 1.5 %collective-permute-done.11.b2 = f32[112,128]{1,0:T(8,128)S(1)} collective-permute-done((f32[112,128]{1,0:T(8,128)S(1)}, f32[112,128]{1,0:T(8,128)S(1)}, u32[]{:S(2)}, u32[]{:S(2)}) %collective-permute-start.11) | collective-permute-done | bytes 57376 | tf_op jit(solution)/shard_map/ppermute | solution.py:770
  78.0 1.4 %collective-permute-done.10.b1 = f32[112,128]{1,0:T(8,128)S(1)} collective-permute-done((f32[112,128]{1,0:T(8,128)S(1)}, f32[112,128]{1,0:T(8,128)S(1)}, u32[]{:S(2)}, u32[]{:S(2)}) %collective-permute-start.10) | collective-permute-done | bytes 57376 | tf_op jit(solution)/shard_map/ppermute | solution.py:770
  79.4 1.2 %solve_col.1.e0 = f32[32,128]{1,0:T(8,128)S(1)} custom-call(s32[4]{0:T(128)S(1)} %pad_add_fusion.spots_ref.refs_0_, f32[112,128]{1,0:T(8,128)S(1)} %get-tuple-element.40.b0, f32[112,128]{1,0:T(8,128)S(1)} %collective-permute-done.10.b1, f32[112,128]{1,0:T(8,128)S(1)} %collective-permute-done.11.b2, f32[112,128]{1,0:T(8,128)S(1)} %collective-permute-done.12.b3, ...), custom_call_target="tpu_custom_call" | custom-call | tf_op jit(solution)/shard_map/solve_col/pallas_call | solution.py:733
  80.6 0.1 collective-permute-start.15
  80.7 2.3 %collective-permute-start.14 = (f32[32,128]{1,0:T(8,128)S(1)}, f32[32,128]{1,0:T(8,128)S(1)}, u32[]{:S(2)}, u32[]{:S(2)}) collective-permute-start(f32[32,128]{1,0:T(8,128)S(1)} %solve_col.1.e0), channel_id=1, source_target_pairs={{0,2},{1,3},{2,0},{3,1},{4,6},{5,7},{6,4},{7,5},{8,10},{9,11},{10,... | collective-permute-start | bytes 49160 | tf_op jit(solution)/shard_map/ppermute | solution.py:753
  83.0 1.9 %collective-permute-start.13 = (f32[32,128]{1,0:T(8,128)S(1)}, f32[32,128]{1,0:T(8,128)S(1)}, u32[]{:S(2)}, u32[]{:S(2)}) collective-permute-start(f32[32,128]{1,0:T(8,128)S(1)} %solve_col.1.e0), channel_id=1, source_target_pairs={{0,3},{1,0},{2,1},{3,2},{4,7},{5,4},{6,5},{7,6},{8,11},{9,8},{10,9... | collective-permute-start | bytes 49160 | tf_op jit(solution)/shard_map/ppermute | solution.py:753
  84.9 0.8 collective-permute-done.15.e3
  85.6 0.4 collective-permute-done.14.e2
  86.0 0.7 collective-permute-done.13.e1
  86.7 5.4 %backward_y.1 = f32[5,512,128]{2,1,0:T(8,128)} custom-call(s32[4]{0:T(128)S(1)} %pad_add_fusion.spots_ref.refs_0_, f32[32,60,8,128]{3,2,1,0:T(8,128)S(1)} %get-tuple-element.34.fac_ref, f32[60,8,128]{2,1,0:T(8,128)S(1)} %get-tuple-element.35.mid_ref, f32[32,128]{1,0:T(8,128)S(1)} %solve_col.1.e0, f32[32,128]{1,0:T(8,128)S(1)} %collective-permute-done.13.e1, ...), custom_call_target="tpu_custom_call" | custom-call | tf_op jit(solution)/shard_map/backward_y/pallas_call | solution.py:780
  (13 shorter events, 0.0 us)
Async XLA Ops:
  0.0 9.7 %copy-start.6 = (s32[2]{0:T(128)S(1)}, s32[2]{0:T(128)}, u32[]{:S(2)}) copy-start(s32[2]{0:T(128)} %constant.57) | copy-start | bytes 28
  0.0 11.3 %copy-start = (f32[5,4,128,128]{3,2,1,0:T(8,128)S(1)}, f32[5,4,128,128]{3,2,1,0:T(8,128)}, u32[]{:S(2)}) copy-start(f32[5,4,128,128]{3,2,1,0:T(8,128)} %param.7) | copy-start | bytes 3932164
  0.0 9.9 %copy-start.4 = (f32[5,5,128]{2,1,0:T(8,128)S(1)}, f32[5,5,128]{2,1,0:T(8,128)}, u32[]{:S(2)}) copy-start(f32[5,5,128]{2,1,0:T(8,128)} %param.12) | copy-start | bytes 38404
  0.0 9.9 %copy-start.5 = (f32[5,5,128]{2,1,0:T(8,128)S(1)}, f32[5,5,128]{2,1,0:T(8,128)}, u32[]{:S(2)}) copy-start(f32[5,5,128]{2,1,0:T(8,128)} %param.11) | copy-start | bytes 38404
  0.0 11.3 %copy-start.2 = (f32[128,128]{1,0:T(8,128)S(1)}, f32[128,128]{1,0:T(8,128)}, u32[]{:S(2)}) copy-start(f32[128,128]{1,0:T(8,128)} %my_ref.3) | copy-start | bytes 196612
  0.0 11.3 %copy-start.3 = (f32[128,128]{1,0:T(8,128)S(1)}, f32[128,128]{1,0:T(8,128)}, u32[]{:S(2)}) copy-start(f32[128,128]{1,0:T(8,128)} %mx_ref.1) | copy-start | bytes 196612
  0.0 11.3 %copy-start.1 = (f32[4,128,128]{2,1,0:T(8,128)S(1)}, f32[4,128,128]{2,1,0:T(8,128)}, u32[]{:S(2)}) copy-start(f32[4,128,128]{2,1,0:T(8,128)} %param.8) | copy-start | bytes 786436
  3.0 8.3 %collective-permute-start = (f32[20,128]{1,0:T(8,128)S(1)}, f32[20,128]{1,0:T(8,128)S(1)}, u32[]{:S(2)}, u32[]{:S(2)}) collective-permute-start(f32[20,128]{1,0:T(8,128)S(1)} %reshape_squeeze.6), channel_id=1, source_target_pairs={{0,1},{1,2},{2,3},{3,4},{4,5},{5,6},{6,7},{7,8},{8,9},{9,10},{10,1... | collective-permute-start | bytes 30728 | tf_op jit(solution)/shard_map/ppermute | solution.py:800
  5.1 6.2 %collective-permute-start.1 = (f32[20,128]{1,0:T(8,128)S(1)}, f32[20,128]{1,0:T(8,128)S(1)}, u32[]{:S(2)}, u32[]{:S(2)}) collective-permute-start(f32[20,128]{1,0:T(8,128)S(1)} %reshape_squeeze.7), channel_id=1, source_target_pairs={{1,0},{2,1},{3,2},{4,3},{5,4},{6,5},{7,6},{8,7},{9,8},{10,9},{11,1... | collective-permute-start | bytes 30728 | tf_op jit(solution)/shard_map/ppermute | solution.py:800
  27.1 1.4 %collective-permute-start.2 = (f32[224,128]{1,0:T(8,128)S(1)}, f32[224,128]{1,0:T(8,128)S(1)}, u32[]{:S(2)}, u32[]{:S(2)}) collective-permute-start(f32[224,128]{1,0:T(8,128)S(1)} %get-tuple-element.28), channel_id=1, source_target_pairs={{0,16},{16,0},{32,48},{48,32},{64,80},{80,64},{96,112},{112,96},{1... | collective-permute-start | bytes 344072 | tf_op jit(solution)/shard_map/ppermute | solution.py:753
  29.3 6.5 %collective-permute-start.5 = (f32[224,128]{1,0:T(8,128)S(1)}, f32[224,128]{1,0:T(8,128)S(1)}, u32[]{:S(2)}, u32[]{:S(2)}) collective-permute-start(f32[224,128]{1,0:T(8,128)S(1)} %get-tuple-element.29.b0), channel_id=1, source_target_pairs={{96,0},{112,16},{0,32},{16,48},{32,64},{48,80},{64,96},{80,112},{9... | collective-permute-start | bytes 344072 | tf_op jit(solution)/shard_map/ppermute | solution.py:770
  30.9 8.4 %collective-permute-start.4 = (f32[224,128]{1,0:T(8,128)S(1)}, f32[224,128]{1,0:T(8,128)S(1)}, u32[]{:S(2)}, u32[]{:S(2)}) collective-permute-start(f32[224,128]{1,0:T(8,128)S(1)} %get-tuple-element.29.b0), channel_id=1, source_target_pairs={{64,0},{80,16},{96,32},{112,48},{0,64},{16,80},{32,96},{48,112},{6... | collective-permute-start | bytes 344072 | tf_op jit(solution)/shard_map/ppermute | solution.py:770
  33.6 5.6 %collective-permute-start.3 = (f32[224,128]{1,0:T(8,128)S(1)}, f32[224,128]{1,0:T(8,128)S(1)}, u32[]{:S(2)}, u32[]{:S(2)}) collective-permute-start(f32[224,128]{1,0:T(8,128)S(1)} %get-tuple-element.29.b0), channel_id=1, source_target_pairs={{32,0},{48,16},{64,32},{80,48},{96,64},{112,80},{0,96},{16,112},{3... | collective-permute-start | bytes 344072 | tf_op jit(solution)/shard_map/ppermute | solution.py:770
  40.4 1.4 %collective-permute-start.6 = (f32[32,128]{1,0:T(8,128)S(1)}, f32[32,128]{1,0:T(8,128)S(1)}, u32[]{:S(2)}, u32[]{:S(2)}) collective-permute-start(f32[32,128]{1,0:T(8,128)S(1)} %solve_row.1.e0), channel_id=1, source_target_pairs={{0,16},{16,0},{32,48},{48,32},{64,80},{80,64},{96,112},{112,96},{1... | collective-permute-start | bytes 49160 | tf_op jit(solution)/shard_map/ppermute | solution.py:753
  60.1 4.9 %collective-permute-start.7 = (f32[112,128]{1,0:T(8,128)S(1)}, f32[112,128]{1,0:T(8,128)S(1)}, u32[]{:S(2)}, u32[]{:S(2)}) collective-permute-start(f32[112,128]{1,0:T(8,128)S(1)} %get-tuple-element.37), channel_id=1, source_target_pairs={{0,3},{1,0},{2,1},{3,2},{4,7},{5,4},{6,5},{7,6},{8,11},{9,8},{10,9... | collective-permute-start | bytes 172040 | tf_op jit(solution)/shard_map/ppermute | solution.py:753
  62.1 5.9 %collective-permute-start.8 = (f32[112,128]{1,0:T(8,128)S(1)}, f32[112,128]{1,0:T(8,128)S(1)}, u32[]{:S(2)}, u32[]{:S(2)}) collective-permute-start(f32[112,128]{1,0:T(8,128)S(1)} %get-tuple-element.38), channel_id=1, source_target_pairs={{0,2},{1,3},{2,0},{3,1},{4,6},{5,7},{6,4},{7,5},{8,10},{9,11},{10,... | collective-permute-start | bytes 172040 | tf_op jit(solution)/shard_map/ppermute | solution.py:753
  62.1 6.1 %collective-permute-start.9 = (f32[112,128]{1,0:T(8,128)S(1)}, f32[112,128]{1,0:T(8,128)S(1)}, u32[]{:S(2)}, u32[]{:S(2)}) collective-permute-start(f32[112,128]{1,0:T(8,128)S(1)} %get-tuple-element.39), channel_id=1, source_target_pairs={{0,1},{1,2},{2,3},{3,0},{4,5},{5,6},{6,7},{7,4},{8,9},{9,10},{10,1... | collective-permute-start | bytes 172040 | tf_op jit(solution)/shard_map/ppermute | solution.py:753
  69.6 6.9 %collective-permute-start.12 = (f32[112,128]{1,0:T(8,128)S(1)}, f32[112,128]{1,0:T(8,128)S(1)}, u32[]{:S(2)}, u32[]{:S(2)}) collective-permute-start(f32[112,128]{1,0:T(8,128)S(1)} %get-tuple-element.40.b0), channel_id=1, source_target_pairs={{12,0},{13,1},{14,2},{15,3},{0,4},{1,5},{2,6},{3,7},{4,8},{5,9},{6... | collective-permute-start | bytes 172040 | tf_op jit(solution)/shard_map/ppermute | solution.py:770
  71.3 6.8 %collective-permute-start.11 = (f32[112,128]{1,0:T(8,128)S(1)}, f32[112,128]{1,0:T(8,128)S(1)}, u32[]{:S(2)}, u32[]{:S(2)}) collective-permute-start(f32[112,128]{1,0:T(8,128)S(1)} %get-tuple-element.40.b0), channel_id=1, source_target_pairs={{8,0},{9,1},{10,2},{11,3},{12,4},{13,5},{14,6},{15,7},{0,8},{1,9},... | collective-permute-start | bytes 172040 | tf_op jit(solution)/shard_map/ppermute | solution.py:770
  75.3 4.2 %collective-permute-start.10 = (f32[112,128]{1,0:T(8,128)S(1)}, f32[112,128]{1,0:T(8,128)S(1)}, u32[]{:S(2)}, u32[]{:S(2)}) collective-permute-start(f32[112,128]{1,0:T(8,128)S(1)} %get-tuple-element.40.b0), channel_id=1, source_target_pairs={{4,0},{5,1},{6,2},{7,3},{8,4},{9,5},{10,6},{11,7},{12,8},{13,9},{1... | collective-permute-start | bytes 172040 | tf_op jit(solution)/shard_map/ppermute | solution.py:770
  80.6 5.0 %collective-permute-start.15 = (f32[32,128]{1,0:T(8,128)S(1)}, f32[32,128]{1,0:T(8,128)S(1)}, u32[]{:S(2)}, u32[]{:S(2)}) collective-permute-start(f32[32,128]{1,0:T(8,128)S(1)} %solve_col.1.e0), channel_id=1, source_target_pairs={{0,1},{1,2},{2,3},{3,0},{4,5},{5,6},{6,7},{7,4},{8,9},{9,10},{10,1... | collective-permute-start | bytes 49160 | tf_op jit(solution)/shard_map/ppermute | solution.py:753
  80.7 5.3 %collective-permute-start.14 = (f32[32,128]{1,0:T(8,128)S(1)}, f32[32,128]{1,0:T(8,128)S(1)}, u32[]{:S(2)}, u32[]{:S(2)}) collective-permute-start(f32[32,128]{1,0:T(8,128)S(1)} %solve_col.1.e0), channel_id=1, source_target_pairs={{0,2},{1,3},{2,0},{3,1},{4,6},{5,7},{6,4},{7,5},{8,10},{9,11},{10,... | collective-permute-start | bytes 49160 | tf_op jit(solution)/shard_map/ppermute | solution.py:753
  83.0 3.7 %collective-permute-start.13 = (f32[32,128]{1,0:T(8,128)S(1)}, f32[32,128]{1,0:T(8,128)S(1)}, u32[]{:S(2)}, u32[]{:S(2)}) collective-permute-start(f32[32,128]{1,0:T(8,128)S(1)} %solve_col.1.e0), channel_id=1, source_target_pairs={{0,3},{1,0},{2,1},{3,2},{4,7},{5,4},{6,5},{7,6},{8,11},{9,8},{10,9... | collective-permute-start | bytes 49160 | tf_op jit(solution)/shard_map/ppermute | solution.py:753

commit v6 on v5

--- a/solution.py
+++ b/solution.py
@@ -619,16 +619,19 @@
         write(2 * m + 1, here)
         return here
 
+    def two(pair, following):
+        return one(2 * pair + 1, one(2 * pair, following))
+
     @pl.when(step == 0)
     def _():
-        here = one(1, tuple(edge[5 + i] for i in range(5)))
+        here = two(1, one(1, tuple(edge[5 + i] for i in range(5))))
         for i in range(5):
             edge[5 + i] = here[i]
 
-    def two(pair, following):
-        return one(2 * pair + 1, one(2 * pair, following))
-
-    final = lax.fori_loop(begin, CHUNK // 2, two, tuple(edge[5 + i] for i in range(5)))
+    def four(quad, following):
+        return two(2 * quad + 1, two(2 * quad, following))
+
+    final = lax.fori_loop(begin, CHUNK // 4, four, tuple(edge[5 + i] for i in range(5)))
     for i in range(5):
         edge[5 + i] = final[i]
 

time: 92.2 us -> 91.3 us (level)
  no operation moved by 1% of the time
where the time goes in v6:
time: 91.3 us; the launch traced here: 91.2 us
  Pallas kernels  43 us (47%)
  starting transfers between devices  25.7 us (28%)
  waiting for transfers between devices  19.2 us (21%)
  local copies, waits for them, and re-layouts  3 us (3%)
    pallas_call x2, Pallas kernels, forward(): pl.pallas_call(kernel, grid=(STEPS,), in_specs=[scalars() for _ in flags]...  29.8 us
    ppermute x6, starting transfers between devices, line_ends(): blocks[far] = lax.ppermute(port, axis, moves)  11.5 us
    ppermute x8, waiting for transfers between devices, exchange(): received[offset] = lax.ppermute(values[back], axis, moves)  9.54 us
    pallas_call x2, Pallas kernels, backward(): pl.pallas_call(kernel, grid=(STEPS,), in_specs=[scalars(), pl.BlockSpec((...  8.58 us
    ppermute x6, waiting for transfers between devices, line_ends(): blocks[far] = lax.ppermute(port, axis, moves)  8.24 us
    ppermute x8, starting transfers between devices, exchange(): received[offset] = lax.ppermute(values[back], axis, moves)  7.51 us
    ppermute x2, starting transfers between devices, halos(): return (lax.ppermute(last, axis, up), lax.ppermute(initial, axis, down))  6.74 us
    pallas_call x4, Pallas kernels, small(): pl.pallas_call(kernel, out_shape=tuple((jax.ShapeDtypeStruct(shape, F32)...  4.59 us
  transfers between devices with their start and end apart: 16, of which 14 were waited for; matrix products, arithmetic and copies ran while one was open for 0% of the time, Pallas kernels for 0%

profile of v6, /device:TPU:0, one launch (start us, length us, event | category | flops | bytes accessed | tf_op | source)
XLA Modules:
  0.0 91.2 jit_solution(7289040718934898896)
XLA Ops:
  0.0 0.0 copy-start.3
  0.0 0.0 copy-start.1
  0.0 2.9 %slice_reduce_fusion = (f32[5,4,128]{2,1,0:T(4,128)S(1)}, f32[5,4,128]{2,1,0:T(4,128)S(1)}) fusion(f32[5,4,128,128]{3,2,1,0:T(8,128)} %param.7), kind=kLoop, calls=%fused_computation | loop fusion | bytes 40960 | tf_op jit(solution)/shard_map/slice | solution.py:819
  3.0 2.1 %collective-permute-start = (f32[20,128]{1,0:T(8,128)S(1)}, f32[20,128]{1,0:T(8,128)S(1)}, u32[]{:S(2)}, u32[]{:S(2)}) collective-permute-start(f32[20,128]{1,0:T(8,128)S(1)} %reshape_squeeze.6), channel_id=1, source_target_pairs={{0,1},{1,2},{2,3},{3,4},{4,5},{5,6},{6,7},{7,8},{8,9},{9,10},{10,1... | collective-permute-start | bytes 30728 | tf_op jit(solution)/shard_map/ppermute | solution.py:803
  5.1 4.7 %collective-permute-start.1 = (f32[20,128]{1,0:T(8,128)S(1)}, f32[20,128]{1,0:T(8,128)S(1)}, u32[]{:S(2)}, u32[]{:S(2)}) collective-permute-start(f32[20,128]{1,0:T(8,128)S(1)} %reshape_squeeze.7), channel_id=1, source_target_pairs={{1,0},{2,1},{3,2},{4,3},{5,4},{6,5},{7,6},{8,7},{9,8},{10,9},{11,1... | collective-permute-start | bytes 30728 | tf_op jit(solution)/shard_map/ppermute | solution.py:803
  9.7 0.1 compare_convert_fusion
  9.8 0.1 pad_add_fusion.spots_ref.refs_0_
  9.9 0.0 copy-done.4
  9.9 1.4 %collective-permute-done.south_ref = f32[20,128]{1,0:T(8,128)S(1)} collective-permute-done((f32[20,128]{1,0:T(8,128)S(1)}, f32[20,128]{1,0:T(8,128)S(1)}, u32[]{:S(2)}, u32[]{:S(2)}) %collective-permute-start) | collective-permute-done | bytes 10272 | tf_op jit(solution)/shard_map/ppermute | solution.py:803
  11.3 0.0 collective-permute-done.1.north_ref
  11.3 0.0 copy-done.3
  11.3 0.0 copy-done.1
  11.4 15.7 %forward_x.1 = (f32[32,60,8,128]{3,2,1,0:T(8,128)S(1)}, f32[60,8,128]{2,1,0:T(8,128)S(1)}, f32[512,128]{1,0:T(8,128)S(1)}, f32[512,128]{1,0:T(8,128)S(1)}, f32[5...) custom-call(s32[4]{0:T(128)S(1)} %pad_add_fusion.spots_ref.refs_0_, ...), custom_call_target="tpu_custom_call" | custom-call | tf_op jit(solution)/shard_map/forward_x/pallas_call | solution.py:722
  27.1 0.1 collective-permute-start.2
  27.2 1.3 %collective-permute-done.2.refs_2_ = f32[224,128]{1,0:T(8,128)S(1)} collective-permute-done((f32[224,128]{1,0:T(8,128)S(1)}, f32[224,128]{1,0:T(8,128)S(1)}, u32[]{:S(2)}, u32[]{:S(2)}) %collective-permute-start.2) | collective-permute-done | bytes 114720 | tf_op jit(solution)/shard_map/ppermute | solution.py:756
  28.5 0.9 join_row.1
  29.3 1.6 %collective-permute-start.5 = (f32[224,128]{1,0:T(8,128)S(1)}, f32[224,128]{1,0:T(8,128)S(1)}, u32[]{:S(2)}, u32[]{:S(2)}) collective-permute-start(f32[224,128]{1,0:T(8,128)S(1)} %get-tuple-element.29.b0), channel_id=1, source_target_pairs={{96,0},{112,16},{0,32},{16,48},{32,64},{48,80},{64,96},{80,112},{9... | collective-permute-start | bytes 344072 | tf_op jit(solution)/shard_map/ppermute | solution.py:773
  30.9 2.7 %collective-permute-start.4 = (f32[224,128]{1,0:T(8,128)S(1)}, f32[224,128]{1,0:T(8,128)S(1)}, u32[]{:S(2)}, u32[]{:S(2)}) collective-permute-start(f32[224,128]{1,0:T(8,128)S(1)} %get-tuple-element.29.b0), channel_id=1, source_target_pairs={{64,0},{80,16},{96,32},{112,48},{0,64},{16,80},{32,96},{48,112},{6... | collective-permute-start | bytes 344072 | tf_op jit(solution)/shard_map/ppermute | solution.py:773
  33.6 1.4 %collective-permute-start.3 = (f32[224,128]{1,0:T(8,128)S(1)}, f32[224,128]{1,0:T(8,128)S(1)}, u32[]{:S(2)}, u32[]{:S(2)}) collective-permute-start(f32[224,128]{1,0:T(8,128)S(1)} %get-tuple-element.29.b0), channel_id=1, source_target_pairs={{32,0},{48,16},{64,32},{80,48},{96,64},{112,80},{0,96},{16,112},{3... | collective-permute-start | bytes 344072 | tf_op jit(solution)/shard_map/ppermute | solution.py:773
  35.1 0.8 collective-permute-done.5.b3
  35.8 3.4 %collective-permute-done.4.b2 = f32[224,128]{1,0:T(8,128)S(1)} collective-permute-done((f32[224,128]{1,0:T(8,128)S(1)}, f32[224,128]{1,0:T(8,128)S(1)}, u32[]{:S(2)}, u32[]{:S(2)}) %collective-permute-start.4) | collective-permute-done | bytes 114720 | tf_op jit(solution)/shard_map/ppermute | solution.py:773
  39.3 0.0 collective-permute-done.3.b1
  39.3 1.2 %solve_row.1.e0 = f32[32,128]{1,0:T(8,128)S(1)} custom-call(s32[4]{0:T(128)S(1)} %pad_add_fusion.spots_ref.refs_0_, f32[224,128]{1,0:T(8,128)S(1)} %get-tuple-element.29.b0, f32[224,128]{1,0:T(8,128)S(1)} %collective-permute-done.3.b1, f32[224,128]{1,0:T(8,128)S(1)} %collective-permute-done.4.b2, f32[224,128]{1,0:T(8,128)S(1)} %collective-permute-done.5.b3, ...), custom_call_target="tpu_custom_call" | custom-call | tf_op jit(solution)/shard_map/solve_row/pallas_call | solution.py:736
  40.4 0.3 collective-permute-start.6
  40.7 1.2 %collective-permute-done.6.e1 = f32[32,128]{1,0:T(8,128)S(1)} collective-permute-done((f32[32,128]{1,0:T(8,128)S(1)}, f32[32,128]{1,0:T(8,128)S(1)}, u32[]{:S(2)}, u32[]{:S(2)}) %collective-permute-start.6) | collective-permute-done | bytes 16416 | tf_op jit(solution)/shard_map/ppermute | solution.py:756
  41.9 3.7 %backward_x.1.p_ref = f32[5,512,128]{2,1,0:T(8,128)S(1)} custom-call(s32[4]{0:T(128)S(1)} %pad_add_fusion.spots_ref.refs_0_, f32[32,60,8,128]{3,2,1,0:T(8,128)S(1)} %get-tuple-element.25.fac_ref, f32[60,8,128]{2,1,0:T(8,128)S(1)} %get-tuple-element.26.mid_ref, f32[32,128]{1,0:T(8,128)S(1)} %solve_row.1.e0, f32[32,128]{1,0:T(8,128)S(1)} %collective-permute-done.6.e1, ...), custom_call_target="tpu_custom_call" | custom-call | tf_op jit(solution)/shard_map/backward_x/pallas_call | solution.py:783
  45.6 14.1 %forward_y.1 = (f32[32,60,8,128]{3,2,1,0:T(8,128)S(1)}, f32[60,8,128]{2,1,0:T(8,128)S(1)}, f32[512,128]{1,0:T(8,128)S(1)}, f32[512,128]{1,0:T(8,128)S(1)}, f32[5...) custom-call(s32[4]{0:T(128)S(1)} %pad_add_fusion.spots_ref.refs_0_, ...), custom_call_target="tpu_custom_call" | custom-call | tf_op jit(solution)/shard_map/forward_y/pallas_call | solution.py:722
  59.7 2.0 %collective-permute-start.7 = (f32[112,128]{1,0:T(8,128)S(1)}, f32[112,128]{1,0:T(8,128)S(1)}, u32[]{:S(2)}, u32[]{:S(2)}) collective-permute-start(f32[112,128]{1,0:T(8,128)S(1)} %get-tuple-element.37), channel_id=1, source_target_pairs={{0,3},{1,0},{2,1},{3,2},{4,7},{5,4},{6,5},{7,6},{8,11},{9,8},{10,9... | collective-permute-start | bytes 172040 | tf_op jit(solution)/shard_map/ppermute | solution.py:756
  61.6 0.0 collective-permute-start.8
  61.6 0.9 %collective-permute-start.9 = (f32[112,128]{1,0:T(8,128)S(1)}, f32[112,128]{1,0:T(8,128)S(1)}, u32[]{:S(2)}, u32[]{:S(2)}) collective-permute-start(f32[112,128]{1,0:T(8,128)S(1)} %get-tuple-element.39), channel_id=1, source_target_pairs={{0,1},{1,2},{2,3},{3,0},{4,5},{5,6},{6,7},{7,4},{8,9},{9,10},{10,1... | collective-permute-start | bytes 172040 | tf_op jit(solution)/shard_map/ppermute | solution.py:756
  62.6 1.9 %collective-permute-done.7.refs_2_ = f32[112,128]{1,0:T(8,128)S(1)} collective-permute-done((f32[112,128]{1,0:T(8,128)S(1)}, f32[112,128]{1,0:T(8,128)S(1)}, u32[]{:S(2)}, u32[]{:S(2)}) %collective-permute-start.7) | collective-permute-done | bytes 57376 | tf_op jit(solution)/shard_map/ppermute | solution.py:756
  64.5 3.0 %collective-permute-done.8.refs_3_ = f32[112,128]{1,0:T(8,128)S(1)} collective-permute-done((f32[112,128]{1,0:T(8,128)S(1)}, f32[112,128]{1,0:T(8,128)S(1)}, u32[]{:S(2)}, u32[]{:S(2)}) %collective-permute-start.8) | collective-permute-done | bytes 57376 | tf_op jit(solution)/shard_map/ppermute | solution.py:756
  67.5 0.3 collective-permute-done.9.refs_4_
  67.8 1.4 %join_col.1 = (f32[112,128]{1,0:T(8,128)S(1)}, f32[3,56,128]{2,1,0:T(8,128)S(1)}) custom-call(s32[4]{0:T(128)S(1)} %pad_add_fusion.spots_ref.refs_0_, f32[112,128]{1,0:T(8,128)S(1)} %get-tuple-element.36.refs_1_, f32[112,128]{1,0:T(8,128)S(1)} %collective-permute-done.7.refs_2_, f32[112,128]{1,0:T(8,128)S(1)} %collective-permute-done.8.refs_3_, ...), custom_call_target="tpu_custom_call" | custom-call | tf_op jit(solution)/shard_map/join_col/pallas_call | solution.py:736
  69.2 1.6 %collective-permute-start.12 = (f32[112,128]{1,0:T(8,128)S(1)}, f32[112,128]{1,0:T(8,128)S(1)}, u32[]{:S(2)}, u32[]{:S(2)}) collective-permute-start(f32[112,128]{1,0:T(8,128)S(1)} %get-tuple-element.40.b0), channel_id=1, source_target_pairs={{12,0},{13,1},{14,2},{15,3},{0,4},{1,5},{2,6},{3,7},{4,8},{5,9},{6... | collective-permute-start | bytes 172040 | tf_op jit(solution)/shard_map/ppermute | solution.py:773
  70.9 4.0 %collective-permute-start.11 = (f32[112,128]{1,0:T(8,128)S(1)}, f32[112,128]{1,0:T(8,128)S(1)}, u32[]{:S(2)}, u32[]{:S(2)}) collective-permute-start(f32[112,128]{1,0:T(8,128)S(1)} %get-tuple-element.40.b0), channel_id=1, source_target_pairs={{8,0},{9,1},{10,2},{11,3},{12,4},{13,5},{14,6},{15,7},{0,8},{1,9},... | collective-permute-start | bytes 172040 | tf_op jit(solution)/shard_map/ppermute | solution.py:773
  74.8 0.1 collective-permute-start.10
  75.0 1.2 %collective-permute-done.12.b3 = f32[112,128]{1,0:T(8,128)S(1)} collective-permute-done((f32[112,128]{1,0:T(8,128)S(1)}, f32[112,128]{1,0:T(8,128)S(1)}, u32[]{:S(2)}, u32[]{:S(2)}) %collective-permute-start.12) | collective-permute-done | bytes 57376 | tf_op jit(solution)/shard_map/ppermute | solution.py:773
  76.1 1.5 %collective-permute-done.11.b2 = f32[112,128]{1,0:T(8,128)S(1)} collective-permute-done((f32[112,128]{1,0:T(8,128)S(1)}, f32[112,128]{1,0:T(8,128)S(1)}, u32[]{:S(2)}, u32[]{:S(2)}) %collective-permute-start.11) | collective-permute-done | bytes 57376 | tf_op jit(solution)/shard_map/ppermute | solution.py:773
  77.6 1.4 %collective-permute-done.10.b1 = f32[112,128]{1,0:T(8,128)S(1)} collective-permute-done((f32[112,128]{1,0:T(8,128)S(1)}, f32[112,128]{1,0:T(8,128)S(1)}, u32[]{:S(2)}, u32[]{:S(2)}) %collective-permute-start.10) | collective-permute-done | bytes 57376 | tf_op jit(solution)/shard_map/ppermute | solution.py:773
  79.0 1.2 %solve_col.1.e0 = f32[32,128]{1,0:T(8,128)S(1)} custom-call(s32[4]{0:T(128)S(1)} %pad_add_fusion.spots_ref.refs_0_, f32[112,128]{1,0:T(8,128)S(1)} %get-tuple-element.40.b0, f32[112,128]{1,0:T(8,128)S(1)} %collective-permute-done.10.b1, f32[112,128]{1,0:T(8,128)S(1)} %collective-permute-done.11.b2, f32[112,128]{1,0:T(8,128)S(1)} %collective-permute-done.12.b3, ...), custom_call_target="tpu_custom_call" | custom-call | tf_op jit(solution)/shard_map/solve_col/pallas_call | solution.py:736
  80.2 0.1 collective-permute-start.15
  80.3 2.3 %collective-permute-start.14 = (f32[32,128]{1,0:T(8,128)S(1)}, f32[32,128]{1,0:T(8,128)S(1)}, u32[]{:S(2)}, u32[]{:S(2)}) collective-permute-start(f32[32,128]{1,0:T(8,128)S(1)} %solve_col.1.e0), channel_id=1, source_target_pairs={{0,2},{1,3},{2,0},{3,1},{4,6},{5,7},{6,4},{7,5},{8,10},{9,11},{10,... | collective-permute-start | bytes 49160 | tf_op jit(solution)/shard_map/ppermute | solution.py:756
  82.6 1.9 %collective-permute-start.13 = (f32[32,128]{1,0:T(8,128)S(1)}, f32[32,128]{1,0:T(8,128)S(1)}, u32[]{:S(2)}, u32[]{:S(2)}) collective-permute-start(f32[32,128]{1,0:T(8,128)S(1)} %solve_col.1.e0), channel_id=1, source_target_pairs={{0,3},{1,0},{2,1},{3,2},{4,7},{5,4},{6,5},{7,6},{8,11},{9,8},{10,9... | collective-permute-start | bytes 49160 | tf_op jit(solution)/shard_map/ppermute | solution.py:756
  84.5 0.8 collective-permute-done.15.e3
  85.2 0.4 collective-permute-done.14.e2
  85.6 0.7 collective-permute-done.13.e1
  86.3 4.9 %backward_y.1 = f32[5,512,128]{2,1,0:T(8,128)} custom-call(s32[4]{0:T(128)S(1)} %pad_add_fusion.spots_ref.refs_0_, f32[32,60,8,128]{3,2,1,0:T(8,128)S(1)} %get-tuple-element.34.fac_ref, f32[60,8,128]{2,1,0:T(8,128)S(1)} %get-tuple-element.35.mid_ref, f32[32,128]{1,0:T(8,128)S(1)} %solve_col.1.e0, f32[32,128]{1,0:T(8,128)S(1)} %collective-permute-done.13.e1, ...), custom_call_target="tpu_custom_call" | custom-call | tf_op jit(solution)/shard_map/backward_y/pallas_call | solution.py:783
  (13 shorter events, 0.0 us)
Async XLA Ops:
  0.0 9.7 %copy-start.6 = (s32[2]{0:T(128)S(1)}, s32[2]{0:T(128)}, u32[]{:S(2)}) copy-start(s32[2]{0:T(128)} %constant.57) | copy-start | bytes 28
  0.0 11.3 %copy-start = (f32[5,4,128,128]{3,2,1,0:T(8,128)S(1)}, f32[5,4,128,128]{3,2,1,0:T(8,128)}, u32[]{:S(2)}) copy-start(f32[5,4,128,128]{3,2,1,0:T(8,128)} %param.7) | copy-start | bytes 3932164
  0.0 9.9 %copy-start.4 = (f32[5,5,128]{2,1,0:T(8,128)S(1)}, f32[5,5,128]{2,1,0:T(8,128)}, u32[]{:S(2)}) copy-start(f32[5,5,128]{2,1,0:T(8,128)} %param.12) | copy-start | bytes 38404
  0.0 9.9 %copy-start.5 = (f32[5,5,128]{2,1,0:T(8,128)S(1)}, f32[5,5,128]{2,1,0:T(8,128)}, u32[]{:S(2)}) copy-start(f32[5,5,128]{2,1,0:T(8,128)} %param.11) | copy-start | bytes 38404
  0.0 11.3 %copy-start.2 = (f32[128,128]{1,0:T(8,128)S(1)}, f32[128,128]{1,0:T(8,128)}, u32[]{:S(2)}) copy-start(f32[128,128]{1,0:T(8,128)} %my_ref.3) | copy-start | bytes 196612
  0.0 11.3 %copy-start.3 = (f32[128,128]{1,0:T(8,128)S(1)}, f32[128,128]{1,0:T(8,128)}, u32[]{:S(2)}) copy-start(f32[128,128]{1,0:T(8,128)} %mx_ref.1) | copy-start | bytes 196612
  0.0 11.3 %copy-start.1 = (f32[4,128,128]{2,1,0:T(8,128)S(1)}, f32[4,128,128]{2,1,0:T(8,128)}, u32[]{:S(2)}) copy-start(f32[4,128,128]{2,1,0:T(8,128)} %param.8) | copy-start | bytes 786436
  3.0 8.3 %collective-permute-start = (f32[20,128]{1,0:T(8,128)S(1)}, f32[20,128]{1,0:T(8,128)S(1)}, u32[]{:S(2)}, u32[]{:S(2)}) collective-permute-start(f32[20,128]{1,0:T(8,128)S(1)} %reshape_squeeze.6), channel_id=1, source_target_pairs={{0,1},{1,2},{2,3},{3,4},{4,5},{5,6},{6,7},{7,8},{8,9},{9,10},{10,1... | collective-permute-start | bytes 30728 | tf_op jit(solution)/shard_map/ppermute | solution.py:803
  5.1 6.2 %collective-permute-start.1 = (f32[20,128]{1,0:T(8,128)S(1)}, f32[20,128]{1,0:T(8,128)S(1)}, u32[]{:S(2)}, u32[]{:S(2)}) collective-permute-start(f32[20,128]{1,0:T(8,128)S(1)} %reshape_squeeze.7), channel_id=1, source_target_pairs={{1,0},{2,1},{3,2},{4,3},{5,4},{6,5},{7,6},{8,7},{9,8},{10,9},{11,1... | collective-permute-start | bytes 30728 | tf_op jit(solution)/shard_map/ppermute | solution.py:803
  27.1 1.4 %collective-permute-start.2 = (f32[224,128]{1,0:T(8,128)S(1)}, f32[224,128]{1,0:T(8,128)S(1)}, u32[]{:S(2)}, u32[]{:S(2)}) collective-permute-start(f32[224,128]{1,0:T(8,128)S(1)} %get-tuple-element.28), channel_id=1, source_target_pairs={{0,16},{16,0},{32,48},{48,32},{64,80},{80,64},{96,112},{112,96},{1... | collective-permute-start | bytes 344072 | tf_op jit(solution)/shard_map/ppermute | solution.py:756
  29.3 6.5 %collective-permute-start.5 = (f32[224,128]{1,0:T(8,128)S(1)}, f32[224,128]{1,0:T(8,128)S(1)}, u32[]{:S(2)}, u32[]{:S(2)}) collective-permute-start(f32[224,128]{1,0:T(8,128)S(1)} %get-tuple-element.29.b0), channel_id=1, source_target_pairs={{96,0},{112,16},{0,32},{16,48},{32,64},{48,80},{64,96},{80,112},{9... | collective-permute-start | bytes 344072 | tf_op jit(solution)/shard_map/ppermute | solution.py:773
  30.9 8.4 %collective-permute-start.4 = (f32[224,128]{1,0:T(8,128)S(1)}, f32[224,128]{1,0:T(8,128)S(1)}, u32[]{:S(2)}, u32[]{:S(2)}) collective-permute-start(f32[224,128]{1,0:T(8,128)S(1)} %get-tuple-element.29.b0), channel_id=1, source_target_pairs={{64,0},{80,16},{96,32},{112,48},{0,64},{16,80},{32,96},{48,112},{6... | collective-permute-start | bytes 344072 | tf_op jit(solution)/shard_map/ppermute | solution.py:773
  33.6 5.6 %collective-permute-start.3 = (f32[224,128]{1,0:T(8,128)S(1)}, f32[224,128]{1,0:T(8,128)S(1)}, u32[]{:S(2)}, u32[]{:S(2)}) collective-permute-start(f32[224,128]{1,0:T(8,128)S(1)} %get-tuple-element.29.b0), channel_id=1, source_target_pairs={{32,0},{48,16},{64,32},{80,48},{96,64},{112,80},{0,96},{16,112},{3... | collective-permute-start | bytes 344072 | tf_op jit(solution)/shard_map/ppermute | solution.py:773
  40.4 1.4 %collective-permute-start.6 = (f32[32,128]{1,0:T(8,128)S(1)}, f32[32,128]{1,0:T(8,128)S(1)}, u32[]{:S(2)}, u32[]{:S(2)}) collective-permute-start(f32[32,128]{1,0:T(8,128)S(1)} %solve_row.1.e0), channel_id=1, source_target_pairs={{0,16},{16,0},{32,48},{48,32},{64,80},{80,64},{96,112},{112,96},{1... | collective-permute-start | bytes 49160 | tf_op jit(solution)/shard_map/ppermute | solution.py:756
  59.7 4.9 %collective-permute-start.7 = (f32[112,128]{1,0:T(8,128)S(1)}, f32[112,128]{1,0:T(8,128)S(1)}, u32[]{:S(2)}, u32[]{:S(2)}) collective-permute-start(f32[112,128]{1,0:T(8,128)S(1)} %get-tuple-element.37), channel_id=1, source_target_pairs={{0,3},{1,0},{2,1},{3,2},{4,7},{5,4},{6,5},{7,6},{8,11},{9,8},{10,9... | collective-permute-start | bytes 172040 | tf_op jit(solution)/shard_map/ppermute | solution.py:756
  61.6 5.9 %collective-permute-start.8 = (f32[112,128]{1,0:T(8,128)S(1)}, f32[112,128]{1,0:T(8,128)S(1)}, u32[]{:S(2)}, u32[]{:S(2)}) collective-permute-start(f32[112,128]{1,0:T(8,128)S(1)} %get-tuple-element.38), channel_id=1, source_target_pairs={{0,2},{1,3},{2,0},{3,1},{4,6},{5,7},{6,4},{7,5},{8,10},{9,11},{10,... | collective-permute-start | bytes 172040 | tf_op jit(solution)/shard_map/ppermute | solution.py:756
  61.6 6.1 %collective-permute-start.9 = (f32[112,128]{1,0:T(8,128)S(1)}, f32[112,128]{1,0:T(8,128)S(1)}, u32[]{:S(2)}, u32[]{:S(2)}) collective-permute-start(f32[112,128]{1,0:T(8,128)S(1)} %get-tuple-element.39), channel_id=1, source_target_pairs={{0,1},{1,2},{2,3},{3,0},{4,5},{5,6},{6,7},{7,4},{8,9},{9,10},{10,1... | collective-permute-start | bytes 172040 | tf_op jit(solution)/shard_map/ppermute | solution.py:756
  69.2 6.9 %collective-permute-start.12 = (f32[112,128]{1,0:T(8,128)S(1)}, f32[112,128]{1,0:T(8,128)S(1)}, u32[]{:S(2)}, u32[]{:S(2)}) collective-permute-start(f32[112,128]{1,0:T(8,128)S(1)} %get-tuple-element.40.b0), channel_id=1, source_target_pairs={{12,0},{13,1},{14,2},{15,3},{0,4},{1,5},{2,6},{3,7},{4,8},{5,9},{6... | collective-permute-start | bytes 172040 | tf_op jit(solution)/shard_map/ppermute | solution.py:773
  70.9 6.8 %collective-permute-start.11 = (f32[112,128]{1,0:T(8,128)S(1)}, f32[112,128]{1,0:T(8,128)S(1)}, u32[]{:S(2)}, u32[]{:S(2)}) collective-permute-start(f32[112,128]{1,0:T(8,128)S(1)} %get-tuple-element.40.b0), channel_id=1, source_target_pairs={{8,0},{9,1},{10,2},{11,3},{12,4},{13,5},{14,6},{15,7},{0,8},{1,9},... | collective-permute-start | bytes 172040 | tf_op jit(solution)/shard_map/ppermute | solution.py:773
  74.8 4.2 %collective-permute-start.10 = (f32[112,128]{1,0:T(8,128)S(1)}, f32[112,128]{1,0:T(8,128)S(1)}, u32[]{:S(2)}, u32[]{:S(2)}) collective-permute-start(f32[112,128]{1,0:T(8,128)S(1)} %get-tuple-element.40.b0), channel_id=1, source_target_pairs={{4,0},{5,1},{6,2},{7,3},{8,4},{9,5},{10,6},{11,7},{12,8},{13,9},{1... | collective-permute-start | bytes 172040 | tf_op jit(solution)/shard_map/ppermute | solution.py:773
  80.2 5.0 %collective-permute-start.15 = (f32[32,128]{1,0:T(8,128)S(1)}, f32[32,128]{1,0:T(8,128)S(1)}, u32[]{:S(2)}, u32[]{:S(2)}) collective-permute-start(f32[32,128]{1,0:T(8,128)S(1)} %solve_col.1.e0), channel_id=1, source_target_pairs={{0,1},{1,2},{2,3},{3,0},{4,5},{5,6},{6,7},{7,4},{8,9},{9,10},{10,1... | collective-permute-start | bytes 49160 | tf_op jit(solution)/shard_map/ppermute | solution.py:756
  80.3 5.3 %collective-permute-start.14 = (f32[32,128]{1,0:T(8,128)S(1)}, f32[32,128]{1,0:T(8,128)S(1)}, u32[]{:S(2)}, u32[]{:S(2)}) collective-permute-start(f32[32,128]{1,0:T(8,128)S(1)} %solve_col.1.e0), channel_id=1, source_target_pairs={{0,2},{1,3},{2,0},{3,1},{4,6},{5,7},{6,4},{7,5},{8,10},{9,11},{10,... | collective-permute-start | bytes 49160 | tf_op jit(solution)/shard_map/ppermute | solution.py:756
  82.6 3.7 %collective-permute-start.13 = (f32[32,128]{1,0:T(8,128)S(1)}, f32[32,128]{1,0:T(8,128)S(1)}, u32[]{:S(2)}, u32[]{:S(2)}) collective-permute-start(f32[32,128]{1,0:T(8,128)S(1)} %solve_col.1.e0), channel_id=1, source_target_pairs={{0,3},{1,0},{2,1},{3,2},{4,7},{5,4},{6,5},{7,6},{8,11},{9,8},{10,9... | collective-permute-start | bytes 49160 | tf_op jit(solution)/shard_map/ppermute | solution.py:756
